TPU v7x, 256 devices: a whole 4x4x8 slice. The times are simulated.
256 devices in a mesh: row: 8 (over y, x_hi), col: 32 (over z, x_lo, core).
Axes of the slice: x: 4 (x_hi: 2, x_lo: 2; x = x_hi * 2 + x_lo), y: 4, z: 8, core: 2. Of those that a mesh axis runs over, the one named last changes fastest.
Arguments:
- fingerprints: bfloat16 [32768, 2048], P(('col', 'row')), may hold values from 0 to 4
- activity: bfloat16 [32768, 256], P(('col', 'row')), may hold values from -6 to 6
- label_mask: int32 [32768], P(('col', 'row')), may hold values 0 or 1
- pattern: int32 [64, 24], P('col'), may hold values from 0 to 63, as said below
- counts: int32 [64], P('col'), may hold values from 1 to 24
Outputs:
- labels: bfloat16 [32768, 256], P(('col', 'row'))
Inputs may be any that keep to these rules, and one draw needn't show every extreme that they name: `pattern`: slot 0 of row block I holds I, and the 24 slots of one row block name distinct blocks.
All inputs are finite; a program needn't handle non-finite values. No bound on the sum of `label_mask` on one device may be relied on, other than what follows from the above.
Results may differ from a plain program's by a relative error of at most 0.0034.
Values may be sent and summed in bfloat16 or wider, within the bound.
No kernel may reach another device: no remote copies, remote signals or barrier semaphores. Data moves between devices by JAX's collectives and lax.ppermute only.
A program may use at most 128 MiB of HBM per device.

v0:
```python
import jax
import jax.numpy as jnp
from jax import lax
from jax.sharding import PartitionSpec as P

ITERS = 3


WEIGHT_ROW = 0.6
WEIGHT_COL = 0.3
WEIGHT_SHARED = 0.1
SHARPNESS = 80.0
EPSILON = 1e-05
PROPAGATE = 0.8
ANCHOR = 0.2


def affinity(row_prints, row_squares, col_prints, col_squares, keep_mask):
    inner = lax.dot_general(
        row_prints, col_prints, (((1,), (1,)), ((), ())), preferred_element_type=jnp.float32
    )
    ratio = inner / (
        WEIGHT_ROW * row_squares[:, None]
        + WEIGHT_COL * col_squares[None, :]
        + WEIGHT_SHARED * inner
        + EPSILON
    )
    return jnp.where(keep_mask, jnp.exp(SHARPNESS * (ratio - 0.5)), 0.0)


def body(fingerprints, activity, label_mask, pattern, counts):
    row_count = lax.axis_size("row")
    row_index = lax.axis_index("row")
    col_index = lax.axis_index("col")
    per_device = fingerprints.shape[0]
    tasks_width = activity.shape[1]
    row_blocks, slot_count = pattern.shape
    block_size = row_count * per_device // row_blocks
    per_block = block_size // per_device
    col_width = per_device * max(1, per_block // row_count)
    total_rows = row_blocks * block_size
    row_prints = lax.all_gather(fingerprints, "row", axis=0, tiled=True)
    col_prints = lax.all_gather(fingerprints, "col", axis=0, tiled=True)
    row_squares = jnp.sum(jnp.square(row_prints.astype(jnp.float32)), axis=1)
    col_squares = jnp.sum(jnp.square(col_prints.astype(jnp.float32)), axis=1)
    seeded = activity.astype(jnp.float32) * label_mask.astype(jnp.float32)[:, None]
    labels = seeded.astype(jnp.bfloat16)
    row_base = col_index * (row_count * per_device)
    offsets = jnp.arange(col_width, dtype=jnp.int32)
    local_rows = jnp.arange(block_size, dtype=jnp.int32)

    def locate(col_block):
        offset_piece = (row_index - col_block * per_block) % row_count
        first_piece = col_block * per_block + offset_piece
        return (offset_piece < per_block, first_piece, first_piece // row_count * per_device)

    def tile(row_block, column_slot):
        present, first_piece, col_start = locate(pattern[row_block, column_slot])
        rows_here = lax.dynamic_slice_in_dim(row_prints, row_block * block_size, block_size, 0)
        row_sq_here = lax.dynamic_slice_in_dim(row_squares, row_block * block_size, block_size, 0)
        cols_here = lax.dynamic_slice_in_dim(col_prints, col_start, col_width, 0)
        col_sq_here = lax.dynamic_slice_in_dim(col_squares, col_start, col_width, 0)
        row_global = row_base + row_block * block_size + local_rows
        col_global = (
            first_piece + row_count * (offsets // per_device)
        ) * per_device + offsets % per_device
        keep_mask = row_global[:, None] != col_global[None, :]
        return (affinity(rows_here, row_sq_here, cols_here, col_sq_here, keep_mask), col_start)

    def build_per_row_block(row_block, state):
        cache_all, degree_all = state

        def build_per_slot(column_slot, inner_state):
            cache_now, degree_now = inner_state
            present = locate(pattern[row_block, column_slot])[0]

            def active(unused):
                weights, col_start = tile(row_block, column_slot)
                stored = lax.dynamic_update_slice(
                    cache_now,
                    weights.astype(jnp.bfloat16)[None, None],
                    (row_block, column_slot, 0, 0),
                )
                return (stored, degree_now + jnp.sum(weights, axis=1))

            return lax.cond(present, active, lambda unused: inner_state, None)

        cache_all, degree = lax.fori_loop(
            0, counts[row_block], build_per_slot, (cache_all, jnp.zeros((block_size,), jnp.float32))
        )
        return (
            cache_all,
            lax.dynamic_update_slice_in_dim(degree_all, degree, row_block * block_size, 0),
        )

    empty_cache = jnp.zeros((row_blocks, slot_count, block_size, col_width), jnp.bfloat16)
    cache, cached_degree = lax.fori_loop(
        0, row_blocks, build_per_row_block, (empty_cache, jnp.zeros((total_rows,), jnp.float32))
    )
    for iteration in range(ITERS):
        gathered = lax.all_gather(labels, "col", axis=0, tiled=True)

        def action(row_block, column_slot, running):
            col_start = locate(pattern[row_block, column_slot])[2]
            weights = cache[row_block, column_slot]
            labels_here = lax.dynamic_slice_in_dim(gathered, col_start, col_width, 0)
            return (
                running[0] + jnp.dot(weights, labels_here, preferred_element_type=jnp.float32),
                running[1],
            )

        def slot_per_row_block(row_block, totals):
            spread_all, degree_all = totals

            def slot_per_slot(column_slot, running):
                present = locate(pattern[row_block, column_slot])[0]
                return lax.cond(
                    present,
                    lambda unused: action(row_block, column_slot, running),
                    lambda unused: running,
                    None,
                )

            start_state = (
                jnp.zeros((block_size, tasks_width), jnp.float32),
                jnp.zeros((block_size,), jnp.float32),
            )
            spread, degree = lax.fori_loop(0, counts[row_block], slot_per_slot, start_state)
            return (
                lax.dynamic_update_slice_in_dim(spread_all, spread, row_block * block_size, 0),
                lax.dynamic_update_slice_in_dim(degree_all, degree, row_block * block_size, 0),
            )

        empty_state = (
            jnp.zeros((total_rows, tasks_width), jnp.float32),
            jnp.zeros((total_rows,), jnp.float32),
        )
        spread_all = lax.fori_loop(0, row_blocks, slot_per_row_block, empty_state)[0]
        degree_all = cached_degree
        spread_own, degree_own = (
            lax.psum_scatter(spread_all, "row", scatter_dimension=0, tiled=True),
            lax.psum_scatter(degree_all, "row", scatter_dimension=0, tiled=True),
        )
        labels = (PROPAGATE * spread_own / degree_own[:, None] + ANCHOR * seeded).astype(
            jnp.bfloat16
        )
    return labels


def solution(mesh):
    placed = (
        P(("col", "row"), None),
        P(("col", "row"), None),
        P(("col", "row")),
        P("col", None),
        P("col"),
    )
    return jax.shard_map(
        body, mesh=mesh, in_specs=placed, out_specs=P(("col", "row"), None), check_vma=False
    )
```

profile of v0, /device:TPU:1, one launch (start us, length us, event | category | flops | bytes accessed | tf_op | source)
XLA Modules:
  0.0 1017.5 jit_solution(6233472792779026501)
XLA Ops:
  10.3 79.5 %all-gather.6.cloned.1.call-done = bf16[1024,2048]{1,0:T(8,128)(2,1)} async-done(((bf16[128,2048]{1,0:T(8,128)(2,1)}), bf16[1024,2048]{1,0:T(8,128)(2,1)}) %all-gather.6.cloned.1.call-update) | async-done | bytes 4194320 | tf_op jit(solution)/shard_map/all_gather | solution.py:42
  92.9 97.3 %all-gather.8.cloned.1.call-done = bf16[4096,2048]{1,0:T(8,128)(2,1)} async-done(((bf16[128,2048]{1,0:T(8,128)(2,1)}), bf16[4096,2048]{1,0:T(8,128)(2,1)}) %all-gather.8.cloned.1.call-update) | async-done | bytes 16777232 | tf_op jit(solution)/shard_map/all_gather | solution.py:43
  190.3 7.2 multiply_reduce_fusion
  197.5 3.4 broadcast_in_dim.15
  200.9 40.8 %while.215 = (s32[]{:T(128)}, bf16[2,24,512,128]{2,3,1,0:T(8,128)(2,1)}, f32[1024]{0:T(1024)S(1)}, s32[2]{0:T(128)S(1)}, s32[2,24]{1,0:T(2,128)S(1)}, /*index=5*...) while((s32[]{:T(128)}, ...), condition=%wide.region_8.9_spmd.clone.clone, body=%wide.region_2.8_spmd.clone.clone.sunk | while | flops 269161408 | bytes 3311072 | solution.py:97
  201.4 36.6 %while.219 = (s32[]{:T(128)}, bf16[2,24,512,128]{2,3,1,0:T(8,128)(2,1)}, f32[512]{0:T(512)S(1)}, s32[]{:T(128)}, s32[2,24]{1,0:T(2,128)S(1)}, /*index=5*/s32[]{:...) while((s32[]{:T(128)}, ...), condition=%wide.region_7.7_spmd.clone, body=%wide.region_3.6_spmd.clone.sunk | while | flops 269161408 | bytes 3301913 | solution.py:88
  203.3 4.8 conditional.9
  211.8 4.8 conditional.9
  222.2 4.8 conditional.9
  232.6 4.8 conditional.9
  241.6 8.6 copy.11
  250.2 7.0 all-gather.10.cloned.1.call-done
  257.3 32.5 %while.209 = (s32[]{:T(128)}, f32[1024,256]{1,0:T(8,128)S(1)}, s32[2]{0:T(128)S(1)}, s32[2,24]{1,0:T(2,128)S(1)}, s32[]{:T(128)}, /*index=5*/bf16[2,24,512,128]{...) while((s32[]{:T(128)}, f32[1024,256]{1,0:T(8,128)S(1)}, ...), condition=%wide.region_14.15_spmd, body=%wide.region_9.14_spmd.sunk | while | flops 33685564 | bytes 2819246 | solution.py:138
  258.0 28.3 %while.216 = (s32[]{:T(128)}, f32[512,256]{1,0:T(8,128)S(1)}, s32[]{:T(128)}, s32[2,24]{1,0:T(2,128)S(1)}, s32[]{:T(128)}, /*index=5*/s32[]{:T(128)}, bf16[2,24,...) while((s32[]{:T(128)}, f32[512,256]{1,0:T(8,128)S(1)}, ...), condition=%wide.region_13.13_spmd, body=%wide.region_10.12_spmd.sunk | while | flops 33685564 | bytes 1246015 | solution.py:128
  292.1 28.0 %all-reduce = f32[1024]{0:T(1024)S(1)} all-reduce(f32[1024]{0:T(1024)S(1)} %get-tuple-element.2959), channel_id=3, replica_groups=mesh['row'=8,'col'=32] {'row'}, use_global_device_ids=true, to_apply=%region_16.17.clone | all-reduce | flops 1024 | bytes 8192
  320.1 200.6 %reduce-scatter.4.cloned.1.call-done = f32[128,256]{1,0:T(8,128)} async-done(((f32[1024,256]{1,0:T(8,128)}), f32[128,256]{1,0:T(8,128)}) %reduce-scatter.4.cloned.1.call-update) | async-done | bytes 131088 | tf_op jit(solution)/shard_map/reduce_scatter | solution.py:141
  522.5 66.2 %all-gather.12.cloned.1.call-done = bf16[4096,256]{1,0:T(8,128)(2,1)} async-done(((bf16[128,256]{1,0:T(8,128)(2,1)}), bf16[4096,256]{1,0:T(8,128)(2,1)}) %all-gather.12.cloned.1.call-update) | async-done | bytes 2097168 | tf_op jit(solution)/shard_map/all_gather | solution.py:101
  588.7 33.2 %while.211 = (s32[]{:T(128)}, f32[1024,256]{1,0:T(8,128)S(1)}, s32[2]{0:T(128)S(1)}, s32[2,24]{1,0:T(2,128)S(1)}, s32[]{:T(128)}, /*index=5*/bf16[2,24,512,128]{...) while((s32[]{:T(128)}, f32[1024,256]{1,0:T(8,128)S(1)}, ...), condition=%wide.region_22.23_spmd, body=%wide.region_17.22_spmd.sunk | while | flops 33685564 | bytes 2819246 | solution.py:138
  589.4 29.0 %while.217 = (s32[]{:T(128)}, f32[512,256]{1,0:T(8,128)S(1)}, s32[]{:T(128)}, s32[2,24]{1,0:T(2,128)S(1)}, s32[]{:T(128)}, /*index=5*/s32[]{:T(128)}, bf16[2,24,...) while((s32[]{:T(128)}, f32[512,256]{1,0:T(8,128)S(1)}, ...), condition=%wide.region_21.21_spmd, body=%wide.region_18.20_spmd.sunk | while | flops 33685564 | bytes 1246015 | solution.py:128
  623.0 141.8 %reduce-scatter.6.cloned.1.call-done = f32[128,256]{1,0:T(8,128)} async-done(((f32[1024,256]{1,0:T(8,128)}), f32[128,256]{1,0:T(8,128)}) %reduce-scatter.6.cloned.1.call-update) | async-done | bytes 131088 | tf_op jit(solution)/shard_map/reduce_scatter | solution.py:141
  766.5 66.2 %all-gather.14.cloned.1.call-done = bf16[4096,256]{1,0:T(8,128)(2,1)} async-done(((bf16[128,256]{1,0:T(8,128)(2,1)}), bf16[4096,256]{1,0:T(8,128)(2,1)}) %all-gather.14.cloned.1.call-update) | async-done | bytes 2097168 | tf_op jit(solution)/shard_map/all_gather | solution.py:101
  832.9 33.2 %while.213 = (s32[]{:T(128)}, f32[1024,256]{1,0:T(8,128)S(1)}, s32[2]{0:T(128)S(1)}, s32[2,24]{1,0:T(2,128)S(1)}, s32[]{:T(128)}, /*index=5*/bf16[2,24,512,128]{...) while((s32[]{:T(128)}, f32[1024,256]{1,0:T(8,128)S(1)}, ...), condition=%wide.region_29.30_spmd, body=%wide.region_24.29_spmd.sunk | while | flops 33685564 | bytes 2819246 | solution.py:138
  833.5 29.0 %while.218 = (s32[]{:T(128)}, f32[512,256]{1,0:T(8,128)S(1)}, s32[]{:T(128)}, s32[2,24]{1,0:T(2,128)S(1)}, s32[]{:T(128)}, /*index=5*/s32[]{:T(128)}, bf16[2,24,...) while((s32[]{:T(128)}, f32[512,256]{1,0:T(8,128)S(1)}, ...), condition=%wide.region_28.28_spmd, body=%wide.region_25.27_spmd.sunk | while | flops 33685564 | bytes 1246015 | solution.py:128
  867.1 141.9 %reduce-scatter.8.cloned.1.call-done = f32[128,256]{1,0:T(8,128)} async-done(((f32[1024,256]{1,0:T(8,128)}), f32[128,256]{1,0:T(8,128)}) %reduce-scatter.8.cloned.1.call-update) | async-done | bytes 131088 | tf_op jit(solution)/shard_map/reduce_scatter | solution.py:141
  (206 shorter events, 125.1 us)
Async XLA Ops:
  6.5 83.3 %all-gather.6.cloned.1.call-start = ((), (), s32[]{:S(2)}) async-start(), calls=%async_computation.3 | async-start | bytes 4718592 | tf_op jit(solution)/shard_map/all_gather | solution.py:42
  7.3 183.0 %all-gather.8.cloned.1.call-start = ((), (), s32[]{:S(2)}) async-start(), calls=%async_computation.4 | async-start | bytes 17301504 | tf_op jit(solution)/shard_map/all_gather | solution.py:43
  8.0 249.2 %all-gather.10.cloned.1.call-start = ((), (), s32[]{:S(2)}) async-start(), calls=%async_computation.5 | async-start | bytes 2162688 | tf_op jit(solution)/shard_map/all_gather | solution.py:101
  10.3 510.4 %reduce-scatter.4.cloned.1.call-start = ((), (), s32[]{:S(2)}) async-start(), calls=%async_computation.6 | async-start | bytes 1179648 | tf_op jit(solution)/shard_map/reduce_scatter | solution.py:141
  197.4 3.4 copy-start
  197.4 3.4 copy-start.5
  257.3 33.6 %copy-start.6 = (u32[256]{0:T(256)S(1)}, u32[256]{0:T(256)}, u32[]{:S(2)}) copy-start(u32[256]{0:T(256)} %constant.673) | copy-start | bytes 3076
  257.3 263.4 %copy-start.4 = (bf16[128,256]{1,0:T(8,128)(2,1)S(1)}, bf16[128,256]{1,0:T(8,128)(2,1)}, u32[]{:S(2)}) copy-start(bf16[128,256]{1,0:T(8,128)(2,1)} %param.30) | copy-start | bytes 196612
  289.8 1.0 copy-start.1
  290.8 297.9 %all-gather.12.cloned.1.call-start = ((), (), s32[]{:S(2)}) async-start(), calls=%async_computation.7 | async-start | bytes 2162688 | tf_op jit(solution)/shard_map/all_gather | solution.py:101
  522.4 242.4 %reduce-scatter.6.cloned.1.call-start = ((), (), s32[]{:S(2)}) async-start(), calls=%async_computation.8 | async-start | bytes 1179648 | tf_op jit(solution)/shard_map/reduce_scatter | solution.py:141
  621.9 1.0 copy-start.2
  622.9 209.9 %all-gather.14.cloned.1.call-start = ((), (), s32[]{:S(2)}) async-start(), calls=%async_computation.9 | async-start | bytes 2162688 | tf_op jit(solution)/shard_map/all_gather | solution.py:101
  766.5 242.5 %reduce-scatter.8.cloned.1.call-start = ((), (), s32[]{:S(2)}) async-start(), calls=%async_computation.10 | async-start | bytes 1179648 | tf_op jit(solution)/shard_map/reduce_scatter | solution.py:141
  866.0 1.0 copy-start.3
Sparse Core Ops, SparseCore 0:
  10.0 79.8 all-gather.5
  91.7 98.4 all-gather.7
  192.1 65.0 all-gather.9
  290.9 229.7 reduce-scatter.3
  522.6 66.0 all-gather.11
  623.0 141.7 reduce-scatter.5
  766.7 66.0 all-gather.13
  867.2 141.7 reduce-scatter.7
where the time goes:
time: 1000 us; the launch traced here: 1020 us
  waiting for transfers between devices  802 us (80%)
  loops' own time  70.5 us (7%)
  local copies, waits for them, and re-layouts  57.4 us (6%)
  blocking collectives  28 us (3%)
  matrix products  26.6 us (3%)
  other arithmetic  18.3 us (2%)
  between operations  14.3 us (1%)
    reduce_scatter x3, waiting for transfers between devices, body(): lax.psum_scatter(spread_all, 'row', scatter_dimension=0, tiled=True)  484 us
    all_gather x3, waiting for transfers between devices, body(): gathered = lax.all_gather(labels, 'col', axis=0, tiled=True)  139 us
    all_gather x1, waiting for transfers between devices, body(): col_prints = lax.all_gather(fingerprints, 'col', axis=0, tiled=True)  97.3 us
    all_gather x1, waiting for transfers between devices, body(): row_prints = lax.all_gather(fingerprints, 'row', axis=0, tiled=True)  79.5 us
    another operation x6, loops' own time, slot_per_row_block(): lax.fori_loop(0, counts[row_block], slot_per_slot, start_state)  45.1 us
    unnamed x1, blocking collectives  28 us
  transfers between devices with their start and end apart: 8, of which 8 were waited for; matrix products, arithmetic and copies ran while one was open for 5% of the time, Pallas kernels for 0%

commit v1 on v0

v1 whole, which is shorter than its diff:
```python
import jax
import jax.numpy as jnp
from jax import lax
from jax.experimental import pallas as pl
from jax.experimental.pallas import tpu as pltpu
from jax.sharding import Mesh, PartitionSpec as P

ITERS = 3

WEIGHT_ROW = 0.6
WEIGHT_COL = 0.3
WEIGHT_SHARED = 0.1
SHARPNESS = 80.0
EPSILON = 1e-05
PROPAGATE = 0.8
ANCHOR = 0.2

AXES = ("y", "xh", "z", "xl", "core")
SIZES = (4, 2, 8, 2, 2)
LINE = ("core", "z")
PLANE = ("xl", "y", "xh")
PIECE = 128
ROWS = 16
BLOCKS = 4
WIDTH = 512
TILES = ROWS * BLOCKS
VMEM_LIMIT = 48 * 1024 * 1024


def weights_kernel(ids, meta, starts, rows, cols, row_sq, col_sq, weights, degree,
                   col_buf, row_buf, tile_buf, col_sem, row_sem, tile_sem):
    live = meta[0]
    own_tile = meta[1]
    own_offset = meta[2]

    def row_copy(t):
        slot = lax.rem(t, 3)
        return pltpu.make_async_copy(
            rows.at[lax.rem(ids[t], ROWS)], row_buf.at[slot], row_sem.at[slot]
        )

    def col_copy(j):
        return pltpu.make_async_copy(cols.at[j], col_buf.at[j], col_sem.at[j])

    def tile_copy(t):
        return pltpu.make_async_copy(
            tile_buf.at[ids[t]], weights.at[ids[t]], tile_sem.at[ids[t]]
        )

    col_copy(0).start()
    for first in range(2):
        @pl.when(first < live)
        def _():
            row_copy(first).start()
    for j in range(1, BLOCKS):
        col_copy(j).start()
    degree[...] = jnp.zeros_like(degree)
    gap = (
        lax.broadcasted_iota(jnp.int32, (PIECE, WIDTH), 1)
        - lax.broadcasted_iota(jnp.int32, (PIECE, WIDTH), 0)
    )

    def block(j, carry):
        col_copy(j).wait()

        def tile(t, inner_carry):
            @pl.when(t + 2 < live)
            def _():
                row_copy(t + 2).start()

            row_copy(t).wait()
            a = lax.rem(ids[t], ROWS)
            inner = lax.dot_general(
                row_buf[lax.rem(t, 3)], col_buf[j], (((1,), (1,)), ((), ())),
                preferred_element_type=jnp.float32,
            )
            ratio = inner / (
                WEIGHT_ROW * row_sq[a]
                + WEIGHT_COL * col_sq[j]
                + WEIGHT_SHARED * inner
                + EPSILON
            )
            offset = jnp.where(ids[t] == own_tile, own_offset, -2 * WIDTH)
            value = jnp.where(gap == offset, 0.0, jnp.exp(SHARPNESS * (ratio - 0.5)))
            tile_buf[ids[t]] = value.astype(jnp.bfloat16)
            tile_copy(t).start()
            degree[a] += (
                value[:, :128] + value[:, 128:256] + value[:, 256:384] + value[:, 384:]
            )
            return inner_carry

        return lax.fori_loop(starts[j], starts[j + 1], tile, carry)

    lax.fori_loop(0, BLOCKS, block, 0)

    def finish(t, carry):
        tile_copy(t).wait()
        return carry

    lax.fori_loop(0, live, finish, 0)


def build_weights(ids, meta, starts, rows, cols, row_sq, col_sq):
    smem = pl.BlockSpec(memory_space=pltpu.SMEM)
    vmem = pl.BlockSpec(memory_space=pltpu.VMEM)
    hbm = pl.BlockSpec(memory_space=pl.ANY)
    depth = rows.shape[-1]
    return pl.pallas_call(
        weights_kernel,
        out_shape=(
            jax.ShapeDtypeStruct((TILES, PIECE, WIDTH), jnp.bfloat16),
            jax.ShapeDtypeStruct((ROWS, PIECE, 128), jnp.float32),
        ),
        in_specs=[smem, smem, smem, hbm, hbm, vmem, vmem],
        out_specs=(hbm, vmem),
        scratch_shapes=[
            pltpu.VMEM((BLOCKS, WIDTH, depth), jnp.bfloat16),
            pltpu.VMEM((3, PIECE, depth), jnp.bfloat16),
            pltpu.VMEM((TILES, PIECE, WIDTH), jnp.bfloat16),
            pltpu.SemaphoreType.DMA((BLOCKS,)),
            pltpu.SemaphoreType.DMA((3,)),
            pltpu.SemaphoreType.DMA((TILES,)),
        ],
        compiler_params=pltpu.CompilerParams(vmem_limit_bytes=VMEM_LIMIT),
        name="weights",
    )(ids, meta, starts, rows, cols, row_sq, col_sq)


def spread_kernel(ids, meta, weights, labels, keep, send, total, tile_buf, tile_sem):
    live = meta[0]
    core = meta[3]
    half = ROWS // 2

    def tile_copy(t):
        return pltpu.make_async_copy(
            weights.at[ids[t]], tile_buf.at[ids[t]], tile_sem.at[ids[t]]
        )

    def begin(t, carry):
        tile_copy(t).start()
        return carry

    lax.fori_loop(0, live, begin, 0)
    total[...] = jnp.zeros_like(total)

    def tile(t, carry):
        tile_copy(t).wait()
        total[lax.rem(ids[t], ROWS)] += jnp.dot(
            tile_buf[ids[t]], labels[ids[t] // ROWS], preferred_element_type=jnp.float32
        )
        return carry

    lax.fori_loop(0, live, tile, 0)
    for piece in range(half):
        keep[piece] = total[core * half + piece]
        send[piece] = total[(1 - core) * half + piece].astype(jnp.bfloat16)


def spread_rows(ids, meta, weights, labels):
    smem = pl.BlockSpec(memory_space=pltpu.SMEM)
    vmem = pl.BlockSpec(memory_space=pltpu.VMEM)
    hbm = pl.BlockSpec(memory_space=pl.ANY)
    tasks = labels.shape[-1]
    return pl.pallas_call(
        spread_kernel,
        out_shape=(
            jax.ShapeDtypeStruct((ROWS // 2, PIECE, tasks), jnp.float32),
            jax.ShapeDtypeStruct((ROWS // 2, PIECE, tasks), jnp.bfloat16),
        ),
        in_specs=[smem, smem, hbm, vmem],
        out_specs=(vmem, vmem),
        scratch_shapes=[
            pltpu.VMEM((ROWS, PIECE, tasks), jnp.float32),
            pltpu.VMEM((TILES, PIECE, WIDTH), jnp.bfloat16),
            pltpu.SemaphoreType.DMA((TILES,)),
        ],
        compiler_params=pltpu.CompilerParams(vmem_limit_bytes=VMEM_LIMIT),
        name="spread",
    )(ids, meta, weights, labels)


def swap_cores(value):
    return lax.ppermute(value, "core", [(0, 1), (1, 0)])


def gather_labels(labels):
    copies = jnp.broadcast_to(labels[None], (ROWS,) + labels.shape)
    return lax.all_to_all(copies, PLANE, 0, 0).reshape(BLOCKS, WIDTH, labels.shape[1])


def body(fingerprints, activity, label_mask, pattern, counts):
    y, xh, z, xl, core = [lax.axis_index(axis) for axis in AXES]
    depth = fingerprints.shape[1]
    slots = pattern.shape[1]
    rows = lax.all_gather(fingerprints, LINE, axis=0, tiled=True).reshape(ROWS, PIECE, depth)
    cols = lax.all_gather(fingerprints, PLANE, axis=0, tiled=True).reshape(BLOCKS, WIDTH, depth)
    squares = jnp.sum(jnp.square(fingerprints.astype(jnp.float32)), axis=1)

    table = jnp.concatenate([counts[:, None], pattern], axis=1).astype(jnp.float32).reshape(-1)
    packed = jnp.concatenate([squares, table, jnp.zeros((PIECE - table.size,), jnp.float32)])
    line_info = lax.all_gather(packed, LINE, axis=0)
    row_sq = line_info[:, :PIECE].reshape(ROWS, PIECE, 1)
    tables = line_info[:, PIECE:PIECE + table.size].reshape(ROWS, 2, slots + 1).astype(jnp.int32)
    mine = lax.dynamic_index_in_dim(tables, y // 2, 1, keepdims=False)
    col_sq = lax.all_gather(squares, PLANE, axis=0, tiled=True).reshape(BLOCKS, 1, WIDTH)

    j = jnp.arange(BLOCKS, dtype=jnp.int32)
    col_block = (z * 4 + (j // 2) * 2 + core) * 2 + j % 2
    hit = (mine[None, :, 1:] == col_block[:, None, None]) & (
        jnp.arange(slots, dtype=jnp.int32)[None, None, :] < mine[None, :, :1]
    )
    live = jnp.any(hit, axis=2)
    flat = live.reshape(TILES).astype(jnp.int32)
    order = jnp.arange(TILES, dtype=jnp.int32)
    before = jnp.sum(jnp.where(order[None, :] < order[:, None], flat[None, :], 0), axis=1)
    ids = jnp.sum(
        jnp.where((before[None, :] == order[:, None]) & (flat[None, :] > 0), order[None, :], 0),
        axis=1,
    ).astype(jnp.int32)
    starts = jnp.sum(
        jnp.where(
            order[None, :] < (jnp.arange(8, dtype=jnp.int32) * ROWS)[:, None], flat[None, :], 0
        ),
        axis=1,
    ).astype(jnp.int32)
    own_tile = (xl * 2 + y // 2) * ROWS + core * 8 + z
    own_offset = ((y % 2) * 2 + xh) * PIECE
    meta = jnp.stack([jnp.sum(flat), own_tile, own_offset, core]).astype(jnp.int32)

    seeded = activity.astype(jnp.float32) * label_mask.astype(jnp.float32)[:, None]
    labels = seeded.astype(jnp.bfloat16)
    gathered = gather_labels(labels)
    weights, degree = build_weights(ids, meta, starts, rows, cols, row_sq, col_sq)

    degree = jnp.sum(degree, axis=2)
    degree_keep = lax.dynamic_slice_in_dim(degree, core * 8, 8, 0)
    degree_send = lax.dynamic_slice_in_dim(degree, (1 - core) * 8, 8, 0)
    degree_sum = degree_keep + swap_cores(degree_send)
    high = lax.reduce_precision(degree_sum, 8, 7)
    low = degree_sum - high
    degree_rows = jnp.concatenate([high, low], axis=1).astype(jnp.bfloat16)[:, None, :]
    degree_rows = jnp.concatenate(
        [degree_rows, jnp.zeros((8, 15, 2 * PIECE), jnp.bfloat16)], axis=1
    )

    for iteration in range(ITERS):
        keep, send = spread_rows(ids, meta, weights, gathered)
        part = (keep + swap_cores(send).astype(jnp.float32)).astype(jnp.bfloat16)
        if iteration == 0:
            part = jnp.concatenate([part, degree_rows], axis=1)
        parts = lax.all_to_all(part, "z", 0, 0)
        summed = jnp.sum(parts.astype(jnp.float32), axis=0)
        if iteration == 0:
            degree_own = summed[PIECE, :PIECE] + summed[PIECE, PIECE:]
            summed = summed[:PIECE]
        labels = (PROPAGATE * summed / degree_own[:, None] + ANCHOR * seeded).astype(jnp.bfloat16)
        if iteration < ITERS - 1:
            gathered = gather_labels(labels)
    return labels


def solution(mesh):
    split = Mesh(mesh.devices.reshape(SIZES), AXES)
    whole = ("z", "xl", "core", "y", "xh")
    blocks = ("z", "xl", "core")
    placed = (P(whole, None), P(whole, None), P(whole), P(blocks, None), P(blocks))
    return jax.shard_map(
        body, mesh=split, in_specs=placed, out_specs=P(whole, None), check_vma=False
    )
```

time: 1000 us -> 421 us (0.42); the launches traced: 1020 us -> 419 us
  waiting for transfers between devices: 802 us -> 191 us
  blocking collectives: 28 us -> 172 us
  loops' own time: 70.5 us -> 0 us
  local copies, waits for them, and re-layouts: 57.4 us -> 2.38 us
  matrix products: 26.6 us -> 0 us
  Pallas kernels: 0 us -> 21.1 us
  starting transfers between devices: 0.29 us -> 13.7 us
  other arithmetic: 18.3 us -> 6.12 us
    reduce_scatter x3 -> x0, waiting for transfers between devices: 484 us -> none  [body(): lax.psum_scatter(spread_all, 'row', scatter_dimension=0, tiled=True)]
    all_gather x5 -> x2, waiting for transfers between devices: 316 us -> 185 us  [the longest x1 185 us: body(): lax.all_gather(fingerprints, PLANE, axis=0, tiled=True)]
    all_to_all x0 -> x5, blocking collectives: none -> 109 us  [the longest x3 73.7 us: body(): parts = lax.all_to_all(part, 'z', 0, 0)]
    another operation x52 -> x0, loops' own time: 70.5 us -> none  [the longest x6 45.1 us: slot_per_row_block(): lax.fori_loop(0, counts[row_block], slot_per_slot, start_state)]
    all_gather x0 -> x2, blocking collectives: none -> 62.6 us  [the longest x1 32.1 us: body(): lax.all_gather(squares, PLANE, axis=0, tiled=True).reshape(BLOCKS, 1, WIDTH)]
    dynamic_slice x64 -> x3, local copies, waits for them, and re-layouts: 40.6 us -> 0.11 us  [the longest x2 0.1 us: body(): mine = lax.dynamic_index_in_dim(tables, y // 2, 1, keepdims=False)]
    unnamed x1 -> x0, blocking collectives: 28 us -> none
    dot_general x16 -> x0, matrix products: 26.6 us -> none  [the longest x12 13.6 us: action(): jnp.dot(weights, labels_here, preferred_element_type=jnp.float32)]
  transfers between devices with their start and end apart: 8 -> 7, of which waited for: 8 -> 5; matrix products, arithmetic and copies ran while one was open for 5% -> 2% of each run, Pallas kernels for 0% -> 2%
where the time goes in v1:
time: 421 us; the launch traced here: 419 us
  waiting for transfers between devices  191 us (45%)
  blocking collectives  172 us (41%)
  Pallas kernels  21.1 us (5%)
  starting transfers between devices  13.7 us (3%)
  between operations  13.7 us (3%)
  other arithmetic  6.12 us (1%)
    all_gather x1, waiting for transfers between devices, body(): lax.all_gather(fingerprints, PLANE, axis=0, tiled=True)  185 us
    all_to_all x3, blocking collectives, body(): parts = lax.all_to_all(part, 'z', 0, 0)  73.7 us
    all_to_all x2, blocking collectives, gather_labels(): lax.all_to_all(copies, PLANE, 0, 0).reshape(BLOCKS, WIDTH, labels.shape[1])  35.5 us
    all_gather x1, blocking collectives, body(): lax.all_gather(squares, PLANE, axis=0, tiled=True).reshape(BLOCKS, 1, WIDTH)  32.1 us
    all_gather x1, blocking collectives, body(): line_info = lax.all_gather(packed, LINE, axis=0)  30.5 us
    pallas_call x3, Pallas kernels, spread_rows(): pl.pallas_call(spread_kernel, out_shape=(jax.ShapeDtypeStruct((ROWS // 2,...  10.8 us
    pallas_call x1, Pallas kernels, build_weights(): pl.pallas_call(weights_kernel, out_shape=(jax.ShapeDtypeStruct((TILES, PI...  10.2 us
  transfers between devices with their start and end apart: 7, of which 5 were waited for; matrix products, arithmetic and copies ran while one was open for 2% of the time, Pallas kernels for 2%

profile of v1, /device:TPU:1, one launch (start us, length us, event | category | flops | bytes accessed | tf_op | source)
XLA Modules:
  0.0 419.3 jit_solution(3819404056087894609)
XLA Ops:
  6.5 0.7 all-gather.6.cloned.1.call-update
  7.3 0.7 all-gather.8.cloned.1.call-update
  8.7 0.9 fusion.3
  9.6 1.2 broadcast_in_dim.46
  10.8 7.7 %all-to-all-start = ((bf16[16,128,256]{2,1,0:T(8,128)(2,1)}), bf16[16,128,256]{2,1,0:T(8,128)(2,1)S(1)}, u32[]{:S(2)}, u32[]{:S(2)}) async-start(bf16[16,128,256]{2,1,0:T(8,128)(2,1)} %broadcast_in_dim.46), calls=%async_computation | async-start | bytes 2097152 | tf_op jit(solution)/shard_map/all_to_all | solution.py:188
  19.1 30.5 %all-gather.1 = f32[16,1,256]{2,1,0:T(1,128)S(1)} all-gather(f32[1,1,256]{2,1,0:T(1,128)S(1)} %bitcast.38), channel_id=2, replica_groups=mesh['y'=4,'xh'=2,'z'=8,'xl'=2,'core'=2] {'core','z'}, dimensions={0}, use_global_device_ids=true | all-gather | bytes 17408 | tf_op jit(solution)/shard_map/all_gather | solution.py:201
  50.6 32.1 %all-gather.2 = f32[16,1,128]{2,1,0:T(1,128)S(1)} all-gather(f32[1,1,128]{2,1,0:T(1,128)S(1)} %bitcast.37), channel_id=1, replica_groups=mesh['y'=4,'xh'=2,'z'=8,'xl'=2,'core'=2] {'xl','y','xh'}, dimensions={0}, use_global_device_ids=true | all-gather | bytes 8704 | tf_op jit(solution)/shard_map/all_gather | solution.py:205
  83.4 0.7 pad_add_fusion.meta
  84.6 185.0 %all-gather.8.cloned.1.call-done = bf16[2048,2048]{1,0:T(8,128)(2,1)} async-done(((bf16[128,2048]{1,0:T(8,128)(2,1)}), bf16[2048,2048]{1,0:T(8,128)(2,1)}) %all-gather.8.cloned.1.call-update) | async-done | bytes 8388624 | tf_op jit(solution)/shard_map/all_gather | solution.py:196
  269.6 10.2 %weights.1 = (bf16[64,128,512]{2,1,0:T(8,128)(2,1)}, f32[16,128,128]{2,1,0:T(8,128)S(1)}) custom-call(s32[64]{0:T(128)S(1)} %select_reduce_fusion.ids, s32[4]{0:T(128)S(1)} %pad_add_fusion.meta, s32[8]{0:T(128)S(1)} %select_reduce_fusion.2.starts, bf16[16,128,2048]{2,1,0:T(8,128)(2,1)} %bitcast.31, bf16[4,512,2048]{2,1,0:T(8,128)(2,1)} %bitcast.32, ...), custom_call_target="tpu_custom_call" | custom-call | tf_op jit(solution)/shard_map/weights/pallas_call | solution.py:108
  279.8 4.1 spread.3
  285.1 0.9 collective-permute-done.1
  286.5 32.9 %all_to_all.30 = bf16[8,144,256]{2,1,0:T(8,128)(2,1)S(1)} all-to-all(bf16[8,144,256]{2,1,0:T(8,128)(2,1)S(1)} %maximum_maximum_fusion), channel_id=1, replica_groups=mesh['y'=4,'xh'=2,'z'=8,'xl'=2,'core'=2] {'z'}, dimensions={0} | all-to-all | bytes 1179648 | tf_op jit(solution)/shard_map/all_to_all | solution.py:251
  319.8 17.0 %all_to_all.31 = bf16[16,128,256]{2,1,0:T(8,128)(2,1)S(1)} all-to-all(bf16[16,128,256]{2,1,0:T(8,128)(2,1)S(1)} %broadcast_in_dim.48), channel_id=1, replica_groups=mesh['y'=4,'xh'=2,'z'=8,'xl'=2,'core'=2] {'xl','y','xh'}, dimensions={0} | all-to-all | bytes 2097152 | tf_op jit(solution)/shard_map/all_to_all | solution.py:188
  336.8 3.4 spread.4
  340.1 2.9 collective-permute-start.2
  343.1 1.5 collective-permute-done.2
  344.7 20.4 %all_to_all.32 = bf16[8,128,256]{2,1,0:T(8,128)(2,1)S(1)} all-to-all(bf16[8,128,256]{2,1,0:T(8,128)(2,1)S(1)} %add_convert_fusion.1), channel_id=1, replica_groups=mesh['y'=4,'xh'=2,'z'=8,'xl'=2,'core'=2] {'z'}, dimensions={0} | all-to-all | bytes 1048576 | tf_op jit(solution)/shard_map/all_to_all | solution.py:251
  365.4 18.5 %all_to_all.33 = bf16[16,128,256]{2,1,0:T(8,128)(2,1)S(1)} all-to-all(bf16[16,128,256]{2,1,0:T(8,128)(2,1)S(1)} %broadcast_in_dim.49), channel_id=1, replica_groups=mesh['y'=4,'xh'=2,'z'=8,'xl'=2,'core'=2] {'xl','y','xh'}, dimensions={0} | all-to-all | bytes 2097152 | tf_op jit(solution)/shard_map/all_to_all | solution.py:188
  383.9 3.4 spread.5
  387.3 2.3 collective-permute-start.3
  389.6 1.5 collective-permute-done.3
  391.3 20.4 %all_to_all.34 = bf16[8,128,256]{2,1,0:T(8,128)(2,1)S(1)} all-to-all(bf16[8,128,256]{2,1,0:T(8,128)(2,1)S(1)} %add_convert_fusion), channel_id=1, replica_groups=mesh['y'=4,'xh'=2,'z'=8,'xl'=2,'core'=2] {'z'}, dimensions={0} | all-to-all | bytes 1048576 | tf_op jit(solution)/shard_map/all_to_all | solution.py:251
  411.8 0.7 add_convert_fusion.3
  (62 shorter events, 5.9 us)
Async XLA Ops:
  6.5 78.0 %all-gather.6.cloned.1.call-start = ((), (), s32[]{:S(2)}) async-start(), calls=%async_computation.6 | async-start | bytes 8912896 | tf_op jit(solution)/shard_map/all_gather | solution.py:195
  7.3 262.3 %all-gather.8.cloned.1.call-start = ((), (), s32[]{:S(2)}) async-start(), calls=%async_computation.7 | async-start | bytes 8912896 | tf_op jit(solution)/shard_map/all_gather | solution.py:196
  10.8 7.8 %copy-start.3 = (s32[2]{0:T(128)S(1)}, s32[2]{0:T(128)}, u32[]{:S(2)}) copy-start(s32[2]{0:T(128)} %param.9) | copy-start | bytes 28
  10.8 7.9 %copy-start.2 = (s32[2,24]{1,0:T(2,128)S(1)}, s32[2,24]{1,0:T(2,128)}, u32[]{:S(2)}) copy-start(s32[2,24]{1,0:T(2,128)} %param.8) | copy-start | bytes 580
  10.8 8.0 %copy-start = (bf16[128,2048]{1,0:T(8,128)(2,1)S(1)}, bf16[128,2048]{1,0:T(8,128)(2,1)}, u32[]{:S(2)}) copy-start(bf16[128,2048]{1,0:T(8,128)(2,1)} %param.5) | copy-start | bytes 1572868
  10.8 269.1 %all-to-all-start = ((bf16[16,128,256]{2,1,0:T(8,128)(2,1)}), bf16[16,128,256]{2,1,0:T(8,128)(2,1)S(1)}, u32[]{:S(2)}, u32[]{:S(2)}) async-start(bf16[16,128,256]{2,1,0:T(8,128)(2,1)} %broadcast_in_dim.46), calls=%async_computation | async-start | bytes 2097152 | tf_op jit(solution)/shard_map/all_to_all | solution.py:188
  284.0 2.2 collective-permute-start
  284.5 1.5 collective-permute-start.1
  286.5 33.0 %copy-start.1 = (bf16[128,256]{1,0:T(8,128)(2,1)S(1)}, bf16[128,256]{1,0:T(8,128)(2,1)}, u32[]{:S(2)}) copy-start(bf16[128,256]{1,0:T(8,128)(2,1)} %param.6) | copy-start | bytes 196612
  340.1 4.5 %collective-permute-start.2 = (bf16[8,128,256]{2,1,0:T(8,128)(2,1)S(1)}, bf16[8,128,256]{2,1,0:T(8,128)(2,1)S(1)}, u32[]{:S(2)}, u32[]{:S(2)}) collective-permute-start(bf16[8,128,256]{2,1,0:T(8,128)(2,1)S(1)} %get-tuple-element.18), channel_id=1, source_target_pairs={{0,1},{1,0},{2,3},{3,2},{4,5},{5,4},{6,7},{7,6},{8,9},{9,8},{10,11... | collective-permute-start | bytes 1572872 | tf_op jit(solution)/shard_map/ppermute | solution.py:183
  387.3 3.8 collective-permute-start.3
Sparse Core Ops, SparseCore 0:
  9.2 60.2 all-gather.5
  71.3 198.2 all-gather.7

commit v2 on v1

--- a/solution.py
+++ b/solution.py
@@ -17,7 +17,6 @@
 
 AXES = ("y", "xh", "z", "xl", "core")
 SIZES = (4, 2, 8, 2, 2)
-LINE = ("core", "z")
 PLANE = ("xl", "y", "xh")
 PIECE = 128
 ROWS = 16
@@ -27,20 +26,35 @@
 VMEM_LIMIT = 48 * 1024 * 1024
 
 
-def weights_kernel(ids, meta, starts, rows, cols, row_sq, col_sq, weights, degree,
-                   col_buf, row_buf, tile_buf, col_sem, row_sem, tile_sem):
+def weights_kernel(*refs):
+    ids, meta, starts = refs[:3]
+    rows = refs[3:3 + ROWS]
+    (cols, row_sq, weights, degree, col_buf, row_buf, tile_buf, col_sq,
+     col_sem, row_sem, tile_sem) = refs[3 + ROWS:]
     live = meta[0]
-    own_tile = meta[1]
-    own_offset = meta[2]
-
-    def row_copy(t):
+    own_offset = meta[1]
+    own_tile = meta[2]
+
+    def start_row(t):
         slot = lax.rem(t, 3)
+        wanted = lax.rem(ids[t], ROWS)
+        for a in range(ROWS):
+            @pl.when(wanted == a)
+            def _():
+                pltpu.make_async_copy(
+                    rows[a].at[pl.ds(0, PIECE)], row_buf.at[slot], row_sem.at[slot]
+                ).start()
+
+    def wait_row(t):
+        slot = lax.rem(t, 3)
+        pltpu.make_async_copy(
+            rows[0].at[pl.ds(0, PIECE)], row_buf.at[slot], row_sem.at[slot]
+        ).wait()
+
+    def col_copy(j):
         return pltpu.make_async_copy(
-            rows.at[lax.rem(ids[t], ROWS)], row_buf.at[slot], row_sem.at[slot]
+            cols.at[j % 2, :, j // 2], col_buf.at[j], col_sem.at[j]
         )
-
-    def col_copy(j):
-        return pltpu.make_async_copy(cols.at[j], col_buf.at[j], col_sem.at[j])
 
     def tile_copy(t):
         return pltpu.make_async_copy(
@@ -51,7 +65,7 @@
     for first in range(2):
         @pl.when(first < live)
         def _():
-            row_copy(first).start()
+            start_row(first)
     for j in range(1, BLOCKS):
         col_copy(j).start()
     degree[...] = jnp.zeros_like(degree)
@@ -59,24 +73,39 @@
         lax.broadcasted_iota(jnp.int32, (PIECE, WIDTH), 1)
         - lax.broadcasted_iota(jnp.int32, (PIECE, WIDTH), 0)
     )
+    depth = col_buf.shape[-1]
+    ones = jnp.ones((8, 128), jnp.float32)
 
     def block(j, carry):
-        col_copy(j).wait()
+        pltpu.make_async_copy(cols.at[0, :, 0], col_buf.at[j], col_sem.at[j]).wait()
+
+        @pl.when(starts[j] < starts[j + 1])
+        def _():
+            for sub in range(WIDTH // PIECE):
+                partial = jnp.zeros((PIECE, 128), jnp.float32)
+                for part in range(depth // 128):
+                    values = col_buf[j, sub, :, part * 128:(part + 1) * 128].astype(jnp.float32)
+                    partial += values * values
+                col_sq[:, sub * PIECE:(sub + 1) * PIECE] = lax.dot_general(
+                    ones, partial, (((1,), (1,)), ((), ())),
+                    precision=lax.Precision.HIGHEST, preferred_element_type=jnp.float32,
+                )
 
         def tile(t, inner_carry):
             @pl.when(t + 2 < live)
             def _():
-                row_copy(t + 2).start()
-
-            row_copy(t).wait()
+                start_row(t + 2)
+
+            wait_row(t)
             a = lax.rem(ids[t], ROWS)
             inner = lax.dot_general(
-                row_buf[lax.rem(t, 3)], col_buf[j], (((1,), (1,)), ((), ())),
+                row_buf[lax.rem(t, 3)], col_buf[j].reshape(WIDTH, depth),
+                (((1,), (1,)), ((), ())),
                 preferred_element_type=jnp.float32,
             )
             ratio = inner / (
                 WEIGHT_ROW * row_sq[a]
-                + WEIGHT_COL * col_sq[j]
+                + WEIGHT_COL * col_sq[0:1, :]
                 + WEIGHT_SHARED * inner
                 + EPSILON
             )
@@ -100,35 +129,41 @@
     lax.fori_loop(0, live, finish, 0)
 
 
-def build_weights(ids, meta, starts, rows, cols, row_sq, col_sq):
+def build_weights(ids, meta, starts, rows, cols, row_sq):
     smem = pl.BlockSpec(memory_space=pltpu.SMEM)
     vmem = pl.BlockSpec(memory_space=pltpu.VMEM)
     hbm = pl.BlockSpec(memory_space=pl.ANY)
-    depth = rows.shape[-1]
+    depth = cols.shape[-1]
     return pl.pallas_call(
         weights_kernel,
         out_shape=(
             jax.ShapeDtypeStruct((TILES, PIECE, WIDTH), jnp.bfloat16),
             jax.ShapeDtypeStruct((ROWS, PIECE, 128), jnp.float32),
         ),
-        in_specs=[smem, smem, smem, hbm, hbm, vmem, vmem],
+        in_specs=[smem, smem, smem] + [hbm] * ROWS + [hbm, vmem],
         out_specs=(hbm, vmem),
         scratch_shapes=[
-            pltpu.VMEM((BLOCKS, WIDTH, depth), jnp.bfloat16),
+            pltpu.VMEM((BLOCKS, WIDTH // PIECE, PIECE, depth), jnp.bfloat16),
             pltpu.VMEM((3, PIECE, depth), jnp.bfloat16),
             pltpu.VMEM((TILES, PIECE, WIDTH), jnp.bfloat16),
+            pltpu.VMEM((8, WIDTH), jnp.float32),
             pltpu.SemaphoreType.DMA((BLOCKS,)),
             pltpu.SemaphoreType.DMA((3,)),
             pltpu.SemaphoreType.DMA((TILES,)),
         ],
         compiler_params=pltpu.CompilerParams(vmem_limit_bytes=VMEM_LIMIT),
+        cost_estimate=pl.CostEstimate(
+            flops=16 * 2 * PIECE * WIDTH * depth,
+            bytes_accessed=2 * (ROWS + 16) * PIECE * depth,
+            transcendentals=16 * PIECE * WIDTH,
+        ),
         name="weights",
-    )(ids, meta, starts, rows, cols, row_sq, col_sq)
+    )(ids, meta, starts, *rows, cols, row_sq)
 
 
 def spread_kernel(ids, meta, weights, labels, keep, send, total, tile_buf, tile_sem):
     live = meta[0]
-    core = meta[3]
+    z = meta[3]
     half = ROWS // 2
 
     def tile_copy(t):
@@ -152,8 +187,9 @@
 
     lax.fori_loop(0, live, tile, 0)
     for piece in range(half):
-        keep[piece] = total[core * half + piece]
-        send[piece] = total[(1 - core) * half + piece].astype(jnp.bfloat16)
+        place = lax.rem(z - piece + half, half)
+        keep[piece] = total[place]
+        send[piece] = total[half + place].astype(jnp.bfloat16)
 
 
 def spread_rows(ids, meta, weights, labels):
@@ -192,17 +228,35 @@
     y, xh, z, xl, core = [lax.axis_index(axis) for axis in AXES]
     depth = fingerprints.shape[1]
     slots = pattern.shape[1]
-    rows = lax.all_gather(fingerprints, LINE, axis=0, tiled=True).reshape(ROWS, PIECE, depth)
-    cols = lax.all_gather(fingerprints, PLANE, axis=0, tiled=True).reshape(BLOCKS, WIDTH, depth)
+    cols = lax.all_gather(fingerprints, ("y", "xh", "xl"), axis=0, tiled=True)
+    cols = cols.reshape(2, 4, 2, PIECE, depth)
+
     squares = jnp.sum(jnp.square(fingerprints.astype(jnp.float32)), axis=1)
-
-    table = jnp.concatenate([counts[:, None], pattern], axis=1).astype(jnp.float32).reshape(-1)
-    packed = jnp.concatenate([squares, table, jnp.zeros((PIECE - table.size,), jnp.float32)])
-    line_info = lax.all_gather(packed, LINE, axis=0)
-    row_sq = line_info[:, :PIECE].reshape(ROWS, PIECE, 1)
-    tables = line_info[:, PIECE:PIECE + table.size].reshape(ROWS, 2, slots + 1).astype(jnp.int32)
-    mine = lax.dynamic_index_in_dim(tables, y // 2, 1, keepdims=False)
-    col_sq = lax.all_gather(squares, PLANE, axis=0, tiled=True).reshape(BLOCKS, 1, WIDTH)
+    square_high = lax.reduce_precision(squares, 8, 7)
+    square_mid = lax.reduce_precision(squares - square_high, 8, 7)
+    square_low = squares - square_high - square_mid
+    table = jnp.concatenate([counts[:, None], pattern], axis=1).reshape(-1)
+    info = jnp.concatenate([
+        square_high, square_mid, square_low, table.astype(jnp.float32),
+        jnp.zeros((depth - 3 * PIECE - table.size,), jnp.float32),
+    ]).astype(jnp.bfloat16)
+    extended = jnp.concatenate(
+        [fingerprints, info[None], jnp.zeros((15, depth), jnp.bfloat16)], axis=0
+    )
+    upward = [extended]
+    for step in range(4):
+        upward.append(lax.ppermute(upward[-1], "z", [(i, (i + 1) % 8) for i in range(8)]))
+    downward = [extended]
+    for step in range(3):
+        downward.append(lax.ppermute(downward[-1], "z", [(i, (i + 7) % 8) for i in range(8)]))
+    rows = upward + [downward[3], downward[2], downward[1]]
+    rows = rows + [swap_cores(row) for row in rows]
+    line_info = jnp.stack([row[PIECE] for row in rows]).astype(jnp.float32)
+    row_sq = (
+        line_info[:, :PIECE] + line_info[:, PIECE:2 * PIECE] + line_info[:, 2 * PIECE:3 * PIECE]
+    )[:, :, None]
+    tables = line_info[:, 3 * PIECE:3 * PIECE + table.size].reshape(ROWS, 2, slots + 1)
+    mine = lax.dynamic_index_in_dim(tables.astype(jnp.int32), y // 2, 1, keepdims=False)
 
     j = jnp.arange(BLOCKS, dtype=jnp.int32)
     col_block = (z * 4 + (j // 2) * 2 + core) * 2 + j % 2
@@ -223,19 +277,19 @@
         ),
         axis=1,
     ).astype(jnp.int32)
-    own_tile = (xl * 2 + y // 2) * ROWS + core * 8 + z
+    own_tile = (xl * 2 + y // 2) * ROWS
     own_offset = ((y % 2) * 2 + xh) * PIECE
-    meta = jnp.stack([jnp.sum(flat), own_tile, own_offset, core]).astype(jnp.int32)
+    meta = jnp.stack([jnp.sum(flat), own_offset, own_tile, z]).astype(jnp.int32)
 
     seeded = activity.astype(jnp.float32) * label_mask.astype(jnp.float32)[:, None]
     labels = seeded.astype(jnp.bfloat16)
+    labels, cols = lax.optimization_barrier((labels, cols))
     gathered = gather_labels(labels)
-    weights, degree = build_weights(ids, meta, starts, rows, cols, row_sq, col_sq)
+    weights, degree = build_weights(ids, meta, starts, rows, cols, row_sq)
 
     degree = jnp.sum(degree, axis=2)
-    degree_keep = lax.dynamic_slice_in_dim(degree, core * 8, 8, 0)
-    degree_send = lax.dynamic_slice_in_dim(degree, (1 - core) * 8, 8, 0)
-    degree_sum = degree_keep + swap_cores(degree_send)
+    places = (z - jnp.arange(8, dtype=jnp.int32)) % 8
+    degree_sum = degree[:8][places] + swap_cores(degree[8:][places])
     high = lax.reduce_precision(degree_sum, 8, 7)
     low = degree_sum - high
     degree_rows = jnp.concatenate([high, low], axis=1).astype(jnp.bfloat16)[:, None, :]

time: 421 us -> 274 us (0.65)
  waiting for transfers between devices: 191 us -> 46.6 us
  blocking collectives: 172 us -> 101 us
  local copies, waits for them, and re-layouts: 2.38 us -> 32.8 us
  starting transfers between devices: 13.7 us -> 44 us
  other arithmetic: 6.12 us -> 13.6 us
    all_gather x2 -> x1, waiting for transfers between devices: 185 us -> 0.01 us  [body(): cols = lax.all_gather(fingerprints, ('y', 'xh', 'xl'), axis=0, tiled=True)]
    all_gather x2 -> x0, blocking collectives: 62.6 us -> none  [the longest x1 32.1 us: body(): lax.all_gather(squares, PLANE, axis=0, tiled=True).reshape(BLOCKS, 1, WIDTH)]
    ppermute x0 -> x7, waiting for transfers between devices: none -> 42.2 us  [the longest x4 41.5 us: body(): lax.ppermute(upward[-1], 'z', [(i, (i + 1) % 8) for i in range(8)])]
    ppermute x4 -> x12, starting transfers between devices: 5.9 us -> 24.8 us  [swap_cores(): return lax.ppermute(value, 'core', [(0, 1), (1, 0)])]
    slice x0 -> x16, local copies, waits for them, and re-layouts: none -> 16 us  [the longest x15 16 us: body(): line_info = jnp.stack([row[PIECE] for row in rows]).astype(jnp.float32)]
    ppermute x0 -> x7, starting transfers between devices: none -> 12.2 us  [the longest x3 9.67 us: body(): lax.ppermute(downward[-1], 'z', [(i, (i + 7) % 8) for i in range(8)])]
    all_to_all x3, blocking collectives: 73.7 us -> 62.7 us  [body(): parts = lax.all_to_all(part, 'z', 0, 0)]
  transfers between devices with their start and end apart: 7 -> 21, of which waited for: 5 -> 8; matrix products, arithmetic and copies ran while one was open for 2% -> 14% of each run, Pallas kernels for 2% -> 4%
where the time goes in v2:
time: 274 us; the launch traced here: 272 us
  blocking collectives  101 us (37%)
  waiting for transfers between devices  46.6 us (17%)
  starting transfers between devices  44 us (16%)
  local copies, waits for them, and re-layouts  32.8 us (12%)
  Pallas kernels  20.1 us (7%)
  between operations  13.7 us (5%)
  other arithmetic  13.6 us (5%)
    all_to_all x3, blocking collectives, body(): parts = lax.all_to_all(part, 'z', 0, 0)  62.7 us
    ppermute x4, waiting for transfers between devices, body(): lax.ppermute(upward[-1], 'z', [(i, (i + 1) % 8) for i in range(8)])  41.5 us
    all_to_all x2, blocking collectives, gather_labels(): lax.all_to_all(copies, PLANE, 0, 0).reshape(BLOCKS, WIDTH, labels.shape[1])  38.5 us
    ppermute x12, starting transfers between devices, swap_cores(): return lax.ppermute(value, 'core', [(0, 1), (1, 0)])  24.8 us
    slice x15, local copies, waits for them, and re-layouts, body(): line_info = jnp.stack([row[PIECE] for row in rows]).astype(jnp.float32)  16 us
    pallas_call x1, Pallas kernels, build_weights(): pl.pallas_call(weights_kernel, out_shape=(jax.ShapeDtypeStruct((TILES, PI...  11.2 us
    ppermute x3, starting transfers between devices, body(): lax.ppermute(downward[-1], 'z', [(i, (i + 7) % 8) for i in range(8)])  9.67 us
    pallas_call x3, Pallas kernels, spread_rows(): pl.pallas_call(spread_kernel, out_shape=(jax.ShapeDtypeStruct((ROWS // 2,...  8.85 us
  transfers between devices with their start and end apart: 21, of which 8 were waited for; matrix products, arithmetic and copies ran while one was open for 14% of the time, Pallas kernels for 4%

profile of v2, /device:TPU:1, one launch (start us, length us, event | category | flops | bytes accessed | tf_op | source)
XLA Modules:
  0.0 271.8 jit_solution(5801134945419158746)
XLA Ops:
  10.5 2.5 collective-permute-start
  13.0 4.0 %collective-permute-start.4 = (bf16[144,2048]{1,0:T(8,128)(2,1)S(1)}, bf16[144,2048]{1,0:T(8,128)(2,1)S(1)}, u32[]{:S(2)}, u32[]{:S(2)}) collective-permute-start(bf16[144,2048]{1,0:T(8,128)(2,1)S(1)} %maximum_maximum_fusion.refs_3_), channel_id=1, source_target_pairs={{0,28},{4,0},{8,4},{12,8},{16,12},{20,16},{24,20},{28,24},{1,29},{... | collective-permute-start | bytes 1769480 | tf_op jit(solution)/shard_map/ppermute | solution.py:251
  17.0 13.0 %collective-permute-done.refs_4_ = bf16[144,2048]{1,0:T(8,128)(2,1)S(1)} collective-permute-done((bf16[144,2048]{1,0:T(8,128)(2,1)S(1)}, bf16[144,2048]{1,0:T(8,128)(2,1)S(1)}, u32[]{:S(2)}, u32[]{:S(2)}) %collective-permute-start) | collective-permute-done | bytes 589856 | tf_op jit(solution)/shard_map/ppermute | solution.py:248
  30.0 2.7 collective-permute-start.5
  32.7 12.1 %collective-permute-done.1.refs_5_ = bf16[144,2048]{1,0:T(8,128)(2,1)S(1)} collective-permute-done((bf16[144,2048]{1,0:T(8,128)(2,1)S(1)}, bf16[144,2048]{1,0:T(8,128)(2,1)S(1)}, u32[]{:S(2)}, u32[]{:S(2)}) %collective-permute-start.1) | collective-permute-done | bytes 589856 | tf_op jit(solution)/shard_map/ppermute | solution.py:248
  47.5 3.0 %collective-permute-start.6 = (bf16[144,2048]{1,0:T(8,128)(2,1)S(1)}, bf16[144,2048]{1,0:T(8,128)(2,1)}, u32[]{:S(2)}, u32[]{:S(2)}) collective-permute-start(bf16[144,2048]{1,0:T(8,128)(2,1)S(1)} %collective-permute-done.5.refs_9_), channel_id=1, source_target_pairs={{0,28},{4,0},{8,4},{12,8},{16,12},{20,16},{24,20},{28,24},{1,29},{... | collective-permute-start | bytes 1769480 | tf_op jit(solution)/shard_map/ppermute | solution.py:251
  50.4 8.3 %collective-permute-done.2.refs_6_ = bf16[144,2048]{1,0:T(8,128)(2,1)} collective-permute-done((bf16[144,2048]{1,0:T(8,128)(2,1)S(1)}, bf16[144,2048]{1,0:T(8,128)(2,1)}, u32[]{:S(2)}, u32[]{:S(2)}) %collective-permute-start.2) | collective-permute-done | bytes 589856 | tf_op jit(solution)/shard_map/ppermute | solution.py:248
  58.8 3.2 %collective-permute-start.9 = (bf16[144,2048]{1,0:T(8,128)(2,1)S(1)}, bf16[144,2048]{1,0:T(8,128)(2,1)}, u32[]{:S(2)}, u32[]{:S(2)}) collective-permute-start(bf16[144,2048]{1,0:T(8,128)(2,1)S(1)} %collective-permute-done.1.refs_5_), channel_id=1, source_target_pairs={{0,1},{1,0},{2,3},{3,2},{4,5},{5,4},{6,7},{7,6},{8,9},{9,8},{10,11... | collective-permute-start | bytes 1769480 | tf_op jit(solution)/shard_map/ppermute | solution.py:219
  64.0 8.1 %collective-permute-done.3.refs_7_ = bf16[144,2048]{1,0:T(8,128)(2,1)} collective-permute-done((bf16[144,2048]{1,0:T(8,128)(2,1)}, bf16[144,2048]{1,0:T(8,128)(2,1)}, u32[]{:S(2)}, u32[]{:S(2)}) %collective-permute-start.3) | collective-permute-done | bytes 589856 | tf_op jit(solution)/shard_map/ppermute | solution.py:248
  72.1 4.0 %collective-permute-start.11 = (bf16[144,2048]{1,0:T(8,128)(2,1)}, bf16[144,2048]{1,0:T(8,128)(2,1)}, u32[]{:S(2)}, u32[]{:S(2)}) collective-permute-start(bf16[144,2048]{1,0:T(8,128)(2,1)} %collective-permute-done.3.refs_7_), channel_id=1, source_target_pairs={{0,1},{1,0},{2,3},{3,2},{4,5},{5,4},{6,7},{7,6},{8,9},{9,8},{10,11... | collective-permute-start | bytes 1769480 | tf_op jit(solution)/shard_map/ppermute | solution.py:219
  95.3 3.0 %stack.18 = bf16[16,2048]{1,0:T(8,128)(2,1)} concatenate(bf16[1,2048]{1,0:T(2,128)(2,1)S(1)} %concatenate.48, bf16[1,2048]{1,0:T(2,128)(2,1)S(1)} %slice.108, bf16[1,2048]{1,0:T(2,128)(2,1)} %slice.109, bf16[1,2048]{1,0:T(2,128)(2,1)} %slice.110, bf16[1,2048]{1,0:T(2,128)(2,1)} %slice.111, bf16[1,2048]{1,0:T(2,128)(2,1)} %slice.112, bf16[1,2048]{1,0:T(2,128)(2,1)} %slice.113, ...), dimensions={0} | concatenate | bytes 131072 | tf_op jit(solution)/shard_map/stack | solution.py:254
  108.8 6.9 %all-to-all-start = ((bf16[16,128,256]{2,1,0:T(8,128)(2,1)}), bf16[16,128,256]{2,1,0:T(8,128)(2,1)S(1)}, u32[]{:S(2)}, u32[]{:S(2)}) async-start(bf16[16,128,256]{2,1,0:T(8,128)(2,1)} %broadcast_in_dim.52), calls=%async_computation | async-start | bytes 2097152 | tf_op jit(solution)/shard_map/all_to_all | solution.py:224
  121.6 11.2 %weights.1 = (bf16[64,128,512]{2,1,0:T(8,128)(2,1)}, f32[16,128,128]{2,1,0:T(8,128)}) custom-call(s32[64]{0:T(128)S(1)} %select_reduce_fusion.refs_0_.ids, s32[4]{0:T(128)S(1)} %pad_add_fusion.refs_1_.meta, s32[8]{0:T(128)S(1)} %select_reduce_fusion.2.refs_2_, bf16[144,2048]{1,0:T(8,128)(2,1)S(1)} %maximum_maximum_fusion.refs_3_, ...), custom_call_target="tpu_custom_call" | custom-call | flops 4294967296 | bytes 16777216 | tf_op jit(solution)/shard_map/weights/pallas_call | solution.py:137
  132.8 3.0 %spread.3 = (f32[8,128,256]{2,1,0:T(8,128)S(1)}, bf16[8,128,256]{2,1,0:T(8,128)(2,1)S(1)}) custom-call(s32[64]{0:T(128)S(1)} %select_reduce_fusion.refs_0_.ids, s32[4]{0:T(128)S(1)} %pad_add_fusion.refs_1_.meta, bf16[64,128,512]{2,1,0:T(8,128)(2,1)} %get-tuple-element.16.weights, bf16[4,512,256]{2,1,0:T(8,128)(2,1)S(1)} %bitcast.28), custom_call_target="tpu_custom_call" | custom-call | tf_op jit(solution)/shard_map/spread/pallas_call | solution.py:200
  135.8 5.9 %collective-permute-start.15 = (bf16[8,128,256]{2,1,0:T(8,128)(2,1)S(1)}, bf16[8,128,256]{2,1,0:T(8,128)(2,1)S(1)}, u32[]{:S(2)}, u32[]{:S(2)}) collective-permute-start(bf16[8,128,256]{2,1,0:T(8,128)(2,1)S(1)} %get-tuple-element.19), channel_id=1, source_target_pairs={{0,1},{1,0},{2,3},{3,2},{4,5},{5,4},{6,7},{7,6},{8,9},{9,8},{10,11... | collective-permute-start | bytes 1572872 | tf_op jit(solution)/shard_map/ppermute | solution.py:219
  145.5 21.9 %all_to_all.30 = bf16[8,144,256]{2,1,0:T(8,128)(2,1)S(1)} all-to-all(bf16[8,144,256]{2,1,0:T(8,128)(2,1)S(1)} %maximum_maximum_fusion.1), channel_id=1, replica_groups=mesh['y'=4,'xh'=2,'z'=8,'xl'=2,'core'=2] {'z'}, dimensions={0} | all-to-all | bytes 1179648 | tf_op jit(solution)/shard_map/all_to_all | solution.py:305
  167.8 20.7 %all_to_all.31 = bf16[16,128,256]{2,1,0:T(8,128)(2,1)S(1)} all-to-all(bf16[16,128,256]{2,1,0:T(8,128)(2,1)S(1)} %broadcast_in_dim.54), channel_id=1, replica_groups=mesh['y'=4,'xh'=2,'z'=8,'xl'=2,'core'=2] {'xl','y','xh'}, dimensions={0} | all-to-all | bytes 2097152 | tf_op jit(solution)/shard_map/all_to_all | solution.py:224
  188.5 3.0 %spread.4 = (f32[8,128,256]{2,1,0:T(8,128)S(1)}, bf16[8,128,256]{2,1,0:T(8,128)(2,1)S(1)}) custom-call(s32[64]{0:T(128)S(1)} %select_reduce_fusion.refs_0_.ids, s32[4]{0:T(128)S(1)} %pad_add_fusion.refs_1_.meta, bf16[64,128,512]{2,1,0:T(8,128)(2,1)} %get-tuple-element.16.weights, bf16[4,512,256]{2,1,0:T(8,128)(2,1)S(1)} %bitcast.30), custom_call_target="tpu_custom_call" | custom-call | tf_op jit(solution)/shard_map/spread/pallas_call | solution.py:200
  191.4 4.1 %collective-permute-start.17 = (bf16[8,128,256]{2,1,0:T(8,128)(2,1)S(1)}, bf16[8,128,256]{2,1,0:T(8,128)(2,1)S(1)}, u32[]{:S(2)}, u32[]{:S(2)}) collective-permute-start(bf16[8,128,256]{2,1,0:T(8,128)(2,1)S(1)} %get-tuple-element.22), channel_id=1, source_target_pairs={{0,1},{1,0},{2,3},{3,2},{4,5},{5,4},{6,7},{7,6},{8,9},{9,8},{10,11... | collective-permute-start | bytes 1572872 | tf_op jit(solution)/shard_map/ppermute | solution.py:219
  197.2 20.4 %all_to_all.32 = bf16[8,128,256]{2,1,0:T(8,128)(2,1)S(1)} all-to-all(bf16[8,128,256]{2,1,0:T(8,128)(2,1)S(1)} %add_convert_fusion.1), channel_id=1, replica_groups=mesh['y'=4,'xh'=2,'z'=8,'xl'=2,'core'=2] {'z'}, dimensions={0} | all-to-all | bytes 1048576 | tf_op jit(solution)/shard_map/all_to_all | solution.py:305
  217.8 17.8 %all_to_all.33 = bf16[16,128,256]{2,1,0:T(8,128)(2,1)S(1)} all-to-all(bf16[16,128,256]{2,1,0:T(8,128)(2,1)S(1)} %broadcast_in_dim.94), channel_id=1, replica_groups=mesh['y'=4,'xh'=2,'z'=8,'xl'=2,'core'=2] {'xl','y','xh'}, dimensions={0} | all-to-all | bytes 2097152 | tf_op jit(solution)/shard_map/all_to_all | solution.py:224
  235.6 2.9 %spread.5 = (f32[8,128,256]{2,1,0:T(8,128)S(1)}, bf16[8,128,256]{2,1,0:T(8,128)(2,1)S(1)}) custom-call(s32[64]{0:T(128)S(1)} %select_reduce_fusion.refs_0_.ids, s32[4]{0:T(128)S(1)} %pad_add_fusion.refs_1_.meta, bf16[64,128,512]{2,1,0:T(8,128)(2,1)} %get-tuple-element.16.weights, bf16[4,512,256]{2,1,0:T(8,128)(2,1)S(1)} %bitcast.29), custom_call_target="tpu_custom_call" | custom-call | tf_op jit(solution)/shard_map/spread/pallas_call | solution.py:200
  238.5 3.5 %collective-permute-start.18 = (bf16[8,128,256]{2,1,0:T(8,128)(2,1)S(1)}, bf16[8,128,256]{2,1,0:T(8,128)(2,1)S(1)}, u32[]{:S(2)}, u32[]{:S(2)}) collective-permute-start(bf16[8,128,256]{2,1,0:T(8,128)(2,1)S(1)} %get-tuple-element.24), channel_id=1, source_target_pairs={{0,1},{1,0},{2,3},{3,2},{4,5},{5,4},{6,7},{7,6},{8,9},{9,8},{10,11... | collective-permute-start | bytes 1572872 | tf_op jit(solution)/shard_map/ppermute | solution.py:219
  243.7 20.4 %all_to_all.34 = bf16[8,128,256]{2,1,0:T(8,128)(2,1)S(1)} all-to-all(bf16[8,128,256]{2,1,0:T(8,128)(2,1)S(1)} %add_convert_fusion), channel_id=1, replica_groups=mesh['y'=4,'xh'=2,'z'=8,'xl'=2,'core'=2] {'z'}, dimensions={0} | all-to-all | bytes 1048576 | tf_op jit(solution)/shard_map/all_to_all | solution.py:305
  (135 shorter events, 52.5 us)
Async XLA Ops:
  6.5 69.5 %copy-start.15 = (s32[128]{0:T(128)S(1)}, s32[128]{0:T(128)}, u32[]{:S(2)}) copy-start(s32[128]{0:T(128)} %param.7) | copy-start | bytes 1540
  6.5 100.4 %all-gather.2.cloned.1.call-start = ((), (), s32[]{:S(2)}) async-start(), calls=%async_computation.6 | async-start | bytes 8912896 | tf_op jit(solution)/shard_map/all_gather | solution.py:231
  10.5 19.5 %collective-permute-start = (bf16[144,2048]{1,0:T(8,128)(2,1)S(1)}, bf16[144,2048]{1,0:T(8,128)(2,1)S(1)}, u32[]{:S(2)}, u32[]{:S(2)}) collective-permute-start(bf16[144,2048]{1,0:T(8,128)(2,1)S(1)} %maximum_maximum_fusion.refs_3_), channel_id=1, source_target_pairs={{0,4},{4,8},{8,12},{12,16},{16,20},{20,24},{24,28},{28,0},{1,5},{5... | collective-permute-start | bytes 1769480 | tf_op jit(solution)/shard_map/ppermute | solution.py:248
  13.0 17.0 %collective-permute-start.4 = (bf16[144,2048]{1,0:T(8,128)(2,1)S(1)}, bf16[144,2048]{1,0:T(8,128)(2,1)S(1)}, u32[]{:S(2)}, u32[]{:S(2)}) collective-permute-start(bf16[144,2048]{1,0:T(8,128)(2,1)S(1)} %maximum_maximum_fusion.refs_3_), channel_id=1, source_target_pairs={{0,28},{4,0},{8,4},{12,8},{16,12},{20,16},{24,20},{28,24},{1,29},{... | collective-permute-start | bytes 1769480 | tf_op jit(solution)/shard_map/ppermute | solution.py:251
  30.0 14.8 %collective-permute-start.1 = (bf16[144,2048]{1,0:T(8,128)(2,1)S(1)}, bf16[144,2048]{1,0:T(8,128)(2,1)S(1)}, u32[]{:S(2)}, u32[]{:S(2)}) collective-permute-start(bf16[144,2048]{1,0:T(8,128)(2,1)S(1)} %collective-permute-done.refs_4_), channel_id=1, source_target_pairs={{0,4},{4,8},{8,12},{12,16},{16,20},{20,24},{24,28},{28,0},{1,5},{5... | collective-permute-start | bytes 1769480 | tf_op jit(solution)/shard_map/ppermute | solution.py:248
  30.0 17.5 %collective-permute-start.5 = (bf16[144,2048]{1,0:T(8,128)(2,1)S(1)}, bf16[144,2048]{1,0:T(8,128)(2,1)S(1)}, u32[]{:S(2)}, u32[]{:S(2)}) collective-permute-start(bf16[144,2048]{1,0:T(8,128)(2,1)S(1)} %collective-permute-done.4.refs_10_), channel_id=1, source_target_pairs={{0,28},{4,0},{8,4},{12,8},{16,12},{20,16},{24,20},{28,24},{1,29},{... | collective-permute-start | bytes 1769480 | tf_op jit(solution)/shard_map/ppermute | solution.py:251
  44.8 14.0 %collective-permute-start.2 = (bf16[144,2048]{1,0:T(8,128)(2,1)S(1)}, bf16[144,2048]{1,0:T(8,128)(2,1)}, u32[]{:S(2)}, u32[]{:S(2)}) collective-permute-start(bf16[144,2048]{1,0:T(8,128)(2,1)S(1)} %collective-permute-done.1.refs_5_), channel_id=1, source_target_pairs={{0,4},{4,8},{8,12},{12,16},{16,20},{20,24},{24,28},{28,0},{1,5},{5... | collective-permute-start | bytes 1769480 | tf_op jit(solution)/shard_map/ppermute | solution.py:248
  44.8 14.0 %collective-permute-start.7 = (bf16[144,2048]{1,0:T(8,128)(2,1)S(1)}, bf16[144,2048]{1,0:T(8,128)(2,1)S(1)}, u32[]{:S(2)}, u32[]{:S(2)}) collective-permute-start(bf16[144,2048]{1,0:T(8,128)(2,1)S(1)} %maximum_maximum_fusion.refs_3_), channel_id=1, source_target_pairs={{0,1},{1,0},{2,3},{3,2},{4,5},{5,4},{6,7},{7,6},{8,9},{9,8},{10,11... | collective-permute-start | bytes 1769480 | tf_op jit(solution)/shard_map/ppermute | solution.py:219
  47.0 15.0 %collective-permute-start.8 = (bf16[144,2048]{1,0:T(8,128)(2,1)S(1)}, bf16[144,2048]{1,0:T(8,128)(2,1)S(1)}, u32[]{:S(2)}, u32[]{:S(2)}) collective-permute-start(bf16[144,2048]{1,0:T(8,128)(2,1)S(1)} %collective-permute-done.refs_4_), channel_id=1, source_target_pairs={{0,1},{1,0},{2,3},{3,2},{4,5},{5,4},{6,7},{7,6},{8,9},{9,8},{10,11... | collective-permute-start | bytes 1769480 | tf_op jit(solution)/shard_map/ppermute | solution.py:219
  47.0 15.1 %collective-permute-start.14 = (bf16[144,2048]{1,0:T(8,128)(2,1)S(1)}, bf16[144,2048]{1,0:T(8,128)(2,1)S(1)}, u32[]{:S(2)}, u32[]{:S(2)}) collective-permute-start(bf16[144,2048]{1,0:T(8,128)(2,1)S(1)} %collective-permute-done.4.refs_10_), channel_id=1, source_target_pairs={{0,1},{1,0},{2,3},{3,2},{4,5},{5,4},{6,7},{7,6},{8,9},{9,8},{10,11... | collective-permute-start | bytes 1769480 | tf_op jit(solution)/shard_map/ppermute | solution.py:219
  47.5 61.4 %copy-start = (bf16[144,2048]{1,0:T(8,128)(2,1)}, bf16[144,2048]{1,0:T(8,128)(2,1)S(1)}, u32[]{:S(2)}) copy-start(bf16[144,2048]{1,0:T(8,128)(2,1)S(1)} %collective-permute-done.5.refs_9_) | copy-start | bytes 1769476
  47.5 15.7 %collective-permute-start.6 = (bf16[144,2048]{1,0:T(8,128)(2,1)S(1)}, bf16[144,2048]{1,0:T(8,128)(2,1)}, u32[]{:S(2)}, u32[]{:S(2)}) collective-permute-start(bf16[144,2048]{1,0:T(8,128)(2,1)S(1)} %collective-permute-done.5.refs_9_), channel_id=1, source_target_pairs={{0,28},{4,0},{8,4},{12,8},{16,12},{20,16},{24,20},{28,24},{1,29},{... | collective-permute-start | bytes 1769480 | tf_op jit(solution)/shard_map/ppermute | solution.py:251
  58.8 13.3 %collective-permute-start.3 = (bf16[144,2048]{1,0:T(8,128)(2,1)}, bf16[144,2048]{1,0:T(8,128)(2,1)}, u32[]{:S(2)}, u32[]{:S(2)}) collective-permute-start(bf16[144,2048]{1,0:T(8,128)(2,1)} %collective-permute-done.2.refs_6_), channel_id=1, source_target_pairs={{0,4},{4,8},{8,12},{12,16},{16,20},{20,24},{24,28},{28,0},{1,5},{5... | collective-permute-start | bytes 1769480 | tf_op jit(solution)/shard_map/ppermute | solution.py:248
  58.8 50.0 %copy-start.2 = (bf16[144,2048]{1,0:T(8,128)(2,1)}, bf16[144,2048]{1,0:T(8,128)(2,1)S(1)}, u32[]{:S(2)}) copy-start(bf16[144,2048]{1,0:T(8,128)(2,1)S(1)} %collective-permute-done.7.refs_11_) | copy-start | bytes 1769476
  58.8 28.3 %collective-permute-start.9 = (bf16[144,2048]{1,0:T(8,128)(2,1)S(1)}, bf16[144,2048]{1,0:T(8,128)(2,1)}, u32[]{:S(2)}, u32[]{:S(2)}) collective-permute-start(bf16[144,2048]{1,0:T(8,128)(2,1)S(1)} %collective-permute-done.1.refs_5_), channel_id=1, source_target_pairs={{0,1},{1,0},{2,3},{3,2},{4,5},{5,4},{6,7},{7,6},{8,9},{9,8},{10,11... | collective-permute-start | bytes 1769480 | tf_op jit(solution)/shard_map/ppermute | solution.py:219
  62.0 26.5 %collective-permute-start.13 = (bf16[144,2048]{1,0:T(8,128)(2,1)S(1)}, bf16[144,2048]{1,0:T(8,128)(2,1)}, u32[]{:S(2)}, u32[]{:S(2)}) collective-permute-start(bf16[144,2048]{1,0:T(8,128)(2,1)S(1)} %collective-permute-done.5.refs_9_), channel_id=1, source_target_pairs={{0,1},{1,0},{2,3},{3,2},{4,5},{5,4},{6,7},{7,6},{8,9},{9,8},{10,11... | collective-permute-start | bytes 1769480 | tf_op jit(solution)/shard_map/ppermute | solution.py:219
  62.1 29.1 %collective-permute-start.10 = (bf16[144,2048]{1,0:T(8,128)(2,1)}, bf16[144,2048]{1,0:T(8,128)(2,1)}, u32[]{:S(2)}, u32[]{:S(2)}) collective-permute-start(bf16[144,2048]{1,0:T(8,128)(2,1)} %collective-permute-done.2.refs_6_), channel_id=1, source_target_pairs={{0,1},{1,0},{2,3},{3,2},{4,5},{5,4},{6,7},{7,6},{8,9},{9,8},{10,11... | collective-permute-start | bytes 1769480 | tf_op jit(solution)/shard_map/ppermute | solution.py:219
  63.1 29.4 %collective-permute-start.12 = (bf16[144,2048]{1,0:T(8,128)(2,1)}, bf16[144,2048]{1,0:T(8,128)(2,1)}, u32[]{:S(2)}, u32[]{:S(2)}) collective-permute-start(bf16[144,2048]{1,0:T(8,128)(2,1)} %collective-permute-done.6.refs_8_), channel_id=1, source_target_pairs={{0,1},{1,0},{2,3},{3,2},{4,5},{5,4},{6,7},{7,6},{8,9},{9,8},{10,11... | collective-permute-start | bytes 1769480 | tf_op jit(solution)/shard_map/ppermute | solution.py:219
  72.1 21.8 %collective-permute-start.11 = (bf16[144,2048]{1,0:T(8,128)(2,1)}, bf16[144,2048]{1,0:T(8,128)(2,1)}, u32[]{:S(2)}, u32[]{:S(2)}) collective-permute-start(bf16[144,2048]{1,0:T(8,128)(2,1)} %collective-permute-done.3.refs_7_), channel_id=1, source_target_pairs={{0,1},{1,0},{2,3},{3,2},{4,5},{5,4},{6,7},{7,6},{8,9},{9,8},{10,11... | collective-permute-start | bytes 1769480 | tf_op jit(solution)/shard_map/ppermute | solution.py:219
  108.8 24.0 %all-to-all-start = ((bf16[16,128,256]{2,1,0:T(8,128)(2,1)}), bf16[16,128,256]{2,1,0:T(8,128)(2,1)S(1)}, u32[]{:S(2)}, u32[]{:S(2)}) async-start(bf16[16,128,256]{2,1,0:T(8,128)(2,1)} %broadcast_in_dim.52), calls=%async_computation | async-start | bytes 2097152 | tf_op jit(solution)/shard_map/all_to_all | solution.py:224
  135.8 9.4 %collective-permute-start.15 = (bf16[8,128,256]{2,1,0:T(8,128)(2,1)S(1)}, bf16[8,128,256]{2,1,0:T(8,128)(2,1)S(1)}, u32[]{:S(2)}, u32[]{:S(2)}) collective-permute-start(bf16[8,128,256]{2,1,0:T(8,128)(2,1)S(1)} %get-tuple-element.19), channel_id=1, source_target_pairs={{0,1},{1,0},{2,3},{3,2},{4,5},{5,4},{6,7},{7,6},{8,9},{9,8},{10,11... | collective-permute-start | bytes 1572872 | tf_op jit(solution)/shard_map/ppermute | solution.py:219
  143.9 1.3 collective-permute-start.16
  191.4 5.6 %collective-permute-start.17 = (bf16[8,128,256]{2,1,0:T(8,128)(2,1)S(1)}, bf16[8,128,256]{2,1,0:T(8,128)(2,1)S(1)}, u32[]{:S(2)}, u32[]{:S(2)}) collective-permute-start(bf16[8,128,256]{2,1,0:T(8,128)(2,1)S(1)} %get-tuple-element.22), channel_id=1, source_target_pairs={{0,1},{1,0},{2,3},{3,2},{4,5},{5,4},{6,7},{7,6},{8,9},{9,8},{10,11... | collective-permute-start | bytes 1572872 | tf_op jit(solution)/shard_map/ppermute | solution.py:219
  238.5 5.1 %collective-permute-start.18 = (bf16[8,128,256]{2,1,0:T(8,128)(2,1)S(1)}, bf16[8,128,256]{2,1,0:T(8,128)(2,1)S(1)}, u32[]{:S(2)}, u32[]{:S(2)}) collective-permute-start(bf16[8,128,256]{2,1,0:T(8,128)(2,1)S(1)} %get-tuple-element.24), channel_id=1, source_target_pairs={{0,1},{1,0},{2,3},{3,2},{4,5},{5,4},{6,7},{7,6},{8,9},{9,8},{10,11... | collective-permute-start | bytes 1572872 | tf_op jit(solution)/shard_map/ppermute | solution.py:219
  (14 other events, 97.7 us)
Sparse Core Ops, SparseCore 0:
  9.8 79.5 all-gather.1

commit v3 on v2

--- a/solution.py
+++ b/solution.py
@@ -19,6 +19,7 @@
 SIZES = (4, 2, 8, 2, 2)
 PLANE = ("xl", "y", "xh")
 PIECE = 128
+EXTRA = 16
 ROWS = 16
 BLOCKS = 4
 WIDTH = 512
@@ -29,8 +30,9 @@
 def weights_kernel(*refs):
     ids, meta, starts = refs[:3]
     rows = refs[3:3 + ROWS]
-    (cols, row_sq, weights, degree, col_buf, row_buf, tile_buf, col_sq,
-     col_sem, row_sem, tile_sem) = refs[3 + ROWS:]
+    (cols, row_sq, weights, keep, send, degree_keep, degree_send,
+     col_buf, row_buf, tile_buf, label_raw, labels, total, degree, col_sq,
+     col_sem, row_sem, tile_sem, label_sem) = refs[3 + ROWS:]
     live = meta[0]
     own_offset = meta[1]
     own_tile = meta[2]
@@ -42,18 +44,16 @@
             @pl.when(wanted == a)
             def _():
                 pltpu.make_async_copy(
-                    rows[a].at[pl.ds(0, PIECE)], row_buf.at[slot], row_sem.at[slot]
+                    rows[a], row_buf.at[slot], row_sem.at[slot]
                 ).start()
 
     def wait_row(t):
         slot = lax.rem(t, 3)
-        pltpu.make_async_copy(
-            rows[0].at[pl.ds(0, PIECE)], row_buf.at[slot], row_sem.at[slot]
-        ).wait()
+        pltpu.make_async_copy(rows[0], row_buf.at[slot], row_sem.at[slot]).wait()
 
     def col_copy(j):
         return pltpu.make_async_copy(
-            cols.at[j % 2, :, j // 2], col_buf.at[j], col_sem.at[j]
+            cols.at[j % 2, :, j // 2, pl.ds(0, PIECE)], col_buf.at[j], col_sem.at[j]
         )
 
     def tile_copy(t):
@@ -66,9 +66,23 @@
         @pl.when(first < live)
         def _():
             start_row(first)
+    label_copy = pltpu.make_async_copy(
+        cols.at[:, :, :, pl.ds(PIECE, EXTRA)], label_raw, label_sem
+    )
+    label_copy.start()
     for j in range(1, BLOCKS):
         col_copy(j).start()
     degree[...] = jnp.zeros_like(degree)
+    total[...] = jnp.zeros_like(total)
+    label_copy.wait()
+    tasks = labels.shape[-1]
+    for j in range(BLOCKS):
+        for sub in range(WIDTH // PIECE):
+            for group in range(PIECE // EXTRA):
+                first_row = sub * PIECE + group * EXTRA
+                labels[j, first_row:first_row + EXTRA, :] = label_raw[
+                    j % 2, sub, j // 2, :, group * tasks:(group + 1) * tasks
+                ]
     gap = (
         lax.broadcasted_iota(jnp.int32, (PIECE, WIDTH), 1)
         - lax.broadcasted_iota(jnp.int32, (PIECE, WIDTH), 0)
@@ -77,7 +91,9 @@
     ones = jnp.ones((8, 128), jnp.float32)
 
     def block(j, carry):
-        pltpu.make_async_copy(cols.at[0, :, 0], col_buf.at[j], col_sem.at[j]).wait()
+        pltpu.make_async_copy(
+            cols.at[0, :, 0, pl.ds(0, PIECE)], col_buf.at[j], col_sem.at[j]
+        ).wait()
 
         @pl.when(starts[j] < starts[j + 1])
         def _():
@@ -111,8 +127,10 @@
             )
             offset = jnp.where(ids[t] == own_tile, own_offset, -2 * WIDTH)
             value = jnp.where(gap == offset, 0.0, jnp.exp(SHARPNESS * (ratio - 0.5)))
-            tile_buf[ids[t]] = value.astype(jnp.bfloat16)
+            half = value.astype(jnp.bfloat16)
+            tile_buf[ids[t]] = half
             tile_copy(t).start()
+            total[a] += jnp.dot(half, labels[j], preferred_element_type=jnp.float32)
             degree[a] += (
                 value[:, :128] + value[:, 128:256] + value[:, 256:384] + value[:, 384:]
             )
@@ -121,12 +139,29 @@
         return lax.fori_loop(starts[j], starts[j + 1], tile, carry)
 
     lax.fori_loop(0, BLOCKS, block, 0)
+    split_rows(meta[3], total, keep, send)
+    half_rows = ROWS // 2
+    for piece in range(half_rows):
+        place = lax.rem(meta[3] - piece + half_rows, half_rows)
+        for target, where in ((degree_keep, place), (degree_send, half_rows + place)):
+            target[piece:piece + 1, :] = lax.dot_general(
+                ones, degree[where], (((1,), (1,)), ((), ())),
+                precision=lax.Precision.HIGHEST, preferred_element_type=jnp.float32,
+            )[0:1, :]
 
     def finish(t, carry):
         tile_copy(t).wait()
         return carry
 
     lax.fori_loop(0, live, finish, 0)
+
+
+def split_rows(z, total, keep, send):
+    half = ROWS // 2
+    for piece in range(half):
+        place = lax.rem(z - piece + half, half)
+        keep[piece] = total[place]
+        send[piece] = total[half + place].astype(jnp.bfloat16)
 
 
 def build_weights(ids, meta, starts, rows, cols, row_sq):
@@ -134,22 +169,31 @@
     vmem = pl.BlockSpec(memory_space=pltpu.VMEM)
     hbm = pl.BlockSpec(memory_space=pl.ANY)
     depth = cols.shape[-1]
+    tasks = depth * EXTRA // PIECE
     return pl.pallas_call(
         weights_kernel,
         out_shape=(
             jax.ShapeDtypeStruct((TILES, PIECE, WIDTH), jnp.bfloat16),
-            jax.ShapeDtypeStruct((ROWS, PIECE, 128), jnp.float32),
+            jax.ShapeDtypeStruct((ROWS // 2, PIECE, tasks), jnp.float32),
+            jax.ShapeDtypeStruct((ROWS // 2, PIECE, tasks), jnp.bfloat16),
+            jax.ShapeDtypeStruct((ROWS // 2, PIECE), jnp.float32),
+            jax.ShapeDtypeStruct((ROWS // 2, PIECE), jnp.float32),
         ),
         in_specs=[smem, smem, smem] + [hbm] * ROWS + [hbm, vmem],
-        out_specs=(hbm, vmem),
+        out_specs=(hbm, vmem, vmem, vmem, vmem),
         scratch_shapes=[
             pltpu.VMEM((BLOCKS, WIDTH // PIECE, PIECE, depth), jnp.bfloat16),
             pltpu.VMEM((3, PIECE, depth), jnp.bfloat16),
             pltpu.VMEM((TILES, PIECE, WIDTH), jnp.bfloat16),
+            pltpu.VMEM((2, 4, 2, EXTRA, depth), jnp.bfloat16),
+            pltpu.VMEM((BLOCKS, WIDTH, tasks), jnp.bfloat16),
+            pltpu.VMEM((ROWS, PIECE, tasks), jnp.float32),
+            pltpu.VMEM((ROWS, PIECE, 128), jnp.float32),
             pltpu.VMEM((8, WIDTH), jnp.float32),
             pltpu.SemaphoreType.DMA((BLOCKS,)),
             pltpu.SemaphoreType.DMA((3,)),
             pltpu.SemaphoreType.DMA((TILES,)),
+            pltpu.SemaphoreType.DMA,
         ],
         compiler_params=pltpu.CompilerParams(vmem_limit_bytes=VMEM_LIMIT),
         cost_estimate=pl.CostEstimate(
@@ -163,8 +207,6 @@
 
 def spread_kernel(ids, meta, weights, labels, keep, send, total, tile_buf, tile_sem):
     live = meta[0]
-    z = meta[3]
-    half = ROWS // 2
 
     def tile_copy(t):
         return pltpu.make_async_copy(
@@ -186,10 +228,7 @@
         return carry
 
     lax.fori_loop(0, live, tile, 0)
-    for piece in range(half):
-        place = lax.rem(z - piece + half, half)
-        keep[piece] = total[place]
-        send[piece] = total[half + place].astype(jnp.bfloat16)
+    split_rows(meta[3], total, keep, send)
 
 
 def spread_rows(ids, meta, weights, labels):
@@ -228,34 +267,34 @@
     y, xh, z, xl, core = [lax.axis_index(axis) for axis in AXES]
     depth = fingerprints.shape[1]
     slots = pattern.shape[1]
-    cols = lax.all_gather(fingerprints, ("y", "xh", "xl"), axis=0, tiled=True)
-    cols = cols.reshape(2, 4, 2, PIECE, depth)
-
-    squares = jnp.sum(jnp.square(fingerprints.astype(jnp.float32)), axis=1)
-    square_high = lax.reduce_precision(squares, 8, 7)
-    square_mid = lax.reduce_precision(squares - square_high, 8, 7)
-    square_low = squares - square_high - square_mid
-    table = jnp.concatenate([counts[:, None], pattern], axis=1).reshape(-1)
-    info = jnp.concatenate([
-        square_high, square_mid, square_low, table.astype(jnp.float32),
-        jnp.zeros((depth - 3 * PIECE - table.size,), jnp.float32),
-    ]).astype(jnp.bfloat16)
+    tasks = activity.shape[1]
+    seeded = activity.astype(jnp.float32) * label_mask.astype(jnp.float32)[:, None]
+    labels = seeded.astype(jnp.bfloat16).reshape(PIECE // EXTRA, EXTRA, tasks)
     extended = jnp.concatenate(
-        [fingerprints, info[None], jnp.zeros((15, depth), jnp.bfloat16)], axis=0
-    )
-    upward = [extended]
+        [fingerprints, labels.transpose(1, 0, 2).reshape(EXTRA, depth)], axis=0
+    )
+    cols = lax.all_gather(extended, ("y", "xh", "xl"), axis=0, tiled=True)
+    cols = cols.reshape(2, 4, 2, PIECE + EXTRA, depth)
+
+    upward = [fingerprints]
     for step in range(4):
         upward.append(lax.ppermute(upward[-1], "z", [(i, (i + 1) % 8) for i in range(8)]))
-    downward = [extended]
+    downward = [fingerprints]
     for step in range(3):
         downward.append(lax.ppermute(downward[-1], "z", [(i, (i + 7) % 8) for i in range(8)]))
     rows = upward + [downward[3], downward[2], downward[1]]
     rows = rows + [swap_cores(row) for row in rows]
-    line_info = jnp.stack([row[PIECE] for row in rows]).astype(jnp.float32)
-    row_sq = (
-        line_info[:, :PIECE] + line_info[:, PIECE:2 * PIECE] + line_info[:, 2 * PIECE:3 * PIECE]
-    )[:, :, None]
-    tables = line_info[:, 3 * PIECE:3 * PIECE + table.size].reshape(ROWS, 2, slots + 1)
+
+    squares = jnp.sum(jnp.square(fingerprints.astype(jnp.float32)), axis=1)
+    table = jnp.concatenate([counts[:, None], pattern], axis=1).astype(jnp.float32).reshape(-1)
+    info = jnp.concatenate([squares, table, jnp.zeros((PIECE - table.size,), jnp.float32)])
+    info = jnp.broadcast_to(info[None, None], (ROWS, 8, 2 * PIECE))
+    info = lax.all_to_all(info, ("core", "z"), 0, 0)[:, 0]
+    away = jnp.arange(8, dtype=jnp.int32)
+    nearby = (z - away) % 8
+    line_info = info[jnp.concatenate([core * 8 + nearby, (1 - core) * 8 + nearby])]
+    row_sq = line_info[:, :PIECE].reshape(ROWS, PIECE, 1)
+    tables = line_info[:, PIECE:PIECE + table.size].reshape(ROWS, 2, slots + 1)
     mine = lax.dynamic_index_in_dim(tables.astype(jnp.int32), y // 2, 1, keepdims=False)
 
     j = jnp.arange(BLOCKS, dtype=jnp.int32)
@@ -281,15 +320,10 @@
     own_offset = ((y % 2) * 2 + xh) * PIECE
     meta = jnp.stack([jnp.sum(flat), own_offset, own_tile, z]).astype(jnp.int32)
 
-    seeded = activity.astype(jnp.float32) * label_mask.astype(jnp.float32)[:, None]
-    labels = seeded.astype(jnp.bfloat16)
-    labels, cols = lax.optimization_barrier((labels, cols))
-    gathered = gather_labels(labels)
-    weights, degree = build_weights(ids, meta, starts, rows, cols, row_sq)
-
-    degree = jnp.sum(degree, axis=2)
-    places = (z - jnp.arange(8, dtype=jnp.int32)) % 8
-    degree_sum = degree[:8][places] + swap_cores(degree[8:][places])
+    weights, keep, send, degree_keep, degree_send = build_weights(
+        ids, meta, starts, rows, cols, row_sq
+    )
+    degree_sum = degree_keep + swap_cores(degree_send)
     high = lax.reduce_precision(degree_sum, 8, 7)
     low = degree_sum - high
     degree_rows = jnp.concatenate([high, low], axis=1).astype(jnp.bfloat16)[:, None, :]
@@ -298,7 +332,8 @@
     )
 
     for iteration in range(ITERS):
-        keep, send = spread_rows(ids, meta, weights, gathered)
+        if iteration > 0:
+            keep, send = spread_rows(ids, meta, weights, gathered)
         part = (keep + swap_cores(send).astype(jnp.float32)).astype(jnp.bfloat16)
         if iteration == 0:
             part = jnp.concatenate([part, degree_rows], axis=1)

time: 274 us -> 246 us (0.90)
  local copies, waits for them, and re-layouts: 32.8 us -> 6.72 us
  starting transfers between devices: 44 us -> 37.9 us
  waiting for transfers between devices: 46.6 us -> 52.2 us
  other arithmetic: 13.6 us -> 9.16 us
  blocking collectives: 101 us -> 104 us
    ppermute x4, waiting for transfers between devices: 41.5 us -> 20.2 us  [body(): lax.ppermute(upward[-1], 'z', [(i, (i + 1) % 8) for i in range(8)])]
    all_gather x1, waiting for transfers between devices: 0.01 us -> 19.4 us  [body(): cols = lax.all_gather(extended, ('y', 'xh', 'xl'), axis=0, tiled=True)]
    slice x16 -> x1, local copies, waits for them, and re-layouts: 16 us -> 0.01 us  [body(): info = lax.all_to_all(info, ('core', 'z'), 0, 0)[:, 0]]
    all_to_all x1, waiting for transfers between devices: 0.01 us -> 4.89 us  [body(): info = lax.all_to_all(info, ('core', 'z'), 0, 0)[:, 0]]
    all_to_all x3, blocking collectives: 62.7 us -> 67.5 us  [body(): parts = lax.all_to_all(part, 'z', 0, 0)]
    pallas_call x1, Pallas kernels: 11.2 us -> 15.8 us  [build_weights(): pl.pallas_call(weights_kernel, out_shape=(jax.ShapeDtypeStruct((TILES, PI...]
    ppermute x12, starting transfers between devices: 24.8 us -> 21.4 us  [swap_cores(): return lax.ppermute(value, 'core', [(0, 1), (1, 0)])]
    another operation x1 -> x0, local copies, waits for them, and re-layouts: 3.02 us -> none  [body(): line_info = jnp.stack([row[PIECE] for row in rows]).astype(jnp.float32)]
  transfers between devices with their start and end apart: 21 -> 21, of which waited for: 8 -> 10; matrix products, arithmetic and copies ran while one was open for 14% -> 2% of each run, Pallas kernels for 4% -> 0%
where the time goes in v3:
time: 246 us
  blocking collectives  104 us (42%)
  waiting for transfers between devices  52.2 us (21%)
  starting transfers between devices  37.9 us (15%)
  Pallas kernels  22.1 us (9%)
  between operations  13.7 us (6%)
  other arithmetic  9.16 us (4%)
  local copies, waits for them, and re-layouts  6.72 us (3%)
    all_to_all x3, blocking collectives, body(): parts = lax.all_to_all(part, 'z', 0, 0)  67.5 us
    all_to_all x2, blocking collectives, gather_labels(): lax.all_to_all(copies, PLANE, 0, 0).reshape(BLOCKS, WIDTH, labels.shape[1])  37 us
    ppermute x12, starting transfers between devices, swap_cores(): return lax.ppermute(value, 'core', [(0, 1), (1, 0)])  21.4 us
    ppermute x4, waiting for transfers between devices, body(): lax.ppermute(upward[-1], 'z', [(i, (i + 1) % 8) for i in range(8)])  20.2 us
    all_gather x1, waiting for transfers between devices, body(): cols = lax.all_gather(extended, ('y', 'xh', 'xl'), axis=0, tiled=True)  19.4 us
    pallas_call x1, Pallas kernels, build_weights(): pl.pallas_call(weights_kernel, out_shape=(jax.ShapeDtypeStruct((TILES, PI...  15.8 us
    ppermute x3, starting transfers between devices, body(): lax.ppermute(downward[-1], 'z', [(i, (i + 7) % 8) for i in range(8)])  8.05 us
    pallas_call x2, Pallas kernels, spread_rows(): pl.pallas_call(spread_kernel, out_shape=(jax.ShapeDtypeStruct((ROWS // 2,...  6.31 us
  transfers between devices with their start and end apart: 21, of which 10 were waited for; matrix products, arithmetic and copies ran while one was open for 2% of the time, Pallas kernels for 0%

profile of v3, /device:TPU:1, one launch (start us, length us, event | category | flops | bytes accessed | tf_op | source)
XLA Modules:
  0.0 246.2 jit_solution(1331688997416161911)
XLA Ops:
  10.1 2.5 %collective-permute-start = (bf16[128,2048]{1,0:T(8,128)(2,1)S(1)}, bf16[128,2048]{1,0:T(8,128)(2,1)S(1)}, u32[]{:S(2)}, u32[]{:S(2)}) collective-permute-start(bf16[128,2048]{1,0:T(8,128)(2,1)S(1)} %copy-done), channel_id=1, source_target_pairs={{0,4},{4,8},{8,12},{12,16},{16,20},{20,24},{24,28},{28,0},{1,5},{5... | collective-permute-start | bytes 1572872 | tf_op jit(solution)/shard_map/ppermute | solution.py:281
  12.7 4.0 %collective-permute-start.4 = (bf16[128,2048]{1,0:T(8,128)(2,1)S(1)}, bf16[128,2048]{1,0:T(8,128)(2,1)S(1)}, u32[]{:S(2)}, u32[]{:S(2)}) collective-permute-start(bf16[128,2048]{1,0:T(8,128)(2,1)S(1)} %copy-done), channel_id=1, source_target_pairs={{0,28},{4,0},{8,4},{12,8},{16,12},{20,16},{24,20},{28,24},{1,29},{... | collective-permute-start | bytes 1572872 | tf_op jit(solution)/shard_map/ppermute | solution.py:284
  18.9 5.9 %all-to-all-start = ((f32[16,8,256]{2,1,0:T(8,128)}), f32[16,8,256]{2,1,0:T(8,128)S(1)}, u32[]{:S(2)}, u32[]{:S(2)}) async-start(f32[16,8,256]{2,1,0:T(8,128)} %broadcast_in_dim.42), calls=%async_computation | async-start | bytes 262144 | tf_op jit(solution)/shard_map/all_to_all | solution.py:292
  24.8 3.5 %collective-permute-done.refs_4_ = bf16[128,2048]{1,0:T(8,128)(2,1)S(1)} collective-permute-done((bf16[128,2048]{1,0:T(8,128)(2,1)S(1)}, bf16[128,2048]{1,0:T(8,128)(2,1)S(1)}, u32[]{:S(2)}, u32[]{:S(2)}) %collective-permute-start) | collective-permute-done | bytes 524320 | tf_op jit(solution)/shard_map/ppermute | solution.py:281
  28.4 4.9 %all-to-all-done = f32[16,8,256]{2,1,0:T(8,128)S(1)} async-done(((f32[16,8,256]{2,1,0:T(8,128)}), f32[16,8,256]{2,1,0:T(8,128)S(1)}, u32[]{:S(2)}, u32[]{:S(2)}) %all-to-all-start) | async-done | bytes 131104 | tf_op jit(solution)/shard_map/all_to_all | solution.py:292
  35.6 6.8 %collective-permute-done.1.refs_5_ = bf16[128,2048]{1,0:T(8,128)(2,1)S(1)} collective-permute-done((bf16[128,2048]{1,0:T(8,128)(2,1)S(1)}, bf16[128,2048]{1,0:T(8,128)(2,1)S(1)}, u32[]{:S(2)}, u32[]{:S(2)}) %collective-permute-start.1) | collective-permute-done | bytes 524320 | tf_op jit(solution)/shard_map/ppermute | solution.py:281
  44.6 3.2 %collective-permute-done.5.refs_9_ = bf16[128,2048]{1,0:T(8,128)(2,1)S(1)} collective-permute-done((bf16[128,2048]{1,0:T(8,128)(2,1)S(1)}, bf16[128,2048]{1,0:T(8,128)(2,1)S(1)}, u32[]{:S(2)}, u32[]{:S(2)}) %collective-permute-start.5) | collective-permute-done | bytes 524320 | tf_op jit(solution)/shard_map/ppermute | solution.py:284
  47.9 2.4 collective-permute-start.6
  50.3 5.0 %collective-permute-done.2.refs_6_ = bf16[128,2048]{1,0:T(8,128)(2,1)} collective-permute-done((bf16[128,2048]{1,0:T(8,128)(2,1)S(1)}, bf16[128,2048]{1,0:T(8,128)(2,1)}, u32[]{:S(2)}, u32[]{:S(2)}) %collective-permute-start.2) | collective-permute-done | bytes 524320 | tf_op jit(solution)/shard_map/ppermute | solution.py:281
  57.8 2.9 %collective-permute-start.13 = (bf16[128,2048]{1,0:T(8,128)(2,1)S(1)}, bf16[128,2048]{1,0:T(8,128)(2,1)S(1)}, u32[]{:S(2)}, u32[]{:S(2)}) collective-permute-start(bf16[128,2048]{1,0:T(8,128)(2,1)S(1)} %collective-permute-done.5.refs_9_), channel_id=1, source_target_pairs={{0,1},{1,0},{2,3},{3,2},{4,5},{5,4},{6,7},{7,6},{8,9},{9,8},{10,11... | collective-permute-start | bytes 1572872 | tf_op jit(solution)/shard_map/ppermute | solution.py:258
  62.4 5.0 %collective-permute-done.3.refs_7_ = bf16[128,2048]{1,0:T(8,128)(2,1)} collective-permute-done((bf16[128,2048]{1,0:T(8,128)(2,1)}, bf16[128,2048]{1,0:T(8,128)(2,1)}, u32[]{:S(2)}, u32[]{:S(2)}) %collective-permute-start.3) | collective-permute-done | bytes 524320 | tf_op jit(solution)/shard_map/ppermute | solution.py:281
  67.4 3.7 %collective-permute-start.11 = (bf16[128,2048]{1,0:T(8,128)(2,1)}, bf16[128,2048]{1,0:T(8,128)(2,1)}, u32[]{:S(2)}, u32[]{:S(2)}) collective-permute-start(bf16[128,2048]{1,0:T(8,128)(2,1)} %collective-permute-done.3.refs_7_), channel_id=1, source_target_pairs={{0,1},{1,0},{2,3},{3,2},{4,5},{5,4},{6,7},{7,6},{8,9},{9,8},{10,11... | collective-permute-start | bytes 1572872 | tf_op jit(solution)/shard_map/ppermute | solution.py:258
  75.4 19.4 %all-gather.2.cloned.1.call-done = bf16[2304,2048]{1,0:T(8,128)(2,1)} async-done(((bf16[144,2048]{1,0:T(8,128)(2,1)}), bf16[2304,2048]{1,0:T(8,128)(2,1)}) %all-gather.2.cloned.1.call-update) | async-done | bytes 9437200 | tf_op jit(solution)/shard_map/all_gather | solution.py:276
  94.8 15.8 %weights.1 = (bf16[64,128,512]{2,1,0:T(8,128)(2,1)}, f32[8,128,256]{2,1,0:T(8,128)}, bf16[8,128,256]{2,1,0:T(8,128)(2,1)S(1)}, f32[8,128]{1,0:T(8,128)S(1)}, f32[8,128]{1,0:T(8,128)S(1)}) custom-call(s32[64]{0:T(128)S(1)} %select_reduce_fusion.refs_0_.ids, s32[4]{0:T(128)S(1)} %pad_add_fusion.refs_1_.meta, s32[8]{0:T(128)S(1)} %select_reduce_fusion.2.refs_2_, ...), custom_call_target="tpu_custom_call" | custom-call | flops 4294967296 | bytes 16777216 | tf_op jit(solution)/shard_map/weights/pallas_call | solution.py:173
  110.6 3.0 %collective-permute-start.15 = (bf16[8,128,256]{2,1,0:T(8,128)(2,1)S(1)}, bf16[8,128,256]{2,1,0:T(8,128)(2,1)S(1)}, u32[]{:S(2)}, u32[]{:S(2)}) collective-permute-start(bf16[8,128,256]{2,1,0:T(8,128)(2,1)S(1)} %get-tuple-element.16), channel_id=1, source_target_pairs={{0,1},{1,0},{2,3},{3,2},{4,5},{5,4},{6,7},{7,6},{8,9},{9,8},{10,11... | collective-permute-start | bytes 1572872 | tf_op jit(solution)/shard_map/ppermute | solution.py:258
  116.7 27.4 %all_to_all.30 = bf16[8,144,256]{2,1,0:T(8,128)(2,1)S(1)} all-to-all(bf16[8,144,256]{2,1,0:T(8,128)(2,1)S(1)} %maximum_maximum_fusion), channel_id=1, replica_groups=mesh['y'=4,'xh'=2,'z'=8,'xl'=2,'core'=2] {'z'}, dimensions={0} | all-to-all | bytes 1179648 | tf_op jit(solution)/shard_map/all_to_all | solution.py:340
  144.4 18.3 %all_to_all.31 = bf16[16,128,256]{2,1,0:T(8,128)(2,1)S(1)} all-to-all(bf16[16,128,256]{2,1,0:T(8,128)(2,1)S(1)} %broadcast_in_dim.48), channel_id=1, replica_groups=mesh['y'=4,'xh'=2,'z'=8,'xl'=2,'core'=2] {'xl','y','xh'}, dimensions={0} | all-to-all | bytes 2097152 | tf_op jit(solution)/shard_map/all_to_all | solution.py:263
  162.7 3.2 %spread.2 = (f32[8,128,256]{2,1,0:T(8,128)S(1)}, bf16[8,128,256]{2,1,0:T(8,128)(2,1)S(1)}) custom-call(s32[64]{0:T(128)S(1)} %select_reduce_fusion.refs_0_.ids, s32[4]{0:T(128)S(1)} %pad_add_fusion.refs_1_.meta, bf16[64,128,512]{2,1,0:T(8,128)(2,1)} %get-tuple-element.14.weights, bf16[4,512,256]{2,1,0:T(8,128)(2,1)S(1)} %bitcast.34), custom_call_target="tpu_custom_call" | custom-call | tf_op jit(solution)/shard_map/spread/pallas_call | solution.py:239
  165.9 3.9 %collective-permute-start.17 = (bf16[8,128,256]{2,1,0:T(8,128)(2,1)S(1)}, bf16[8,128,256]{2,1,0:T(8,128)(2,1)S(1)}, u32[]{:S(2)}, u32[]{:S(2)}) collective-permute-start(bf16[8,128,256]{2,1,0:T(8,128)(2,1)S(1)} %get-tuple-element.20), channel_id=1, source_target_pairs={{0,1},{1,0},{2,3},{3,2},{4,5},{5,4},{6,7},{7,6},{8,9},{9,8},{10,11... | collective-permute-start | bytes 1572872 | tf_op jit(solution)/shard_map/ppermute | solution.py:258
  171.4 19.8 %all_to_all.32 = bf16[8,128,256]{2,1,0:T(8,128)(2,1)S(1)} all-to-all(bf16[8,128,256]{2,1,0:T(8,128)(2,1)S(1)} %add_convert_fusion.1), channel_id=1, replica_groups=mesh['y'=4,'xh'=2,'z'=8,'xl'=2,'core'=2] {'z'}, dimensions={0} | all-to-all | bytes 1048576 | tf_op jit(solution)/shard_map/all_to_all | solution.py:340
  191.5 18.7 %all_to_all.33 = bf16[16,128,256]{2,1,0:T(8,128)(2,1)S(1)} all-to-all(bf16[16,128,256]{2,1,0:T(8,128)(2,1)S(1)} %broadcast_in_dim.49), channel_id=1, replica_groups=mesh['y'=4,'xh'=2,'z'=8,'xl'=2,'core'=2] {'xl','y','xh'}, dimensions={0} | all-to-all | bytes 2097152 | tf_op jit(solution)/shard_map/all_to_all | solution.py:263
  210.2 3.2 %spread.3 = (f32[8,128,256]{2,1,0:T(8,128)S(1)}, bf16[8,128,256]{2,1,0:T(8,128)(2,1)S(1)}) custom-call(s32[64]{0:T(128)S(1)} %select_reduce_fusion.refs_0_.ids, s32[4]{0:T(128)S(1)} %pad_add_fusion.refs_1_.meta, bf16[64,128,512]{2,1,0:T(8,128)(2,1)} %get-tuple-element.14.weights, bf16[4,512,256]{2,1,0:T(8,128)(2,1)S(1)} %bitcast.33), custom_call_target="tpu_custom_call" | custom-call | tf_op jit(solution)/shard_map/spread/pallas_call | solution.py:239
  213.3 3.1 %collective-permute-start.18 = (bf16[8,128,256]{2,1,0:T(8,128)(2,1)S(1)}, bf16[8,128,256]{2,1,0:T(8,128)(2,1)S(1)}, u32[]{:S(2)}, u32[]{:S(2)}) collective-permute-start(bf16[8,128,256]{2,1,0:T(8,128)(2,1)S(1)} %get-tuple-element.22), channel_id=1, source_target_pairs={{0,1},{1,0},{2,3},{3,2},{4,5},{5,4},{6,7},{7,6},{8,9},{9,8},{10,11... | collective-permute-start | bytes 1572872 | tf_op jit(solution)/shard_map/ppermute | solution.py:258
  218.2 20.4 %all_to_all.34 = bf16[8,128,256]{2,1,0:T(8,128)(2,1)S(1)} all-to-all(bf16[8,128,256]{2,1,0:T(8,128)(2,1)S(1)} %add_convert_fusion), channel_id=1, replica_groups=mesh['y'=4,'xh'=2,'z'=8,'xl'=2,'core'=2] {'z'}, dimensions={0} | all-to-all | bytes 1048576 | tf_op jit(solution)/shard_map/all_to_all | solution.py:340
  (99 shorter events, 26.8 us)
Async XLA Ops:
  6.5 11.1 %copy-start.7 = (s32[2]{0:T(128)S(1)}, s32[2]{0:T(128)}, u32[]{:S(2)}) copy-start(s32[2]{0:T(128)} %param.9) | copy-start | bytes 28
  6.5 11.2 %copy-start.6 = (s32[2,24]{1,0:T(2,128)S(1)}, s32[2,24]{1,0:T(2,128)}, u32[]{:S(2)}) copy-start(s32[2,24]{1,0:T(2,128)} %param.8) | copy-start | bytes 580
  6.5 88.3 %all-gather.2.cloned.1.call-start = ((), (), s32[]{:S(2)}) async-start(), calls=%async_computation.6 | async-start | bytes 10027008 | tf_op jit(solution)/shard_map/all_gather | solution.py:276
  10.1 18.1 %collective-permute-start = (bf16[128,2048]{1,0:T(8,128)(2,1)S(1)}, bf16[128,2048]{1,0:T(8,128)(2,1)S(1)}, u32[]{:S(2)}, u32[]{:S(2)}) collective-permute-start(bf16[128,2048]{1,0:T(8,128)(2,1)S(1)} %copy-done), channel_id=1, source_target_pairs={{0,4},{4,8},{8,12},{12,16},{16,20},{20,24},{24,28},{28,0},{1,5},{5... | collective-permute-start | bytes 1572872 | tf_op jit(solution)/shard_map/ppermute | solution.py:281
  12.7 21.3 %collective-permute-start.4 = (bf16[128,2048]{1,0:T(8,128)(2,1)S(1)}, bf16[128,2048]{1,0:T(8,128)(2,1)S(1)}, u32[]{:S(2)}, u32[]{:S(2)}) collective-permute-start(bf16[128,2048]{1,0:T(8,128)(2,1)S(1)} %copy-done), channel_id=1, source_target_pairs={{0,28},{4,0},{8,4},{12,8},{16,12},{20,16},{24,20},{28,24},{1,29},{... | collective-permute-start | bytes 1572872 | tf_op jit(solution)/shard_map/ppermute | solution.py:284
  16.7 41.0 %collective-permute-start.7 = (bf16[128,2048]{1,0:T(8,128)(2,1)S(1)}, bf16[128,2048]{1,0:T(8,128)(2,1)S(1)}, u32[]{:S(2)}, u32[]{:S(2)}) collective-permute-start(bf16[128,2048]{1,0:T(8,128)(2,1)S(1)} %copy-done), channel_id=1, source_target_pairs={{0,1},{1,0},{2,3},{3,2},{4,5},{5,4},{6,7},{7,6},{8,9},{9,8},{10,11... | collective-permute-start | bytes 1572872 | tf_op jit(solution)/shard_map/ppermute | solution.py:258
  18.9 14.4 %all-to-all-start = ((f32[16,8,256]{2,1,0:T(8,128)}), f32[16,8,256]{2,1,0:T(8,128)S(1)}, u32[]{:S(2)}, u32[]{:S(2)}) async-start(f32[16,8,256]{2,1,0:T(8,128)} %broadcast_in_dim.42), calls=%async_computation | async-start | bytes 262144 | tf_op jit(solution)/shard_map/all_to_all | solution.py:292
  28.3 14.1 %collective-permute-start.1 = (bf16[128,2048]{1,0:T(8,128)(2,1)S(1)}, bf16[128,2048]{1,0:T(8,128)(2,1)S(1)}, u32[]{:S(2)}, u32[]{:S(2)}) collective-permute-start(bf16[128,2048]{1,0:T(8,128)(2,1)S(1)} %collective-permute-done.refs_4_), channel_id=1, source_target_pairs={{0,4},{4,8},{8,12},{12,16},{16,20},{20,24},{24,28},{28,0},{1,5},{5... | collective-permute-start | bytes 1572872 | tf_op jit(solution)/shard_map/ppermute | solution.py:281
  34.0 13.9 %collective-permute-start.5 = (bf16[128,2048]{1,0:T(8,128)(2,1)S(1)}, bf16[128,2048]{1,0:T(8,128)(2,1)S(1)}, u32[]{:S(2)}, u32[]{:S(2)}) collective-permute-start(bf16[128,2048]{1,0:T(8,128)(2,1)S(1)} %collective-permute-done.4.refs_10_), channel_id=1, source_target_pairs={{0,28},{4,0},{8,4},{12,8},{16,12},{20,16},{24,20},{28,24},{1,29},{... | collective-permute-start | bytes 1572872 | tf_op jit(solution)/shard_map/ppermute | solution.py:284
  42.4 12.9 %collective-permute-start.2 = (bf16[128,2048]{1,0:T(8,128)(2,1)S(1)}, bf16[128,2048]{1,0:T(8,128)(2,1)}, u32[]{:S(2)}, u32[]{:S(2)}) collective-permute-start(bf16[128,2048]{1,0:T(8,128)(2,1)S(1)} %collective-permute-done.1.refs_5_), channel_id=1, source_target_pairs={{0,4},{4,8},{8,12},{12,16},{16,20},{20,24},{24,28},{28,0},{1,5},{5... | collective-permute-start | bytes 1572872 | tf_op jit(solution)/shard_map/ppermute | solution.py:281
  42.6 18.0 %collective-permute-start.14 = (bf16[128,2048]{1,0:T(8,128)(2,1)S(1)}, bf16[128,2048]{1,0:T(8,128)(2,1)}, u32[]{:S(2)}, u32[]{:S(2)}) collective-permute-start(bf16[128,2048]{1,0:T(8,128)(2,1)S(1)} %collective-permute-done.4.refs_10_), channel_id=1, source_target_pairs={{0,1},{1,0},{2,3},{3,2},{4,5},{5,4},{6,7},{7,6},{8,9},{9,8},{10,11... | collective-permute-start | bytes 1572872 | tf_op jit(solution)/shard_map/ppermute | solution.py:258
  44.5 16.2 %collective-permute-start.8 = (bf16[128,2048]{1,0:T(8,128)(2,1)S(1)}, bf16[128,2048]{1,0:T(8,128)(2,1)}, u32[]{:S(2)}, u32[]{:S(2)}) collective-permute-start(bf16[128,2048]{1,0:T(8,128)(2,1)S(1)} %collective-permute-done.refs_4_), channel_id=1, source_target_pairs={{0,1},{1,0},{2,3},{3,2},{4,5},{5,4},{6,7},{7,6},{8,9},{9,8},{10,11... | collective-permute-start | bytes 1572872 | tf_op jit(solution)/shard_map/ppermute | solution.py:258
  47.9 13.3 %collective-permute-start.6 = (bf16[128,2048]{1,0:T(8,128)(2,1)S(1)}, bf16[128,2048]{1,0:T(8,128)(2,1)}, u32[]{:S(2)}, u32[]{:S(2)}) collective-permute-start(bf16[128,2048]{1,0:T(8,128)(2,1)S(1)} %collective-permute-done.5.refs_9_), channel_id=1, source_target_pairs={{0,28},{4,0},{8,4},{12,8},{16,12},{20,16},{24,20},{28,24},{1,29},{... | collective-permute-start | bytes 1572872 | tf_op jit(solution)/shard_map/ppermute | solution.py:284
  55.2 12.1 %collective-permute-start.3 = (bf16[128,2048]{1,0:T(8,128)(2,1)}, bf16[128,2048]{1,0:T(8,128)(2,1)}, u32[]{:S(2)}, u32[]{:S(2)}) collective-permute-start(bf16[128,2048]{1,0:T(8,128)(2,1)} %collective-permute-done.2.refs_6_), channel_id=1, source_target_pairs={{0,4},{4,8},{8,12},{12,16},{16,20},{20,24},{24,28},{28,0},{1,5},{5... | collective-permute-start | bytes 1572872 | tf_op jit(solution)/shard_map/ppermute | solution.py:281
  57.8 14.4 %collective-permute-start.13 = (bf16[128,2048]{1,0:T(8,128)(2,1)S(1)}, bf16[128,2048]{1,0:T(8,128)(2,1)S(1)}, u32[]{:S(2)}, u32[]{:S(2)}) collective-permute-start(bf16[128,2048]{1,0:T(8,128)(2,1)S(1)} %collective-permute-done.5.refs_9_), channel_id=1, source_target_pairs={{0,1},{1,0},{2,3},{3,2},{4,5},{5,4},{6,7},{7,6},{8,9},{9,8},{10,11... | collective-permute-start | bytes 1572872 | tf_op jit(solution)/shard_map/ppermute | solution.py:258
  60.7 11.5 %collective-permute-start.9 = (bf16[128,2048]{1,0:T(8,128)(2,1)S(1)}, bf16[128,2048]{1,0:T(8,128)(2,1)S(1)}, u32[]{:S(2)}, u32[]{:S(2)}) collective-permute-start(bf16[128,2048]{1,0:T(8,128)(2,1)S(1)} %collective-permute-done.1.refs_5_), channel_id=1, source_target_pairs={{0,1},{1,0},{2,3},{3,2},{4,5},{5,4},{6,7},{7,6},{8,9},{9,8},{10,11... | collective-permute-start | bytes 1572872 | tf_op jit(solution)/shard_map/ppermute | solution.py:258
  60.8 12.3 %collective-permute-start.10 = (bf16[128,2048]{1,0:T(8,128)(2,1)}, bf16[128,2048]{1,0:T(8,128)(2,1)S(1)}, u32[]{:S(2)}, u32[]{:S(2)}) collective-permute-start(bf16[128,2048]{1,0:T(8,128)(2,1)} %collective-permute-done.2.refs_6_), channel_id=1, source_target_pairs={{0,1},{1,0},{2,3},{3,2},{4,5},{5,4},{6,7},{7,6},{8,9},{9,8},{10,11... | collective-permute-start | bytes 1572872 | tf_op jit(solution)/shard_map/ppermute | solution.py:258
  61.2 12.7 %collective-permute-start.12 = (bf16[128,2048]{1,0:T(8,128)(2,1)}, bf16[128,2048]{1,0:T(8,128)(2,1)S(1)}, u32[]{:S(2)}, u32[]{:S(2)}) collective-permute-start(bf16[128,2048]{1,0:T(8,128)(2,1)} %collective-permute-done.6.refs_8_), channel_id=1, source_target_pairs={{0,1},{1,0},{2,3},{3,2},{4,5},{5,4},{6,7},{7,6},{8,9},{9,8},{10,11... | collective-permute-start | bytes 1572872 | tf_op jit(solution)/shard_map/ppermute | solution.py:258
  67.4 8.1 %collective-permute-start.11 = (bf16[128,2048]{1,0:T(8,128)(2,1)}, bf16[128,2048]{1,0:T(8,128)(2,1)}, u32[]{:S(2)}, u32[]{:S(2)}) collective-permute-start(bf16[128,2048]{1,0:T(8,128)(2,1)} %collective-permute-done.3.refs_7_), channel_id=1, source_target_pairs={{0,1},{1,0},{2,3},{3,2},{4,5},{5,4},{6,7},{7,6},{8,9},{9,8},{10,11... | collective-permute-start | bytes 1572872 | tf_op jit(solution)/shard_map/ppermute | solution.py:258
  110.6 4.5 %collective-permute-start.15 = (bf16[8,128,256]{2,1,0:T(8,128)(2,1)S(1)}, bf16[8,128,256]{2,1,0:T(8,128)(2,1)S(1)}, u32[]{:S(2)}, u32[]{:S(2)}) collective-permute-start(bf16[8,128,256]{2,1,0:T(8,128)(2,1)S(1)} %get-tuple-element.16), channel_id=1, source_target_pairs={{0,1},{1,0},{2,3},{3,2},{4,5},{5,4},{6,7},{7,6},{8,9},{9,8},{10,11... | collective-permute-start | bytes 1572872 | tf_op jit(solution)/shard_map/ppermute | solution.py:258
  113.6 1.5 collective-permute-start.16
  116.7 27.5 %copy-start.1 = (bf16[128,256]{1,0:T(8,128)(2,1)S(1)}, bf16[128,256]{1,0:T(8,128)(2,1)}, u32[]{:S(2)}) copy-start(bf16[128,256]{1,0:T(8,128)(2,1)} %param.6) | copy-start | bytes 196612
  165.9 5.4 %collective-permute-start.17 = (bf16[8,128,256]{2,1,0:T(8,128)(2,1)S(1)}, bf16[8,128,256]{2,1,0:T(8,128)(2,1)S(1)}, u32[]{:S(2)}, u32[]{:S(2)}) collective-permute-start(bf16[8,128,256]{2,1,0:T(8,128)(2,1)S(1)} %get-tuple-element.20), channel_id=1, source_target_pairs={{0,1},{1,0},{2,3},{3,2},{4,5},{5,4},{6,7},{7,6},{8,9},{9,8},{10,11... | collective-permute-start | bytes 1572872 | tf_op jit(solution)/shard_map/ppermute | solution.py:258
  213.3 4.7 %collective-permute-start.18 = (bf16[8,128,256]{2,1,0:T(8,128)(2,1)S(1)}, bf16[8,128,256]{2,1,0:T(8,128)(2,1)S(1)}, u32[]{:S(2)}, u32[]{:S(2)}) collective-permute-start(bf16[8,128,256]{2,1,0:T(8,128)(2,1)S(1)} %get-tuple-element.22), channel_id=1, source_target_pairs={{0,1},{1,0},{2,3},{3,2},{4,5},{5,4},{6,7},{7,6},{8,9},{9,8},{10,11... | collective-permute-start | bytes 1572872 | tf_op jit(solution)/shard_map/ppermute | solution.py:258
  (5 other events, 6.9 us)
Sparse Core Ops, SparseCore 0:
  10.3 84.5 all-gather.1

commit v4 on v3

v4 whole, which is shorter than its diff:
```python
import jax
import jax.numpy as jnp
from jax import lax
from jax.experimental import pallas as pl
from jax.experimental.pallas import tpu as pltpu
from jax.sharding import Mesh, PartitionSpec as P

ITERS = 3

WEIGHT_ROW = 0.6
WEIGHT_COL = 0.3
WEIGHT_SHARED = 0.1
SHARPNESS = 80.0
EPSILON = 1e-05
PROPAGATE = 0.8
ANCHOR = 0.2

AXES = ("y", "xh", "z", "xl", "core")
SIZES = (4, 2, 8, 2, 2)
PLANE = ("xl", "y", "xh")
PIECE = 128
EXTRA = 16
ROWS = 16
BLOCKS = 4
WIDTH = 512
TILES = ROWS * BLOCKS
VMEM_LIMIT = 48 * 1024 * 1024


def split_rows(z, total, keep, send):
    half = ROWS // 2
    for piece in range(half):
        place = lax.rem(z - piece + half, half)
        keep[piece] = total[place]
        send[piece] = total[half + place].astype(jnp.bfloat16)


def weights_kernel(pairs, meta, starts, rows, cols, row_sq, col_sq,
                   weights, keep, send, degree_keep, degree_send,
                   col_buf, row_buf, tile_buf, label_raw, labels, total, degree,
                   col_sem, row_sem, tile_sem, label_sem):
    live = starts[BLOCKS]
    own_offset = meta[1]
    own_tile = meta[2]
    z = meta[3]

    def row_copy(q, side):
        slot = lax.rem(q, 3)
        return pltpu.make_async_copy(
            rows.at[lax.rem(pairs[2 * q + side], ROWS)],
            row_buf.at[slot, pl.ds(side * PIECE, PIECE)],
            row_sem.at[slot, side],
        )

    def col_copy(j):
        return pltpu.make_async_copy(
            cols.at[j % 2, :, j // 2, pl.ds(0, PIECE)], col_buf.at[j], col_sem.at[j]
        )

    def tile_copy(tile_id):
        return pltpu.make_async_copy(
            tile_buf.at[tile_id], weights.at[tile_id], tile_sem.at[tile_id]
        )

    col_copy(0).start()
    for first in range(2):
        @pl.when(first < live)
        def _():
            row_copy(first, 0).start()
            row_copy(first, 1).start()
    label_copy = pltpu.make_async_copy(
        cols.at[:, :, :, pl.ds(PIECE, EXTRA)], label_raw, label_sem
    )
    label_copy.start()
    for j in range(1, BLOCKS):
        col_copy(j).start()
    degree[...] = jnp.zeros_like(degree)
    total[...] = jnp.zeros_like(total)
    label_copy.wait()
    for j in range(BLOCKS):
        for sub in range(WIDTH // PIECE):
            for group in range(labels.shape[1] // EXTRA):
                labels[
                    j, group * EXTRA:(group + 1) * EXTRA, sub * PIECE:(sub + 1) * PIECE
                ] = label_raw[j % 2, sub, j // 2, :, group * PIECE:(group + 1) * PIECE]
    lane = lax.broadcasted_iota(jnp.int32, (WIDTH, 2 * PIECE), 1)
    gap = jnp.where(
        lane < PIECE, lax.broadcasted_iota(jnp.int32, (WIDTH, 2 * PIECE), 0) - lane, -WIDTH
    )
    depth = col_buf.shape[-1]

    def block(j, carry):
        pltpu.make_async_copy(
            cols.at[0, :, 0, pl.ds(0, PIECE)], col_buf.at[j], col_sem.at[j]
        ).wait()

        def pair(q, inner_carry):
            @pl.when(q + 2 < live)
            def _():
                row_copy(q + 2, 0).start()
                row_copy(q + 2, 1).start()

            row_copy(q, 0).wait()
            row_copy(q, 1).wait()
            one = pairs[2 * q]
            two = pairs[2 * q + 1]
            place_one = lax.rem(one, ROWS)
            place_two = lax.rem(two, ROWS)
            inner = lax.dot_general(
                col_buf[j].reshape(WIDTH, depth), row_buf[lax.rem(q, 3)],
                (((1,), (1,)), ((), ())),
                preferred_element_type=jnp.float32,
            )
            row_part = jnp.concatenate([row_sq[place_one], row_sq[place_two]], axis=1)
            ratio = inner / (
                WEIGHT_ROW * row_part
                + WEIGHT_COL * col_sq[j]
                + WEIGHT_SHARED * inner
                + EPSILON
            )
            offset = jnp.where(one == own_tile, own_offset, -2 * WIDTH)
            value = jnp.where(gap == offset, 0.0, jnp.exp(SHARPNESS * (ratio - 0.5)))
            half = value.astype(jnp.bfloat16)
            spread = jnp.dot(labels[j], half, preferred_element_type=jnp.float32)
            sums = jnp.sum(value, axis=0, keepdims=True)
            tile_buf[one] = half[:, :PIECE]
            tile_copy(one).start()
            total[place_one] += spread[:, :PIECE]
            degree[pl.ds(place_one, 1), :] += sums[:, :PIECE]

            @pl.when(one != two)
            def _():
                tile_buf[two] = half[:, PIECE:]
                tile_copy(two).start()
                total[place_two] += spread[:, PIECE:]
                degree[pl.ds(place_two, 1), :] += sums[:, PIECE:]

            return inner_carry

        return lax.fori_loop(starts[j], starts[j + 1], pair, carry)

    lax.fori_loop(0, BLOCKS, block, 0)
    split_rows(z, total, keep, send)
    half_rows = ROWS // 2
    for piece in range(half_rows):
        place = lax.rem(z - piece + half_rows, half_rows)
        degree_keep[piece:piece + 1, :] = degree[pl.ds(place, 1), :]
        degree_send[piece:piece + 1, :] = degree[pl.ds(half_rows + place, 1), :]

    def finish(q, carry):
        tile_copy(pairs[2 * q]).wait()

        @pl.when(pairs[2 * q] != pairs[2 * q + 1])
        def _():
            tile_copy(pairs[2 * q + 1]).wait()

        return carry

    lax.fori_loop(0, live, finish, 0)


def build_weights(pairs, meta, starts, rows, cols, row_sq, col_sq):
    smem = pl.BlockSpec(memory_space=pltpu.SMEM)
    vmem = pl.BlockSpec(memory_space=pltpu.VMEM)
    hbm = pl.BlockSpec(memory_space=pl.ANY)
    depth = cols.shape[-1]
    tasks = depth * EXTRA // PIECE
    return pl.pallas_call(
        weights_kernel,
        out_shape=(
            jax.ShapeDtypeStruct((TILES, WIDTH, PIECE), jnp.bfloat16),
            jax.ShapeDtypeStruct((ROWS // 2, tasks, PIECE), jnp.float32),
            jax.ShapeDtypeStruct((ROWS // 2, tasks, PIECE), jnp.bfloat16),
            jax.ShapeDtypeStruct((ROWS // 2, PIECE), jnp.float32),
            jax.ShapeDtypeStruct((ROWS // 2, PIECE), jnp.float32),
        ),
        in_specs=[smem, smem, smem, hbm, hbm, vmem, vmem],
        out_specs=(hbm, vmem, vmem, vmem, vmem),
        scratch_shapes=[
            pltpu.VMEM((BLOCKS, WIDTH // PIECE, PIECE, depth), jnp.bfloat16),
            pltpu.VMEM((3, 2 * PIECE, depth), jnp.bfloat16),
            pltpu.VMEM((TILES, WIDTH, PIECE), jnp.bfloat16),
            pltpu.VMEM((2, 4, 2, EXTRA, depth), jnp.bfloat16),
            pltpu.VMEM((BLOCKS, tasks, WIDTH), jnp.bfloat16),
            pltpu.VMEM((ROWS, tasks, PIECE), jnp.float32),
            pltpu.VMEM((ROWS, PIECE), jnp.float32),
            pltpu.SemaphoreType.DMA((BLOCKS,)),
            pltpu.SemaphoreType.DMA((3, 2)),
            pltpu.SemaphoreType.DMA((TILES,)),
            pltpu.SemaphoreType.DMA,
        ],
        compiler_params=pltpu.CompilerParams(vmem_limit_bytes=VMEM_LIMIT),
        cost_estimate=pl.CostEstimate(
            flops=16 * 2 * PIECE * WIDTH * depth,
            bytes_accessed=2 * (ROWS + 16) * PIECE * depth,
            transcendentals=16 * PIECE * WIDTH,
        ),
        name="weights",
    )(pairs, meta, starts, rows, cols, row_sq, col_sq)


def spread_kernel(ids, meta, weights, pieces, keep, send, labels, total, tile_buf, tile_sem):
    live = meta[0]

    def tile_copy(t):
        return pltpu.make_async_copy(
            weights.at[ids[t]], tile_buf.at[ids[t]], tile_sem.at[ids[t]]
        )

    def begin(t, carry):
        tile_copy(t).start()
        return carry

    lax.fori_loop(0, live, begin, 0)
    total[...] = jnp.zeros_like(total)
    for j in range(BLOCKS):
        for sub in range(WIDTH // PIECE):
            labels[j, :, sub * PIECE:(sub + 1) * PIECE] = pieces[j * (WIDTH // PIECE) + sub]

    def tile(t, carry):
        tile_copy(t).wait()
        total[lax.rem(ids[t], ROWS)] += jnp.dot(
            labels[ids[t] // ROWS], tile_buf[ids[t]], preferred_element_type=jnp.float32
        )
        return carry

    lax.fori_loop(0, live, tile, 0)
    split_rows(meta[3], total, keep, send)


def spread_rows(ids, meta, weights, pieces):
    smem = pl.BlockSpec(memory_space=pltpu.SMEM)
    vmem = pl.BlockSpec(memory_space=pltpu.VMEM)
    hbm = pl.BlockSpec(memory_space=pl.ANY)
    tasks = pieces.shape[1]
    return pl.pallas_call(
        spread_kernel,
        out_shape=(
            jax.ShapeDtypeStruct((ROWS // 2, tasks, PIECE), jnp.float32),
            jax.ShapeDtypeStruct((ROWS // 2, tasks, PIECE), jnp.bfloat16),
        ),
        in_specs=[smem, smem, hbm, vmem],
        out_specs=(vmem, vmem),
        scratch_shapes=[
            pltpu.VMEM((BLOCKS, tasks, WIDTH), jnp.bfloat16),
            pltpu.VMEM((ROWS, tasks, PIECE), jnp.float32),
            pltpu.VMEM((TILES, WIDTH, PIECE), jnp.bfloat16),
            pltpu.SemaphoreType.DMA((TILES,)),
        ],
        compiler_params=pltpu.CompilerParams(vmem_limit_bytes=VMEM_LIMIT),
        name="spread",
    )(ids, meta, weights, pieces)


def swap_cores(value):
    return lax.ppermute(value, "core", [(0, 1), (1, 0)])


def gather_pieces(piece):
    copies = jnp.broadcast_to(piece[None], (ROWS,) + piece.shape)
    return lax.all_to_all(copies, PLANE, 0, 0)


def body(fingerprints, activity, label_mask, pattern, counts):
    y, xh, z, xl, core = [lax.axis_index(axis) for axis in AXES]
    depth = fingerprints.shape[1]
    slots = pattern.shape[1]
    tasks = activity.shape[1]
    seeded = activity.T.astype(jnp.float32) * label_mask.astype(jnp.float32)[None, :]
    labels = seeded.astype(jnp.bfloat16).reshape(tasks // EXTRA, EXTRA, PIECE)
    extended = jnp.concatenate(
        [fingerprints, labels.transpose(1, 0, 2).reshape(EXTRA, depth)], axis=0
    )
    cols = lax.all_gather(extended, ("y", "xh", "xl"), axis=0, tiled=True)
    cols = cols.reshape(2, 4, 2, PIECE + EXTRA, depth)

    upward = [fingerprints]
    for step in range(4):
        upward.append(lax.ppermute(upward[-1], "z", [(i, (i + 1) % 8) for i in range(8)]))
    downward = [fingerprints]
    for step in range(3):
        downward.append(lax.ppermute(downward[-1], "z", [(i, (i + 7) % 8) for i in range(8)]))
    rows = upward + [downward[3], downward[2], downward[1]]
    rows = jnp.stack(rows + [swap_cores(row) for row in rows])

    squares = jnp.sum(jnp.square(fingerprints.astype(jnp.float32)), axis=1)
    table = jnp.concatenate([counts[:, None], pattern], axis=1).astype(jnp.float32).reshape(-1)
    info = jnp.concatenate([squares, table, jnp.zeros((PIECE - table.size,), jnp.float32)])
    info = jnp.broadcast_to(info[None, None], (ROWS, 8, 2 * PIECE))
    info = lax.all_to_all(info, ("core", "z"), 0, 0)[:, 0]
    away = jnp.arange(8, dtype=jnp.int32)
    nearby = (z - away) % 8
    line_info = info[jnp.concatenate([core * 8 + nearby, (1 - core) * 8 + nearby])]
    row_sq = line_info[:, :PIECE].reshape(ROWS, 1, PIECE)
    col_sq = gather_pieces(jnp.broadcast_to(squares[None], (8, PIECE)))[:, 0]
    col_sq = col_sq.reshape(BLOCKS, WIDTH, 1)
    tables = line_info[:, PIECE:PIECE + table.size].reshape(ROWS, 2, slots + 1)
    mine = lax.dynamic_index_in_dim(tables.astype(jnp.int32), y // 2, 1, keepdims=False)

    j = jnp.arange(BLOCKS, dtype=jnp.int32)
    col_block = (z * 4 + (j // 2) * 2 + core) * 2 + j % 2
    hit = (mine[None, :, 1:] == col_block[:, None, None]) & (
        jnp.arange(slots, dtype=jnp.int32)[None, None, :] < mine[None, :, :1]
    )
    live = jnp.any(hit, axis=2)
    flat = live.reshape(TILES).astype(jnp.int32)
    order = jnp.arange(TILES, dtype=jnp.int32)
    before = jnp.sum(jnp.where(order[None, :] < order[:, None], flat[None, :], 0), axis=1)
    ids = jnp.sum(
        jnp.where((before[None, :] == order[:, None]) & (flat[None, :] > 0), order[None, :], 0),
        axis=1,
    ).astype(jnp.int32)
    counted = jnp.sum(live.astype(jnp.int32), axis=1)
    even = counted + counted % 2
    block_start = jnp.sum(jnp.where(j[None, :] < j[:, None], even[None, :], 0), axis=1)
    block_before = jnp.sum(jnp.where(j[None, :] < j[:, None], counted[None, :], 0), axis=1)
    position = before + jnp.repeat(block_start - block_before, ROWS)
    spot = jnp.arange(TILES + 8, dtype=jnp.int32)
    pairs = jnp.max(
        jnp.where((position[None, :] <= spot[:, None]) & (flat[None, :] > 0), order[None, :], 0),
        axis=1,
    ).astype(jnp.int32)
    starts = (jnp.concatenate([block_start, jnp.sum(even)[None]]) // 2).astype(jnp.int32)
    own_tile = (xl * 2 + y // 2) * ROWS
    own_offset = ((y % 2) * 2 + xh) * PIECE
    meta = jnp.stack([jnp.sum(flat), own_offset, own_tile, z]).astype(jnp.int32)

    weights, keep, send, degree_keep, degree_send = build_weights(
        pairs, meta, starts, rows, cols, row_sq, col_sq
    )
    degree_sum = degree_keep + swap_cores(degree_send)
    high = lax.reduce_precision(degree_sum, 8, 7)
    low = degree_sum - high
    degree_rows = jnp.stack([high, low], axis=1).astype(jnp.bfloat16)
    degree_rows = jnp.concatenate([degree_rows, jnp.zeros((8, 14, PIECE), jnp.bfloat16)], axis=1)

    for iteration in range(ITERS):
        if iteration > 0:
            keep, send = spread_rows(ids, meta, weights, gathered)
        part = (keep + swap_cores(send).astype(jnp.float32)).astype(jnp.bfloat16)
        if iteration == 0:
            part = jnp.concatenate([part, degree_rows], axis=1)
        parts = lax.all_to_all(part, "z", 0, 0)
        summed = jnp.sum(parts.astype(jnp.float32), axis=0)
        if iteration == 0:
            degree_own = summed[tasks] + summed[tasks + 1]
            summed = summed[:tasks]
        labels = (PROPAGATE * summed / degree_own[None, :] + ANCHOR * seeded).astype(jnp.bfloat16)
        if iteration < ITERS - 1:
            gathered = gather_pieces(labels)
    return labels.T


def solution(mesh):
    split = Mesh(mesh.devices.reshape(SIZES), AXES)
    whole = ("z", "xl", "core", "y", "xh")
    blocks = ("z", "xl", "core")
    placed = (P(whole, None), P(whole, None), P(whole), P(blocks, None), P(blocks))
    return jax.shard_map(
        body, mesh=split, in_specs=placed, out_specs=P(whole, None), check_vma=False
    )
```

time: 246 us -> 249 us (1.012)
  blocking collectives: 104 us -> 84.5 us
  local copies, waits for them, and re-layouts: 6.72 us -> 21.8 us
  starting transfers between devices: 37.9 us -> 47.1 us
  Pallas kernels: 22.1 us -> 17.1 us
    all_gather x1, waiting for transfers between devices: 19.4 us -> 0.01 us  [body(): cols = lax.all_gather(extended, ('y', 'xh', 'xl'), axis=0, tiled=True)]
    all_to_all x0 -> x2, waiting for transfers between devices: none -> 17.4 us  [gather_pieces(): return lax.all_to_all(copies, PLANE, 0, 0)]
    all_to_all x2 -> x1, blocking collectives: 37 us -> 20.6 us  [gather_pieces(): return lax.all_to_all(copies, PLANE, 0, 0)]
    unnamed x17, local copies, waits for them, and re-layouts: 3.26 us -> 14.6 us
    all_to_all x0 -> x2, starting transfers between devices: none -> 10.4 us  [gather_pieces(): return lax.all_to_all(copies, PLANE, 0, 0)]
    ppermute x12, starting transfers between devices: 21.4 us -> 15.1 us  [swap_cores(): return lax.ppermute(value, 'core', [(0, 1), (1, 0)])]
    pallas_call x1, Pallas kernels: 15.8 us -> 10.2 us  [build_weights(): pl.pallas_call(weights_kernel, out_shape=(jax.ShapeDtypeStruct((TILES, WI...]
    all_to_all x3, blocking collectives: 67.5 us -> 63.9 us  [body(): parts = lax.all_to_all(part, 'z', 0, 0)]
  transfers between devices with their start and end apart: 21 -> 23, of which waited for: 10 -> 12; matrix products, arithmetic and copies ran while one was open for 2% -> 10% of each run, Pallas kernels for 0% -> 0%
where the time goes in v4:
time: 249 us; the launch traced here: 247 us
  blocking collectives  84.5 us (34%)
  waiting for transfers between devices  53.7 us (22%)
  starting transfers between devices  47.1 us (19%)
  local copies, waits for them, and re-layouts  21.8 us (9%)
  Pallas kernels  17.1 us (7%)
  between operations  13.6 us (5%)
  other arithmetic  9.33 us (4%)
    all_to_all x3, blocking collectives, body(): parts = lax.all_to_all(part, 'z', 0, 0)  63.9 us
    all_to_all x1, blocking collectives, gather_pieces(): return lax.all_to_all(copies, PLANE, 0, 0)  20.6 us
    ppermute x4, waiting for transfers between devices, body(): lax.ppermute(upward[-1], 'z', [(i, (i + 1) % 8) for i in range(8)])  19.6 us
    all_to_all x2, waiting for transfers between devices, gather_pieces(): return lax.all_to_all(copies, PLANE, 0, 0)  17.4 us
    ppermute x12, starting transfers between devices, swap_cores(): return lax.ppermute(value, 'core', [(0, 1), (1, 0)])  15.1 us
    unnamed x17, local copies, waits for them, and re-layouts  14.6 us
    all_to_all x2, starting transfers between devices, gather_pieces(): return lax.all_to_all(copies, PLANE, 0, 0)  10.4 us
    pallas_call x1, Pallas kernels, build_weights(): pl.pallas_call(weights_kernel, out_shape=(jax.ShapeDtypeStruct((TILES, WI...  10.2 us
  transfers between devices with their start and end apart: 23, of which 12 were waited for; matrix products, arithmetic and copies ran while one was open for 10% of the time, Pallas kernels for 0%

profile of v4, /device:TPU:1, one launch (start us, length us, event | category | flops | bytes accessed | tf_op | source)
XLA Modules:
  0.0 247.2 jit_solution(3463506638448124942)
XLA Ops:
  10.1 2.5 %collective-permute-start = (bf16[128,2048]{1,0:T(8,128)(2,1)}, bf16[128,2048]{1,0:T(8,128)(2,1)S(1)}, u32[]{:S(2)}, u32[]{:S(2)}) collective-permute-start(bf16[128,2048]{1,0:T(8,128)(2,1)} %param.5), channel_id=1, source_target_pairs={{0,4},{4,8},{8,12},{12,16},{16,20},{20,24},{24,28},{28,0},{1,5},{5... | collective-permute-start | bytes 1572872 | tf_op jit(solution)/shard_map/ppermute | solution.py:279
  12.7 4.0 %collective-permute-start.4 = (bf16[128,2048]{1,0:T(8,128)(2,1)}, bf16[128,2048]{1,0:T(8,128)(2,1)S(1)}, u32[]{:S(2)}, u32[]{:S(2)}) collective-permute-start(bf16[128,2048]{1,0:T(8,128)(2,1)} %param.5), channel_id=1, source_target_pairs={{0,28},{4,0},{8,4},{12,8},{16,12},{20,16},{24,20},{28,24},{1,29},{... | collective-permute-start | bytes 1572872 | tf_op jit(solution)/shard_map/ppermute | solution.py:282
  19.5 6.8 %all-to-all-start.1 = ((f32[16,8,128]{2,1,0:T(8,128)}), f32[16,8,128]{2,1,0:T(8,128)S(1)}, u32[]{:S(2)}, u32[]{:S(2)}) async-start(f32[16,8,128]{2,1,0:T(8,128)} %broadcast_in_dim_broadcast_in_dim_broadcast_in_dim.2), calls=%async_computation.1 | async-start | bytes 131072 | tf_op jit(solution)/shard_map/all_to_all | solution.py:261
  29.9 3.1 %all-to-all-done.1 = f32[16,8,128]{2,1,0:T(8,128)S(1)} async-done(((f32[16,8,128]{2,1,0:T(8,128)}), f32[16,8,128]{2,1,0:T(8,128)S(1)}, u32[]{:S(2)}, u32[]{:S(2)}) %all-to-all-start.1) | async-done | bytes 65568 | tf_op jit(solution)/shard_map/all_to_all | solution.py:261
  33.7 7.2 %all-to-all-start = ((f32[16,8,256]{2,1,0:T(8,128)}), f32[16,8,256]{2,1,0:T(8,128)S(1)}, u32[]{:S(2)}, u32[]{:S(2)}) async-start(f32[16,8,256]{2,1,0:T(8,128)} %broadcast_in_dim.64), calls=%async_computation | async-start | bytes 262144 | tf_op jit(solution)/shard_map/all_to_all | solution.py:290
  41.9 6.3 %all-to-all-done = f32[16,8,256]{2,1,0:T(8,128)S(1)} async-done(((f32[16,8,256]{2,1,0:T(8,128)}), f32[16,8,256]{2,1,0:T(8,128)S(1)}, u32[]{:S(2)}, u32[]{:S(2)}) %all-to-all-start) | async-done | bytes 131104 | tf_op jit(solution)/shard_map/all_to_all | solution.py:290
  53.6 11.1 %collective-permute-done.1 = bf16[128,2048]{1,0:T(8,128)(2,1)S(1)} collective-permute-done((bf16[128,2048]{1,0:T(8,128)(2,1)S(1)}, bf16[128,2048]{1,0:T(8,128)(2,1)S(1)}, u32[]{:S(2)}, u32[]{:S(2)}) %collective-permute-start.1) | collective-permute-done | bytes 524320 | tf_op jit(solution)/shard_map/ppermute | solution.py:279
  68.2 2.4 collective-permute-start.5
  71.7 5.6 %collective-permute-done.2 = bf16[128,2048]{1,0:T(8,128)(2,1)S(1)} collective-permute-done((bf16[128,2048]{1,0:T(8,128)(2,1)S(1)}, bf16[128,2048]{1,0:T(8,128)(2,1)S(1)}, u32[]{:S(2)}, u32[]{:S(2)}) %collective-permute-start.2) | collective-permute-done | bytes 524320 | tf_op jit(solution)/shard_map/ppermute | solution.py:279
  78.2 3.6 %collective-permute-done.5 = bf16[128,2048]{1,0:T(8,128)(2,1)S(1)} collective-permute-done((bf16[128,2048]{1,0:T(8,128)(2,1)S(1)}, bf16[128,2048]{1,0:T(8,128)(2,1)S(1)}, u32[]{:S(2)}, u32[]{:S(2)}) %collective-permute-start.5) | collective-permute-done | bytes 524320 | tf_op jit(solution)/shard_map/ppermute | solution.py:282
  81.8 3.5 %collective-permute-start.6 = (bf16[128,2048]{1,0:T(8,128)(2,1)S(1)}, bf16[128,2048]{1,0:T(8,128)(2,1)S(1)}, u32[]{:S(2)}, u32[]{:S(2)}) collective-permute-start(bf16[128,2048]{1,0:T(8,128)(2,1)S(1)} %collective-permute-done.5), channel_id=1, source_target_pairs={{0,28},{4,0},{8,4},{12,8},{16,12},{20,16},{24,20},{28,24},{1,29},{... | collective-permute-start | bytes 1572872 | tf_op jit(solution)/shard_map/ppermute | solution.py:282
  86.2 3.0 %collective-permute-done.3 = bf16[128,2048]{1,0:T(8,128)(2,1)S(1)} collective-permute-done((bf16[128,2048]{1,0:T(8,128)(2,1)S(1)}, bf16[128,2048]{1,0:T(8,128)(2,1)S(1)}, u32[]{:S(2)}, u32[]{:S(2)}) %collective-permute-start.3) | collective-permute-done | bytes 524320 | tf_op jit(solution)/shard_map/ppermute | solution.py:279
  89.1 3.7 %collective-permute-start.9 = (bf16[128,2048]{1,0:T(8,128)(2,1)S(1)}, bf16[128,2048]{1,0:T(8,128)(2,1)S(1)}, u32[]{:S(2)}, u32[]{:S(2)}) collective-permute-start(bf16[128,2048]{1,0:T(8,128)(2,1)S(1)} %collective-permute-done.1), channel_id=1, source_target_pairs={{0,1},{1,0},{2,3},{3,2},{4,5},{5,4},{6,7},{7,6},{8,9},{9,8},{10,11... | collective-permute-start | bytes 1572872 | tf_op jit(solution)/shard_map/ppermute | solution.py:256
  107.5 10.2 %weights.1 = (bf16[64,512,128]{2,1,0:T(8,128)(2,1)}, f32[8,256,128]{2,1,0:T(8,128)S(1)}, bf16[8,256,128]{2,1,0:T(8,128)(2,1)S(1)}, f32[8,128]{1,0:T(8,128)S(1)}, f32[8,128]{1,0:T(8,128)S(1)}) custom-call(s32[72]{0:T(128)S(1)} %select_reduce_fusion.pairs, s32[4]{0:T(128)S(1)} %pad_add_fusion.meta, s32[5]{0:T(128)S(1)} %and_select_fusion.starts, ...), custom_call_target="tpu_custom_call" | custom-call | flops 4294967296 | bytes 16777216 | tf_op jit(solution)/shard_map/weights/pallas_call | solution.py:168
  120.1 24.4 %all_to_all.35 = bf16[8,272,128]{2,1,0:T(8,128)(2,1)S(1)} all-to-all(bf16[8,272,128]{2,1,0:T(8,128)(2,1)S(1)} %maximum_maximum_fusion), channel_id=1, replica_groups=mesh['y'=4,'xh'=2,'z'=8,'xl'=2,'core'=2] {'z'}, dimensions={0} | all-to-all | bytes 1114112 | tf_op jit(solution)/shard_map/all_to_all | solution.py:343
  145.8 3.7 %all-to-all-start.3 = ((bf16[16,256,128]{2,1,0:T(8,128)(2,1)}), bf16[16,256,128]{2,1,0:T(8,128)(2,1)S(1)}, u32[]{:S(2)}, u32[]{:S(2)}) async-start(bf16[16,256,128]{2,1,0:T(8,128)(2,1)} %broadcast_in_dim.119), calls=%async_computation.3 | async-start | bytes 2097152 | tf_op jit(solution)/shard_map/all_to_all | solution.py:261
  149.6 14.3 %all-to-all-done.3.pieces = bf16[16,256,128]{2,1,0:T(8,128)(2,1)S(1)} async-done(((bf16[16,256,128]{2,1,0:T(8,128)(2,1)}), bf16[16,256,128]{2,1,0:T(8,128)(2,1)S(1)}, u32[]{:S(2)}, u32[]{:S(2)}) %all-to-all-start.3) | async-done | bytes 1048608 | tf_op jit(solution)/shard_map/all_to_all | solution.py:261
  163.8 3.5 %spread.2 = (f32[8,256,128]{2,1,0:T(8,128)S(1)}, bf16[8,256,128]{2,1,0:T(8,128)(2,1)S(1)}) custom-call(s32[64]{0:T(128)S(1)} %select_reduce_fusion.1.ids, s32[4]{0:T(128)S(1)} %pad_add_fusion.meta, bf16[64,512,128]{2,1,0:T(8,128)(2,1)} %get-tuple-element.14.weights, bf16[16,256,128]{2,1,0:T(8,128)(2,1)S(1)} %all-to-all-done.3.pieces), custom_call_target="tpu_custom_call" | custom-call | tf_op jit(solution)/shard_map/spread/pallas_call | solution.py:236
  167.3 2.6 %collective-permute-start.17 = (bf16[8,256,128]{2,1,0:T(8,128)(2,1)S(1)}, bf16[8,256,128]{2,1,0:T(8,128)(2,1)S(1)}, u32[]{:S(2)}, u32[]{:S(2)}) collective-permute-start(bf16[8,256,128]{2,1,0:T(8,128)(2,1)S(1)} %get-tuple-element.20), channel_id=1, source_target_pairs={{0,1},{1,0},{2,3},{3,2},{4,5},{5,4},{6,7},{7,6},{8,9},{9,8},{10,11... | collective-permute-start | bytes 1572872 | tf_op jit(solution)/shard_map/ppermute | solution.py:256
  171.6 19.1 %all_to_all.36 = bf16[8,256,128]{2,1,0:T(8,128)(2,1)S(1)} all-to-all(bf16[8,256,128]{2,1,0:T(8,128)(2,1)S(1)} %add_convert_fusion.1), channel_id=1, replica_groups=mesh['y'=4,'xh'=2,'z'=8,'xl'=2,'core'=2] {'z'}, dimensions={0} | all-to-all | bytes 1048576 | tf_op jit(solution)/shard_map/all_to_all | solution.py:343
  191.0 20.6 %all_to_all.37.pieces = bf16[16,256,128]{2,1,0:T(8,128)(2,1)S(1)} all-to-all(bf16[16,256,128]{2,1,0:T(8,128)(2,1)S(1)} %broadcast_in_dim.120), channel_id=1, replica_groups=mesh['y'=4,'xh'=2,'z'=8,'xl'=2,'core'=2] {'xl','y','xh'}, dimensions={0} | all-to-all | bytes 2097152 | tf_op jit(solution)/shard_map/all_to_all | solution.py:261
  211.6 3.5 %spread.3 = (f32[8,256,128]{2,1,0:T(8,128)S(1)}, bf16[8,256,128]{2,1,0:T(8,128)(2,1)S(1)}) custom-call(s32[64]{0:T(128)S(1)} %select_reduce_fusion.1.ids, s32[4]{0:T(128)S(1)} %pad_add_fusion.meta, bf16[64,512,128]{2,1,0:T(8,128)(2,1)} %get-tuple-element.14.weights, bf16[16,256,128]{2,1,0:T(8,128)(2,1)S(1)} %all_to_all.37.pieces), custom_call_target="tpu_custom_call" | custom-call | tf_op jit(solution)/shard_map/spread/pallas_call | solution.py:236
  215.1 2.4 collective-permute-start.18
  219.1 20.4 %all_to_all.38 = bf16[8,256,128]{2,1,0:T(8,128)(2,1)S(1)} all-to-all(bf16[8,256,128]{2,1,0:T(8,128)(2,1)S(1)} %add_convert_fusion), channel_id=1, replica_groups=mesh['y'=4,'xh'=2,'z'=8,'xl'=2,'core'=2] {'z'}, dimensions={0} | all-to-all | bytes 1048576 | tf_op jit(solution)/shard_map/all_to_all | solution.py:343
  (113 shorter events, 46.2 us)
Async XLA Ops:
  6.5 101.0 %all-gather.2.cloned.1.call-start = ((), (), s32[]{:S(2)}) async-start(), calls=%async_computation.7 | async-start | bytes 10027008 | tf_op jit(solution)/shard_map/all_gather | solution.py:274
  10.1 41.1 %collective-permute-start = (bf16[128,2048]{1,0:T(8,128)(2,1)}, bf16[128,2048]{1,0:T(8,128)(2,1)S(1)}, u32[]{:S(2)}, u32[]{:S(2)}) collective-permute-start(bf16[128,2048]{1,0:T(8,128)(2,1)} %param.5), channel_id=1, source_target_pairs={{0,4},{4,8},{8,12},{12,16},{16,20},{20,24},{24,28},{28,0},{1,5},{5... | collective-permute-start | bytes 1572872 | tf_op jit(solution)/shard_map/ppermute | solution.py:279
  12.7 55.5 %collective-permute-start.4 = (bf16[128,2048]{1,0:T(8,128)(2,1)}, bf16[128,2048]{1,0:T(8,128)(2,1)S(1)}, u32[]{:S(2)}, u32[]{:S(2)}) collective-permute-start(bf16[128,2048]{1,0:T(8,128)(2,1)} %param.5), channel_id=1, source_target_pairs={{0,28},{4,0},{8,4},{12,8},{16,12},{20,16},{24,20},{28,24},{1,29},{... | collective-permute-start | bytes 1572872 | tf_op jit(solution)/shard_map/ppermute | solution.py:282
  16.7 83.4 %collective-permute-start.7 = (bf16[128,2048]{1,0:T(8,128)(2,1)}, bf16[128,2048]{1,0:T(8,128)(2,1)S(1)}, u32[]{:S(2)}, u32[]{:S(2)}) collective-permute-start(bf16[128,2048]{1,0:T(8,128)(2,1)} %param.5), channel_id=1, source_target_pairs={{0,1},{1,0},{2,3},{3,2},{4,5},{5,4},{6,7},{7,6},{8,9},{9,8},{10,11... | collective-permute-start | bytes 1572872 | tf_op jit(solution)/shard_map/ppermute | solution.py:256
  19.5 13.5 %all-to-all-start.1 = ((f32[16,8,128]{2,1,0:T(8,128)}), f32[16,8,128]{2,1,0:T(8,128)S(1)}, u32[]{:S(2)}, u32[]{:S(2)}) async-start(f32[16,8,128]{2,1,0:T(8,128)} %broadcast_in_dim_broadcast_in_dim_broadcast_in_dim.2), calls=%async_computation.1 | async-start | bytes 131072 | tf_op jit(solution)/shard_map/all_to_all | solution.py:261
  33.7 14.5 %all-to-all-start = ((f32[16,8,256]{2,1,0:T(8,128)}), f32[16,8,256]{2,1,0:T(8,128)S(1)}, u32[]{:S(2)}, u32[]{:S(2)}) async-start(f32[16,8,256]{2,1,0:T(8,128)} %broadcast_in_dim.64), calls=%async_computation | async-start | bytes 262144 | tf_op jit(solution)/shard_map/all_to_all | solution.py:290
  51.2 13.5 %collective-permute-start.1 = (bf16[128,2048]{1,0:T(8,128)(2,1)S(1)}, bf16[128,2048]{1,0:T(8,128)(2,1)S(1)}, u32[]{:S(2)}, u32[]{:S(2)}) collective-permute-start(bf16[128,2048]{1,0:T(8,128)(2,1)S(1)} %collective-permute-done), channel_id=1, source_target_pairs={{0,4},{4,8},{8,12},{12,16},{16,20},{20,24},{24,28},{28,0},{1,5},{5... | collective-permute-start | bytes 1572872 | tf_op jit(solution)/shard_map/ppermute | solution.py:279
  64.7 12.6 %collective-permute-start.2 = (bf16[128,2048]{1,0:T(8,128)(2,1)S(1)}, bf16[128,2048]{1,0:T(8,128)(2,1)S(1)}, u32[]{:S(2)}, u32[]{:S(2)}) collective-permute-start(bf16[128,2048]{1,0:T(8,128)(2,1)S(1)} %collective-permute-done.1), channel_id=1, source_target_pairs={{0,4},{4,8},{8,12},{12,16},{16,20},{20,24},{24,28},{28,0},{1,5},{5... | collective-permute-start | bytes 1572872 | tf_op jit(solution)/shard_map/ppermute | solution.py:279
  65.9 35.0 %collective-permute-start.8 = (bf16[128,2048]{1,0:T(8,128)(2,1)S(1)}, bf16[128,2048]{1,0:T(8,128)(2,1)S(1)}, u32[]{:S(2)}, u32[]{:S(2)}) collective-permute-start(bf16[128,2048]{1,0:T(8,128)(2,1)S(1)} %collective-permute-done), channel_id=1, source_target_pairs={{0,1},{1,0},{2,3},{3,2},{4,5},{5,4},{6,7},{7,6},{8,9},{9,8},{10,11... | collective-permute-start | bytes 1572872 | tf_op jit(solution)/shard_map/ppermute | solution.py:256
  68.2 13.7 %collective-permute-start.5 = (bf16[128,2048]{1,0:T(8,128)(2,1)S(1)}, bf16[128,2048]{1,0:T(8,128)(2,1)S(1)}, u32[]{:S(2)}, u32[]{:S(2)}) collective-permute-start(bf16[128,2048]{1,0:T(8,128)(2,1)S(1)} %collective-permute-done.4), channel_id=1, source_target_pairs={{0,28},{4,0},{8,4},{12,8},{16,12},{20,16},{24,20},{28,24},{1,29},{... | collective-permute-start | bytes 1572872 | tf_op jit(solution)/shard_map/ppermute | solution.py:282
  70.6 36.1 %collective-permute-start.14 = (bf16[128,2048]{1,0:T(8,128)(2,1)S(1)}, bf16[128,2048]{1,0:T(8,128)(2,1)S(1)}, u32[]{:S(2)}, u32[]{:S(2)}) collective-permute-start(bf16[128,2048]{1,0:T(8,128)(2,1)S(1)} %collective-permute-done.4), channel_id=1, source_target_pairs={{0,1},{1,0},{2,3},{3,2},{4,5},{5,4},{6,7},{7,6},{8,9},{9,8},{10,11... | collective-permute-start | bytes 1572872 | tf_op jit(solution)/shard_map/ppermute | solution.py:256
  77.3 11.8 %collective-permute-start.3 = (bf16[128,2048]{1,0:T(8,128)(2,1)S(1)}, bf16[128,2048]{1,0:T(8,128)(2,1)S(1)}, u32[]{:S(2)}, u32[]{:S(2)}) collective-permute-start(bf16[128,2048]{1,0:T(8,128)(2,1)S(1)} %collective-permute-done.2), channel_id=1, source_target_pairs={{0,4},{4,8},{8,12},{12,16},{16,20},{20,24},{24,28},{28,0},{1,5},{5... | collective-permute-start | bytes 1572872 | tf_op jit(solution)/shard_map/ppermute | solution.py:279
  81.8 14.0 %collective-permute-start.6 = (bf16[128,2048]{1,0:T(8,128)(2,1)S(1)}, bf16[128,2048]{1,0:T(8,128)(2,1)S(1)}, u32[]{:S(2)}, u32[]{:S(2)}) collective-permute-start(bf16[128,2048]{1,0:T(8,128)(2,1)S(1)} %collective-permute-done.5), channel_id=1, source_target_pairs={{0,28},{4,0},{8,4},{12,8},{16,12},{20,16},{24,20},{28,24},{1,29},{... | collective-permute-start | bytes 1572872 | tf_op jit(solution)/shard_map/ppermute | solution.py:282
  89.1 13.1 %collective-permute-start.9 = (bf16[128,2048]{1,0:T(8,128)(2,1)S(1)}, bf16[128,2048]{1,0:T(8,128)(2,1)S(1)}, u32[]{:S(2)}, u32[]{:S(2)}) collective-permute-start(bf16[128,2048]{1,0:T(8,128)(2,1)S(1)} %collective-permute-done.1), channel_id=1, source_target_pairs={{0,1},{1,0},{2,3},{3,2},{4,5},{5,4},{6,7},{7,6},{8,9},{9,8},{10,11... | collective-permute-start | bytes 1572872 | tf_op jit(solution)/shard_map/ppermute | solution.py:256
  95.8 10.0 %collective-permute-start.13 = (bf16[128,2048]{1,0:T(8,128)(2,1)S(1)}, bf16[128,2048]{1,0:T(8,128)(2,1)S(1)}, u32[]{:S(2)}, u32[]{:S(2)}) collective-permute-start(bf16[128,2048]{1,0:T(8,128)(2,1)S(1)} %collective-permute-done.5), channel_id=1, source_target_pairs={{0,1},{1,0},{2,3},{3,2},{4,5},{5,4},{6,7},{7,6},{8,9},{9,8},{10,11... | collective-permute-start | bytes 1572872 | tf_op jit(solution)/shard_map/ppermute | solution.py:256
  100.1 3.0 %collective-permute-start.10 = (bf16[128,2048]{1,0:T(8,128)(2,1)S(1)}, bf16[128,2048]{1,0:T(8,128)(2,1)S(1)}, u32[]{:S(2)}, u32[]{:S(2)}) collective-permute-start(bf16[128,2048]{1,0:T(8,128)(2,1)S(1)} %collective-permute-done.2), channel_id=1, source_target_pairs={{0,1},{1,0},{2,3},{3,2},{4,5},{5,4},{6,7},{7,6},{8,9},{9,8},{10,11... | collective-permute-start | bytes 1572872 | tf_op jit(solution)/shard_map/ppermute | solution.py:256
  100.9 4.1 %collective-permute-start.12 = (bf16[128,2048]{1,0:T(8,128)(2,1)S(1)}, bf16[128,2048]{1,0:T(8,128)(2,1)S(1)}, u32[]{:S(2)}, u32[]{:S(2)}) collective-permute-start(bf16[128,2048]{1,0:T(8,128)(2,1)S(1)} %collective-permute-done.6), channel_id=1, source_target_pairs={{0,1},{1,0},{2,3},{3,2},{4,5},{5,4},{6,7},{7,6},{8,9},{9,8},{10,11... | collective-permute-start | bytes 1572872 | tf_op jit(solution)/shard_map/ppermute | solution.py:256
  102.2 1.9 collective-permute-start.11
  117.7 2.0 collective-permute-start.15
  117.8 1.9 collective-permute-start.16
  145.8 18.0 %all-to-all-start.3 = ((bf16[16,256,128]{2,1,0:T(8,128)(2,1)}), bf16[16,256,128]{2,1,0:T(8,128)(2,1)S(1)}, u32[]{:S(2)}, u32[]{:S(2)}) async-start(bf16[16,256,128]{2,1,0:T(8,128)(2,1)} %broadcast_in_dim.119), calls=%async_computation.3 | async-start | bytes 2097152 | tf_op jit(solution)/shard_map/all_to_all | solution.py:261
  167.3 4.1 %collective-permute-start.17 = (bf16[8,256,128]{2,1,0:T(8,128)(2,1)S(1)}, bf16[8,256,128]{2,1,0:T(8,128)(2,1)S(1)}, u32[]{:S(2)}, u32[]{:S(2)}) collective-permute-start(bf16[8,256,128]{2,1,0:T(8,128)(2,1)S(1)} %get-tuple-element.20), channel_id=1, source_target_pairs={{0,1},{1,0},{2,3},{3,2},{4,5},{5,4},{6,7},{7,6},{8,9},{9,8},{10,11... | collective-permute-start | bytes 1572872 | tf_op jit(solution)/shard_map/ppermute | solution.py:256
  215.1 3.9 %collective-permute-start.18 = (bf16[8,256,128]{2,1,0:T(8,128)(2,1)S(1)}, bf16[8,256,128]{2,1,0:T(8,128)(2,1)S(1)}, u32[]{:S(2)}, u32[]{:S(2)}) collective-permute-start(bf16[8,256,128]{2,1,0:T(8,128)(2,1)S(1)} %get-tuple-element.22), channel_id=1, source_target_pairs={{0,1},{1,0},{2,3},{3,2},{4,5},{5,4},{6,7},{7,6},{8,9},{9,8},{10,11... | collective-permute-start | bytes 1572872 | tf_op jit(solution)/shard_map/ppermute | solution.py:256
Sparse Core Ops, SparseCore 0:
  10.3 84.4 all-gather.1

commit v5 on v4

--- a/solution.py
+++ b/solution.py
@@ -35,22 +35,29 @@
         send[piece] = total[half + place].astype(jnp.bfloat16)
 
 
-def weights_kernel(pairs, meta, starts, rows, cols, row_sq, col_sq,
-                   weights, keep, send, degree_keep, degree_send,
-                   col_buf, row_buf, tile_buf, label_raw, labels, total, degree,
-                   col_sem, row_sem, tile_sem, label_sem):
+def weights_kernel(pairs, meta, starts, *refs):
+    rows = refs[:ROWS]
+    (cols, row_sq, col_sq, weights, keep, send, degree_keep, degree_send,
+     col_buf, row_buf, tile_buf, label_raw, labels, total, degree,
+     col_sem, row_sem, tile_sem, label_sem) = refs[ROWS:]
     live = starts[BLOCKS]
     own_offset = meta[1]
     own_tile = meta[2]
     z = meta[3]
 
-    def row_copy(q, side):
+    def row_copy(q, side, source):
         slot = lax.rem(q, 3)
         return pltpu.make_async_copy(
-            rows.at[lax.rem(pairs[2 * q + side], ROWS)],
-            row_buf.at[slot, pl.ds(side * PIECE, PIECE)],
-            row_sem.at[slot, side],
-        )
+            rows[source], row_buf.at[slot, pl.ds(side * PIECE, PIECE)], row_sem.at[slot, side]
+        )
+
+    def start_rows(q):
+        for side in range(2):
+            wanted = lax.rem(pairs[2 * q + side], ROWS)
+            for source in range(ROWS):
+                @pl.when(wanted == source)
+                def _():
+                    row_copy(q, side, source).start()
 
     def col_copy(j):
         return pltpu.make_async_copy(
@@ -66,8 +73,7 @@
     for first in range(2):
         @pl.when(first < live)
         def _():
-            row_copy(first, 0).start()
-            row_copy(first, 1).start()
+            start_rows(first)
     label_copy = pltpu.make_async_copy(
         cols.at[:, :, :, pl.ds(PIECE, EXTRA)], label_raw, label_sem
     )
@@ -97,11 +103,10 @@
         def pair(q, inner_carry):
             @pl.when(q + 2 < live)
             def _():
-                row_copy(q + 2, 0).start()
-                row_copy(q + 2, 1).start()
-
-            row_copy(q, 0).wait()
-            row_copy(q, 1).wait()
+                start_rows(q + 2)
+
+            row_copy(q, 0, 0).wait()
+            row_copy(q, 1, 0).wait()
             one = pairs[2 * q]
             two = pairs[2 * q + 1]
             place_one = lax.rem(one, ROWS)
@@ -174,7 +179,7 @@
             jax.ShapeDtypeStruct((ROWS // 2, PIECE), jnp.float32),
             jax.ShapeDtypeStruct((ROWS // 2, PIECE), jnp.float32),
         ),
-        in_specs=[smem, smem, smem, hbm, hbm, vmem, vmem],
+        in_specs=[smem, smem, smem] + [hbm] * ROWS + [hbm, vmem, vmem],
         out_specs=(hbm, vmem, vmem, vmem, vmem),
         scratch_shapes=[
             pltpu.VMEM((BLOCKS, WIDTH // PIECE, PIECE, depth), jnp.bfloat16),
@@ -196,7 +201,7 @@
             transcendentals=16 * PIECE * WIDTH,
         ),
         name="weights",
-    )(pairs, meta, starts, rows, cols, row_sq, col_sq)
+    )(pairs, meta, starts, *rows, cols, row_sq, col_sq)
 
 
 def spread_kernel(ids, meta, weights, pieces, keep, send, labels, total, tile_buf, tile_sem):
@@ -281,7 +286,7 @@
     for step in range(3):
         downward.append(lax.ppermute(downward[-1], "z", [(i, (i + 7) % 8) for i in range(8)]))
     rows = upward + [downward[3], downward[2], downward[1]]
-    rows = jnp.stack(rows + [swap_cores(row) for row in rows])
+    rows = rows + [swap_cores(row) for row in rows]
 
     squares = jnp.sum(jnp.square(fingerprints.astype(jnp.float32)), axis=1)
     table = jnp.concatenate([counts[:, None], pattern], axis=1).astype(jnp.float32).reshape(-1)
@@ -292,6 +297,7 @@
     nearby = (z - away) % 8
     line_info = info[jnp.concatenate([core * 8 + nearby, (1 - core) * 8 + nearby])]
     row_sq = line_info[:, :PIECE].reshape(ROWS, 1, PIECE)
+    squares, rows[4], rows[5] = lax.optimization_barrier((squares, rows[4], rows[5]))
     col_sq = gather_pieces(jnp.broadcast_to(squares[None], (8, PIECE)))[:, 0]
     col_sq = col_sq.reshape(BLOCKS, WIDTH, 1)
     tables = line_info[:, PIECE:PIECE + table.size].reshape(ROWS, 2, slots + 1)

time: 249 us -> 245 us (0.984)
  local copies, waits for them, and re-layouts: 21.8 us -> 7.76 us
  waiting for transfers between devices: 53.7 us -> 60.8 us
  blocking collectives: 84.5 us -> 87.6 us
  Pallas kernels: 17.1 us -> 20 us
  starting transfers between devices: 47.1 us -> 44.4 us
    unnamed x17 -> x8, local copies, waits for them, and re-layouts: 14.6 us -> 1.02 us
    ppermute x4, waiting for transfers between devices: 19.6 us -> 26.2 us  [body(): lax.ppermute(upward[-1], 'z', [(i, (i + 1) % 8) for i in range(8)])]
    ppermute x3, waiting for transfers between devices: 5.77 us -> 0.01 us  [body(): lax.ppermute(downward[-1], 'z', [(i, (i + 7) % 8) for i in range(8)])]
    ppermute x3, starting transfers between devices: 9.94 us -> 5.04 us  [body(): lax.ppermute(downward[-1], 'z', [(i, (i + 7) % 8) for i in range(8)])]
    all_to_all x3, blocking collectives: 63.9 us -> 67.8 us  [body(): parts = lax.all_to_all(part, 'z', 0, 0)]
    all_to_all x2, waiting for transfers between devices: 17.4 us -> 20.6 us  [gather_pieces(): return lax.all_to_all(copies, PLANE, 0, 0)]
  transfers between devices with their start and end apart: 23 -> 23, of which waited for: 12 -> 10; matrix products, arithmetic and copies ran while one was open for 10% -> 4% of each run, Pallas kernels for 0% -> 0%
where the time goes in v5:
time: 245 us; the launch traced here: 243 us
  blocking collectives  87.6 us (36%)
  waiting for transfers between devices  60.8 us (25%)
  starting transfers between devices  44.4 us (18%)
  Pallas kernels  20 us (8%)
  between operations  13.7 us (6%)
  other arithmetic  8.9 us (4%)
  local copies, waits for them, and re-layouts  7.76 us (3%)
    all_to_all x3, blocking collectives, body(): parts = lax.all_to_all(part, 'z', 0, 0)  67.8 us
    ppermute x4, waiting for transfers between devices, body(): lax.ppermute(upward[-1], 'z', [(i, (i + 1) % 8) for i in range(8)])  26.2 us
    all_to_all x2, waiting for transfers between devices, gather_pieces(): return lax.all_to_all(copies, PLANE, 0, 0)  20.6 us
    all_to_all x1, blocking collectives, gather_pieces(): return lax.all_to_all(copies, PLANE, 0, 0)  19.8 us
    ppermute x12, starting transfers between devices, swap_cores(): return lax.ppermute(value, 'core', [(0, 1), (1, 0)])  14.8 us
    pallas_call x1, Pallas kernels, build_weights(): pl.pallas_call(weights_kernel, out_shape=(jax.ShapeDtypeStruct((TILES, WI...  12.2 us
    all_to_all x2, starting transfers between devices, gather_pieces(): return lax.all_to_all(copies, PLANE, 0, 0)  12 us
    all_to_all x1, waiting for transfers between devices, body(): info = lax.all_to_all(info, ('core', 'z'), 0, 0)[:, 0]  7.85 us
  transfers between devices with their start and end apart: 23, of which 10 were waited for; matrix products, arithmetic and copies ran while one was open for 4% of the time, Pallas kernels for 0%

profile of v5, /device:TPU:1, one launch (start us, length us, event | category | flops | bytes accessed | tf_op | source)
XLA Modules:
  0.0 243.1 jit_solution(3048061618056178576)
XLA Ops:
  10.2 2.5 %collective-permute-start = (bf16[128,2048]{1,0:T(8,128)(2,1)S(1)}, bf16[128,2048]{1,0:T(8,128)(2,1)S(1)}, u32[]{:S(2)}, u32[]{:S(2)}) collective-permute-start(bf16[128,2048]{1,0:T(8,128)(2,1)S(1)} %copy-done), channel_id=1, source_target_pairs={{0,4},{4,8},{8,12},{12,16},{16,20},{20,24},{24,28},{28,0},{1,5},{5... | collective-permute-start | bytes 1572872 | tf_op jit(solution)/shard_map/ppermute | solution.py:284
  12.7 4.0 %collective-permute-start.4 = (bf16[128,2048]{1,0:T(8,128)(2,1)S(1)}, bf16[128,2048]{1,0:T(8,128)(2,1)S(1)}, u32[]{:S(2)}, u32[]{:S(2)}) collective-permute-start(bf16[128,2048]{1,0:T(8,128)(2,1)S(1)} %copy-done), channel_id=1, source_target_pairs={{0,28},{4,0},{8,4},{12,8},{16,12},{20,16},{24,20},{28,24},{1,29},{... | collective-permute-start | bytes 1572872 | tf_op jit(solution)/shard_map/ppermute | solution.py:287
  18.9 5.9 %all-to-all-start = ((f32[16,8,256]{2,1,0:T(8,128)}), f32[16,8,256]{2,1,0:T(8,128)S(1)}, u32[]{:S(2)}, u32[]{:S(2)}) async-start(f32[16,8,256]{2,1,0:T(8,128)} %broadcast_in_dim.64), calls=%async_computation | async-start | bytes 262144 | tf_op jit(solution)/shard_map/all_to_all | solution.py:295
  24.9 7.8 %all-to-all-done = f32[16,8,256]{2,1,0:T(8,128)S(1)} async-done(((f32[16,8,256]{2,1,0:T(8,128)}), f32[16,8,256]{2,1,0:T(8,128)S(1)}, u32[]{:S(2)}, u32[]{:S(2)}) %all-to-all-start) | async-done | bytes 131104 | tf_op jit(solution)/shard_map/all_to_all | solution.py:295
  33.4 3.0 %collective-permute-start.1 = (bf16[128,2048]{1,0:T(8,128)(2,1)S(1)}, bf16[128,2048]{1,0:T(8,128)(2,1)S(1)}, u32[]{:S(2)}, u32[]{:S(2)}) collective-permute-start(bf16[128,2048]{1,0:T(8,128)(2,1)S(1)} %collective-permute-done.refs_1_), channel_id=1, source_target_pairs={{0,4},{4,8},{8,12},{12,16},{16,20},{20,24},{24,28},{28,0},{1,5},{5... | collective-permute-start | bytes 1572872 | tf_op jit(solution)/shard_map/ppermute | solution.py:284
  36.7 11.1 %collective-permute-done.1.refs_2_ = bf16[128,2048]{1,0:T(8,128)(2,1)S(1)} collective-permute-done((bf16[128,2048]{1,0:T(8,128)(2,1)S(1)}, bf16[128,2048]{1,0:T(8,128)(2,1)S(1)}, u32[]{:S(2)}, u32[]{:S(2)}) %collective-permute-start.1) | collective-permute-done | bytes 524320 | tf_op jit(solution)/shard_map/ppermute | solution.py:284
  50.2 2.1 collective-permute-start.8
  53.4 7.9 %collective-permute-done.2.refs_3_ = bf16[128,2048]{1,0:T(8,128)(2,1)} collective-permute-done((bf16[128,2048]{1,0:T(8,128)(2,1)S(1)}, bf16[128,2048]{1,0:T(8,128)(2,1)}, u32[]{:S(2)}, u32[]{:S(2)}) %collective-permute-start.2) | collective-permute-done | bytes 524320 | tf_op jit(solution)/shard_map/ppermute | solution.py:284
  63.1 2.5 %collective-permute-start.9 = (bf16[128,2048]{1,0:T(8,128)(2,1)S(1)}, bf16[128,2048]{1,0:T(8,128)(2,1)}, u32[]{:S(2)}, u32[]{:S(2)}) collective-permute-start(bf16[128,2048]{1,0:T(8,128)(2,1)S(1)} %collective-permute-done.1.refs_2_), channel_id=1, source_target_pairs={{0,1},{1,0},{2,3},{3,2},{4,5},{5,4},{6,7},{7,6},{8,9},{9,8},{10,11... | collective-permute-start | bytes 1572872 | tf_op jit(solution)/shard_map/ppermute | solution.py:261
  66.9 7.2 %collective-permute-done.3.refs_4_ = bf16[128,2048]{1,0:T(8,128)(2,1)} collective-permute-done((bf16[128,2048]{1,0:T(8,128)(2,1)}, bf16[128,2048]{1,0:T(8,128)(2,1)}, u32[]{:S(2)}, u32[]{:S(2)}) %collective-permute-start.3) | collective-permute-done | bytes 524320 | tf_op jit(solution)/shard_map/ppermute | solution.py:284
  74.1 3.1 %collective-permute-start.11 = (bf16[128,2048]{1,0:T(8,128)(2,1)}, bf16[128,2048]{1,0:T(8,128)(2,1)}, u32[]{:S(2)}, u32[]{:S(2)}) collective-permute-start(bf16[128,2048]{1,0:T(8,128)(2,1)} %collective-permute-done.3.refs_4_), channel_id=1, source_target_pairs={{0,1},{1,0},{2,3},{3,2},{4,5},{5,4},{6,7},{7,6},{8,9},{9,8},{10,11... | collective-permute-start | bytes 1572872 | tf_op jit(solution)/shard_map/ppermute | solution.py:261
  77.9 6.8 %all-to-all-start.1 = ((f32[16,8,128]{2,1,0:T(8,128)}), f32[16,8,128]{2,1,0:T(8,128)S(1)}, u32[]{:S(2)}, u32[]{:S(2)}) async-start(f32[16,8,128]{2,1,0:T(8,128)} %broadcast_in_dim_broadcast_in_dim_broadcast_in_dim.2), calls=%async_computation.1 | async-start | bytes 131072 | tf_op jit(solution)/shard_map/all_to_all | solution.py:266
  85.4 6.5 %all-to-all-done.1 = f32[16,8,128]{2,1,0:T(8,128)S(1)} async-done(((f32[16,8,128]{2,1,0:T(8,128)}), f32[16,8,128]{2,1,0:T(8,128)S(1)}, u32[]{:S(2)}, u32[]{:S(2)}) %all-to-all-start.1) | async-done | bytes 65568 | tf_op jit(solution)/shard_map/all_to_all | solution.py:266
  91.9 1.9 reshape_squeeze.4.refs_18_
  95.6 12.2 %weights.1 = (bf16[64,512,128]{2,1,0:T(8,128)(2,1)}, f32[8,256,128]{2,1,0:T(8,128)}, bf16[8,256,128]{2,1,0:T(8,128)(2,1)S(1)}, f32[8,128]{1,0:T(8,128)S(1)}, f32[8,128]{1,0:T(8,128)S(1)}) custom-call(s32[72]{0:T(128)S(1)} %select_reduce_fusion.pairs, s32[4]{0:T(128)S(1)} %pad_add_fusion.meta, s32[5]{0:T(128)S(1)} %and_select_fusion.starts, ...), custom_call_target="tpu_custom_call" | custom-call | flops 4294967296 | bytes 16777216 | tf_op jit(solution)/shard_map/weights/pallas_call | solution.py:173
  111.4 27.0 %all_to_all.35 = bf16[8,272,128]{2,1,0:T(8,128)(2,1)S(1)} all-to-all(bf16[8,272,128]{2,1,0:T(8,128)(2,1)S(1)} %maximum_maximum_fusion), channel_id=1, replica_groups=mesh['y'=4,'xh'=2,'z'=8,'xl'=2,'core'=2] {'z'}, dimensions={0} | all-to-all | bytes 1114112 | tf_op jit(solution)/shard_map/all_to_all | solution.py:349
  139.7 5.2 %all-to-all-start.3 = ((bf16[16,256,128]{2,1,0:T(8,128)(2,1)}), bf16[16,256,128]{2,1,0:T(8,128)(2,1)S(1)}, u32[]{:S(2)}, u32[]{:S(2)}) async-start(bf16[16,256,128]{2,1,0:T(8,128)(2,1)} %broadcast_in_dim.119), calls=%async_computation.3 | async-start | bytes 2097152 | tf_op jit(solution)/shard_map/all_to_all | solution.py:266
  145.1 14.1 %all-to-all-done.3.pieces = bf16[16,256,128]{2,1,0:T(8,128)(2,1)S(1)} async-done(((bf16[16,256,128]{2,1,0:T(8,128)(2,1)}), bf16[16,256,128]{2,1,0:T(8,128)(2,1)S(1)}, u32[]{:S(2)}, u32[]{:S(2)}) %all-to-all-start.3) | async-done | bytes 1048608 | tf_op jit(solution)/shard_map/all_to_all | solution.py:266
  159.2 3.9 %spread.2 = (f32[8,256,128]{2,1,0:T(8,128)S(1)}, bf16[8,256,128]{2,1,0:T(8,128)(2,1)S(1)}) custom-call(s32[64]{0:T(128)S(1)} %select_reduce_fusion.1.ids, s32[4]{0:T(128)S(1)} %pad_add_fusion.meta, bf16[64,512,128]{2,1,0:T(8,128)(2,1)} %get-tuple-element.20.weights, bf16[16,256,128]{2,1,0:T(8,128)(2,1)S(1)} %all-to-all-done.3.pieces), custom_call_target="tpu_custom_call" | custom-call | tf_op jit(solution)/shard_map/spread/pallas_call | solution.py:241
  163.1 2.3 collective-permute-start.17
  167.1 20.4 %all_to_all.36 = bf16[8,256,128]{2,1,0:T(8,128)(2,1)S(1)} all-to-all(bf16[8,256,128]{2,1,0:T(8,128)(2,1)S(1)} %add_convert_fusion.1), channel_id=1, replica_groups=mesh['y'=4,'xh'=2,'z'=8,'xl'=2,'core'=2] {'z'}, dimensions={0} | all-to-all | bytes 1048576 | tf_op jit(solution)/shard_map/all_to_all | solution.py:349
  187.8 19.8 %all_to_all.37.pieces = bf16[16,256,128]{2,1,0:T(8,128)(2,1)S(1)} all-to-all(bf16[16,256,128]{2,1,0:T(8,128)(2,1)S(1)} %broadcast_in_dim.120), channel_id=1, replica_groups=mesh['y'=4,'xh'=2,'z'=8,'xl'=2,'core'=2] {'xl','y','xh'}, dimensions={0} | all-to-all | bytes 2097152 | tf_op jit(solution)/shard_map/all_to_all | solution.py:266
  207.6 3.9 %spread.3 = (f32[8,256,128]{2,1,0:T(8,128)S(1)}, bf16[8,256,128]{2,1,0:T(8,128)(2,1)S(1)}) custom-call(s32[64]{0:T(128)S(1)} %select_reduce_fusion.1.ids, s32[4]{0:T(128)S(1)} %pad_add_fusion.meta, bf16[64,512,128]{2,1,0:T(8,128)(2,1)} %get-tuple-element.20.weights, bf16[16,256,128]{2,1,0:T(8,128)(2,1)S(1)} %all_to_all.37.pieces), custom_call_target="tpu_custom_call" | custom-call | tf_op jit(solution)/shard_map/spread/pallas_call | solution.py:241
  215.0 20.4 %all_to_all.38 = bf16[8,256,128]{2,1,0:T(8,128)(2,1)S(1)} all-to-all(bf16[8,256,128]{2,1,0:T(8,128)(2,1)S(1)} %add_convert_fusion), channel_id=1, replica_groups=mesh['y'=4,'xh'=2,'z'=8,'xl'=2,'core'=2] {'z'}, dimensions={0} | all-to-all | bytes 1048576 | tf_op jit(solution)/shard_map/all_to_all | solution.py:349
  (103 shorter events, 27.9 us)
Async XLA Ops:
  6.5 11.3 %copy-start.1 = (s32[2,24]{1,0:T(2,128)S(1)}, s32[2,24]{1,0:T(2,128)}, u32[]{:S(2)}) copy-start(s32[2,24]{1,0:T(2,128)} %param.8) | copy-start | bytes 580
  6.5 89.0 %all-gather.2.cloned.1.call-start = ((), (), s32[]{:S(2)}) async-start(), calls=%async_computation.7 | async-start | bytes 10027008 | tf_op jit(solution)/shard_map/all_gather | solution.py:279
  10.2 23.2 %collective-permute-start = (bf16[128,2048]{1,0:T(8,128)(2,1)S(1)}, bf16[128,2048]{1,0:T(8,128)(2,1)S(1)}, u32[]{:S(2)}, u32[]{:S(2)}) collective-permute-start(bf16[128,2048]{1,0:T(8,128)(2,1)S(1)} %copy-done), channel_id=1, source_target_pairs={{0,4},{4,8},{8,12},{12,16},{16,20},{20,24},{24,28},{28,0},{1,5},{5... | collective-permute-start | bytes 1572872 | tf_op jit(solution)/shard_map/ppermute | solution.py:284
  12.7 23.9 %collective-permute-start.4 = (bf16[128,2048]{1,0:T(8,128)(2,1)S(1)}, bf16[128,2048]{1,0:T(8,128)(2,1)S(1)}, u32[]{:S(2)}, u32[]{:S(2)}) collective-permute-start(bf16[128,2048]{1,0:T(8,128)(2,1)S(1)} %copy-done), channel_id=1, source_target_pairs={{0,28},{4,0},{8,4},{12,8},{16,12},{20,16},{24,20},{28,24},{1,29},{... | collective-permute-start | bytes 1572872 | tf_op jit(solution)/shard_map/ppermute | solution.py:287
  16.8 46.3 %collective-permute-start.7 = (bf16[128,2048]{1,0:T(8,128)(2,1)S(1)}, bf16[128,2048]{1,0:T(8,128)(2,1)S(1)}, u32[]{:S(2)}, u32[]{:S(2)}) collective-permute-start(bf16[128,2048]{1,0:T(8,128)(2,1)S(1)} %copy-done), channel_id=1, source_target_pairs={{0,1},{1,0},{2,3},{3,2},{4,5},{5,4},{6,7},{7,6},{8,9},{9,8},{10,11... | collective-permute-start | bytes 1572872 | tf_op jit(solution)/shard_map/ppermute | solution.py:261
  18.9 13.9 %all-to-all-start = ((f32[16,8,256]{2,1,0:T(8,128)}), f32[16,8,256]{2,1,0:T(8,128)S(1)}, u32[]{:S(2)}, u32[]{:S(2)}) async-start(f32[16,8,256]{2,1,0:T(8,128)} %broadcast_in_dim.64), calls=%async_computation | async-start | bytes 262144 | tf_op jit(solution)/shard_map/all_to_all | solution.py:295
  33.4 14.4 %collective-permute-start.1 = (bf16[128,2048]{1,0:T(8,128)(2,1)S(1)}, bf16[128,2048]{1,0:T(8,128)(2,1)S(1)}, u32[]{:S(2)}, u32[]{:S(2)}) collective-permute-start(bf16[128,2048]{1,0:T(8,128)(2,1)S(1)} %collective-permute-done.refs_1_), channel_id=1, source_target_pairs={{0,4},{4,8},{8,12},{12,16},{16,20},{20,24},{24,28},{28,0},{1,5},{5... | collective-permute-start | bytes 1572872 | tf_op jit(solution)/shard_map/ppermute | solution.py:284
  36.7 15.8 %collective-permute-start.5 = (bf16[128,2048]{1,0:T(8,128)(2,1)S(1)}, bf16[128,2048]{1,0:T(8,128)(2,1)S(1)}, u32[]{:S(2)}, u32[]{:S(2)}) collective-permute-start(bf16[128,2048]{1,0:T(8,128)(2,1)S(1)} %collective-permute-done.4.refs_7_), channel_id=1, source_target_pairs={{0,28},{4,0},{8,4},{12,8},{16,12},{20,16},{24,20},{28,24},{1,29},{... | collective-permute-start | bytes 1572872 | tf_op jit(solution)/shard_map/ppermute | solution.py:287
  47.8 13.5 %collective-permute-start.2 = (bf16[128,2048]{1,0:T(8,128)(2,1)S(1)}, bf16[128,2048]{1,0:T(8,128)(2,1)}, u32[]{:S(2)}, u32[]{:S(2)}) collective-permute-start(bf16[128,2048]{1,0:T(8,128)(2,1)S(1)} %collective-permute-done.1.refs_2_), channel_id=1, source_target_pairs={{0,4},{4,8},{8,12},{12,16},{16,20},{20,24},{24,28},{28,0},{1,5},{5... | collective-permute-start | bytes 1572872 | tf_op jit(solution)/shard_map/ppermute | solution.py:284
  50.2 15.4 %collective-permute-start.8 = (bf16[128,2048]{1,0:T(8,128)(2,1)S(1)}, bf16[128,2048]{1,0:T(8,128)(2,1)}, u32[]{:S(2)}, u32[]{:S(2)}) collective-permute-start(bf16[128,2048]{1,0:T(8,128)(2,1)S(1)} %collective-permute-done.refs_1_), channel_id=1, source_target_pairs={{0,1},{1,0},{2,3},{3,2},{4,5},{5,4},{6,7},{7,6},{8,9},{9,8},{10,11... | collective-permute-start | bytes 1572872 | tf_op jit(solution)/shard_map/ppermute | solution.py:261
  52.3 13.3 %collective-permute-start.14 = (bf16[128,2048]{1,0:T(8,128)(2,1)S(1)}, bf16[128,2048]{1,0:T(8,128)(2,1)}, u32[]{:S(2)}, u32[]{:S(2)}) collective-permute-start(bf16[128,2048]{1,0:T(8,128)(2,1)S(1)} %collective-permute-done.4.refs_7_), channel_id=1, source_target_pairs={{0,1},{1,0},{2,3},{3,2},{4,5},{5,4},{6,7},{7,6},{8,9},{9,8},{10,11... | collective-permute-start | bytes 1572872 | tf_op jit(solution)/shard_map/ppermute | solution.py:261
  52.4 13.6 %collective-permute-start.6 = (bf16[128,2048]{1,0:T(8,128)(2,1)S(1)}, bf16[128,2048]{1,0:T(8,128)(2,1)}, u32[]{:S(2)}, u32[]{:S(2)}) collective-permute-start(bf16[128,2048]{1,0:T(8,128)(2,1)S(1)} %collective-permute-done.5.refs_6_), channel_id=1, source_target_pairs={{0,28},{4,0},{8,4},{12,8},{16,12},{20,16},{24,20},{28,24},{1,29},{... | collective-permute-start | bytes 1572872 | tf_op jit(solution)/shard_map/ppermute | solution.py:287
  61.3 12.8 %collective-permute-start.3 = (bf16[128,2048]{1,0:T(8,128)(2,1)}, bf16[128,2048]{1,0:T(8,128)(2,1)}, u32[]{:S(2)}, u32[]{:S(2)}) collective-permute-start(bf16[128,2048]{1,0:T(8,128)(2,1)} %collective-permute-done.2.refs_3_), channel_id=1, source_target_pairs={{0,4},{4,8},{8,12},{12,16},{16,20},{20,24},{24,28},{28,0},{1,5},{5... | collective-permute-start | bytes 1572872 | tf_op jit(solution)/shard_map/ppermute | solution.py:284
  63.1 30.7 %collective-permute-start.9 = (bf16[128,2048]{1,0:T(8,128)(2,1)S(1)}, bf16[128,2048]{1,0:T(8,128)(2,1)}, u32[]{:S(2)}, u32[]{:S(2)}) collective-permute-start(bf16[128,2048]{1,0:T(8,128)(2,1)S(1)} %collective-permute-done.1.refs_2_), channel_id=1, source_target_pairs={{0,1},{1,0},{2,3},{3,2},{4,5},{5,4},{6,7},{7,6},{8,9},{9,8},{10,11... | collective-permute-start | bytes 1572872 | tf_op jit(solution)/shard_map/ppermute | solution.py:261
  65.6 28.3 %collective-permute-start.13 = (bf16[128,2048]{1,0:T(8,128)(2,1)S(1)}, bf16[128,2048]{1,0:T(8,128)(2,1)}, u32[]{:S(2)}, u32[]{:S(2)}) collective-permute-start(bf16[128,2048]{1,0:T(8,128)(2,1)S(1)} %collective-permute-done.5.refs_6_), channel_id=1, source_target_pairs={{0,1},{1,0},{2,3},{3,2},{4,5},{5,4},{6,7},{7,6},{8,9},{9,8},{10,11... | collective-permute-start | bytes 1572872 | tf_op jit(solution)/shard_map/ppermute | solution.py:261
  65.7 28.2 %collective-permute-start.10 = (bf16[128,2048]{1,0:T(8,128)(2,1)}, bf16[128,2048]{1,0:T(8,128)(2,1)}, u32[]{:S(2)}, u32[]{:S(2)}) collective-permute-start(bf16[128,2048]{1,0:T(8,128)(2,1)} %collective-permute-done.2.refs_3_), channel_id=1, source_target_pairs={{0,1},{1,0},{2,3},{3,2},{4,5},{5,4},{6,7},{7,6},{8,9},{9,8},{10,11... | collective-permute-start | bytes 1572872 | tf_op jit(solution)/shard_map/ppermute | solution.py:261
  66.1 27.8 %collective-permute-start.12 = (bf16[128,2048]{1,0:T(8,128)(2,1)}, bf16[128,2048]{1,0:T(8,128)(2,1)}, u32[]{:S(2)}, u32[]{:S(2)}) collective-permute-start(bf16[128,2048]{1,0:T(8,128)(2,1)} %collective-permute-done.6.refs_5_), channel_id=1, source_target_pairs={{0,1},{1,0},{2,3},{3,2},{4,5},{5,4},{6,7},{7,6},{8,9},{9,8},{10,11... | collective-permute-start | bytes 1572872 | tf_op jit(solution)/shard_map/ppermute | solution.py:261
  74.1 19.8 %collective-permute-start.11 = (bf16[128,2048]{1,0:T(8,128)(2,1)}, bf16[128,2048]{1,0:T(8,128)(2,1)}, u32[]{:S(2)}, u32[]{:S(2)}) collective-permute-start(bf16[128,2048]{1,0:T(8,128)(2,1)} %collective-permute-done.3.refs_4_), channel_id=1, source_target_pairs={{0,1},{1,0},{2,3},{3,2},{4,5},{5,4},{6,7},{7,6},{8,9},{9,8},{10,11... | collective-permute-start | bytes 1572872 | tf_op jit(solution)/shard_map/ppermute | solution.py:261
  77.9 14.0 %all-to-all-start.1 = ((f32[16,8,128]{2,1,0:T(8,128)}), f32[16,8,128]{2,1,0:T(8,128)S(1)}, u32[]{:S(2)}, u32[]{:S(2)}) async-start(f32[16,8,128]{2,1,0:T(8,128)} %broadcast_in_dim_broadcast_in_dim_broadcast_in_dim.2), calls=%async_computation.1 | async-start | bytes 131072 | tf_op jit(solution)/shard_map/all_to_all | solution.py:266
  107.8 2.0 collective-permute-start.15
  107.9 1.9 collective-permute-start.16
  139.7 19.5 %all-to-all-start.3 = ((bf16[16,256,128]{2,1,0:T(8,128)(2,1)}), bf16[16,256,128]{2,1,0:T(8,128)(2,1)S(1)}, u32[]{:S(2)}, u32[]{:S(2)}) async-start(bf16[16,256,128]{2,1,0:T(8,128)(2,1)} %broadcast_in_dim.119), calls=%async_computation.3 | async-start | bytes 2097152 | tf_op jit(solution)/shard_map/all_to_all | solution.py:266
  163.1 3.8 %collective-permute-start.17 = (bf16[8,256,128]{2,1,0:T(8,128)(2,1)S(1)}, bf16[8,256,128]{2,1,0:T(8,128)(2,1)S(1)}, u32[]{:S(2)}, u32[]{:S(2)}) collective-permute-start(bf16[8,256,128]{2,1,0:T(8,128)(2,1)S(1)} %get-tuple-element.26), channel_id=1, source_target_pairs={{0,1},{1,0},{2,3},{3,2},{4,5},{5,4},{6,7},{7,6},{8,9},{9,8},{10,11... | collective-permute-start | bytes 1572872 | tf_op jit(solution)/shard_map/ppermute | solution.py:261
  211.5 3.4 %collective-permute-start.18 = (bf16[8,256,128]{2,1,0:T(8,128)(2,1)S(1)}, bf16[8,256,128]{2,1,0:T(8,128)(2,1)S(1)}, u32[]{:S(2)}, u32[]{:S(2)}) collective-permute-start(bf16[8,256,128]{2,1,0:T(8,128)(2,1)S(1)} %get-tuple-element.28), channel_id=1, source_target_pairs={{0,1},{1,0},{2,3},{3,2},{4,5},{5,4},{6,7},{7,6},{8,9},{9,8},{10,11... | collective-permute-start | bytes 1572872 | tf_op jit(solution)/shard_map/ppermute | solution.py:261
  (2 other events, 14.8 us)
Sparse Core Ops, SparseCore 0:
  10.3 85.2 all-gather.1

commit v6 on v5

--- a/solution.py
+++ b/solution.py
@@ -204,57 +204,94 @@
     )(pairs, meta, starts, *rows, cols, row_sq, col_sq)
 
 
-def spread_kernel(ids, meta, weights, pieces, keep, send, labels, total, tile_buf, tile_sem):
-    live = meta[0]
-
-    def tile_copy(t):
+def spread_kernel(pairs, meta, starts, weights, *refs):
+    shifted = refs[:4]
+    keep, send, labels, total, tile_buf, tile_sem = refs[4:]
+    live = starts[BLOCKS]
+    z = meta[3]
+    half = ROWS // 2
+
+    def tile_copy(q, side):
         return pltpu.make_async_copy(
-            weights.at[ids[t]], tile_buf.at[ids[t]], tile_sem.at[ids[t]]
+            weights.at[pairs[2 * q + side]],
+            tile_buf.at[q, :, pl.ds(side * PIECE, PIECE)],
+            tile_sem.at[q, side],
         )
 
-    def begin(t, carry):
-        tile_copy(t).start()
+    def begin(q, carry):
+        tile_copy(q, 0).start()
+
+        @pl.when(pairs[2 * q] != pairs[2 * q + 1])
+        def _():
+            tile_copy(q, 1).start()
+
         return carry
 
     lax.fori_loop(0, live, begin, 0)
     total[...] = jnp.zeros_like(total)
-    for j in range(BLOCKS):
-        for sub in range(WIDTH // PIECE):
-            labels[j, :, sub * PIECE:(sub + 1) * PIECE] = pieces[j * (WIDTH // PIECE) + sub]
-
-    def tile(t, carry):
-        tile_copy(t).wait()
-        total[lax.rem(ids[t], ROWS)] += jnp.dot(
-            labels[ids[t] // ROWS], tile_buf[ids[t]], preferred_element_type=jnp.float32
+    for down in range(4):
+        from_y = lax.rem(meta[4] - down + 4, 4)
+        for right in range(4):
+            from_x = lax.rem(meta[5] - right + 4, 4)
+            block = lax.rem(from_x, 2) * 2 + from_y // 2
+            sub = lax.rem(from_y, 2) * 2 + from_x // 2
+            labels[block, sub] = shifted[down][right]
+
+    def add(tile_id, value):
+        a = lax.rem(tile_id, ROWS)
+        side = a // half
+        place = side * half + lax.rem(z - lax.rem(a, half) + half, half)
+        total[place] += value
+
+    def pair(q, carry):
+        one = pairs[2 * q]
+        two = pairs[2 * q + 1]
+        tile_copy(q, 0).wait()
+
+        @pl.when(one != two)
+        def _():
+            tile_copy(q, 1).wait()
+
+        j = one // ROWS
+        spread = jnp.dot(
+            jnp.concatenate([labels[j, sub] for sub in range(WIDTH // PIECE)], axis=1),
+            tile_buf[q], preferred_element_type=jnp.float32,
         )
+        add(one, spread[:, :PIECE])
+
+        @pl.when(one != two)
+        def _():
+            add(two, spread[:, PIECE:])
+
         return carry
 
-    lax.fori_loop(0, live, tile, 0)
-    split_rows(meta[3], total, keep, send)
-
-
-def spread_rows(ids, meta, weights, pieces):
+    lax.fori_loop(0, live, pair, 0)
+    keep[...] = total[:half]
+    send[...] = total[half:].astype(jnp.bfloat16)
+
+
+def spread_rows(pairs, meta, starts, weights, shifted):
     smem = pl.BlockSpec(memory_space=pltpu.SMEM)
     vmem = pl.BlockSpec(memory_space=pltpu.VMEM)
     hbm = pl.BlockSpec(memory_space=pl.ANY)
-    tasks = pieces.shape[1]
+    tasks = shifted[0].shape[1]
     return pl.pallas_call(
         spread_kernel,
         out_shape=(
             jax.ShapeDtypeStruct((ROWS // 2, tasks, PIECE), jnp.float32),
             jax.ShapeDtypeStruct((ROWS // 2, tasks, PIECE), jnp.bfloat16),
         ),
-        in_specs=[smem, smem, hbm, vmem],
+        in_specs=[smem, smem, smem, hbm] + [vmem] * 4,
         out_specs=(vmem, vmem),
         scratch_shapes=[
-            pltpu.VMEM((BLOCKS, tasks, WIDTH), jnp.bfloat16),
+            pltpu.VMEM((BLOCKS, WIDTH // PIECE, tasks, PIECE), jnp.bfloat16),
             pltpu.VMEM((ROWS, tasks, PIECE), jnp.float32),
-            pltpu.VMEM((TILES, WIDTH, PIECE), jnp.bfloat16),
-            pltpu.SemaphoreType.DMA((TILES,)),
+            pltpu.VMEM((TILES // 2, WIDTH, 2 * PIECE), jnp.bfloat16),
+            pltpu.SemaphoreType.DMA((TILES // 2, 2)),
         ],
         compiler_params=pltpu.CompilerParams(vmem_limit_bytes=VMEM_LIMIT),
         name="spread",
-    )(ids, meta, weights, pieces)
+    )(pairs, meta, starts, weights, *shifted)
 
 
 def swap_cores(value):
@@ -264,6 +301,20 @@
 def gather_pieces(piece):
     copies = jnp.broadcast_to(piece[None], (ROWS,) + piece.shape)
     return lax.all_to_all(copies, PLANE, 0, 0)
+
+
+def shift_plane(value, down, right):
+    moves = [
+        (y * 4 + x, (y + down) % 4 * 4 + (x + right) % 4) for y in range(4) for x in range(4)
+    ]
+    return lax.ppermute(value, ("y", "xh", "xl"), moves)
+
+
+def gather_shifted(labels):
+    one, three, two = [shift_plane(labels, 0, right) for right in (1, 3, 2)]
+    line = jnp.stack([labels, one, two, three])
+    one, three, two = [shift_plane(line, down, 0) for down in (1, 3, 2)]
+    return [line, one, two, three]
 
 
 def body(fingerprints, activity, label_mask, pattern, counts):
@@ -312,10 +363,6 @@
     flat = live.reshape(TILES).astype(jnp.int32)
     order = jnp.arange(TILES, dtype=jnp.int32)
     before = jnp.sum(jnp.where(order[None, :] < order[:, None], flat[None, :], 0), axis=1)
-    ids = jnp.sum(
-        jnp.where((before[None, :] == order[:, None]) & (flat[None, :] > 0), order[None, :], 0),
-        axis=1,
-    ).astype(jnp.int32)
     counted = jnp.sum(live.astype(jnp.int32), axis=1)
     even = counted + counted % 2
     block_start = jnp.sum(jnp.where(j[None, :] < j[:, None], even[None, :], 0), axis=1)
@@ -329,7 +376,7 @@
     starts = (jnp.concatenate([block_start, jnp.sum(even)[None]]) // 2).astype(jnp.int32)
     own_tile = (xl * 2 + y // 2) * ROWS
     own_offset = ((y % 2) * 2 + xh) * PIECE
-    meta = jnp.stack([jnp.sum(flat), own_offset, own_tile, z]).astype(jnp.int32)
+    meta = jnp.stack([jnp.sum(flat), own_offset, own_tile, z, y, xh * 2 + xl]).astype(jnp.int32)
 
     weights, keep, send, degree_keep, degree_send = build_weights(
         pairs, meta, starts, rows, cols, row_sq, col_sq
@@ -342,7 +389,7 @@
 
     for iteration in range(ITERS):
         if iteration > 0:
-            keep, send = spread_rows(ids, meta, weights, gathered)
+            keep, send = spread_rows(pairs, meta, starts, weights, gathered)
         part = (keep + swap_cores(send).astype(jnp.float32)).astype(jnp.bfloat16)
         if iteration == 0:
             part = jnp.concatenate([part, degree_rows], axis=1)
@@ -353,7 +400,7 @@
             summed = summed[:tasks]
         labels = (PROPAGATE * summed / degree_own[None, :] + ANCHOR * seeded).astype(jnp.bfloat16)
         if iteration < ITERS - 1:
-            gathered = gather_pieces(labels)
+            gathered = gather_shifted(labels)
     return labels.T
 
 

time: 245 us -> 245 us (level)
  blocking collectives: 87.6 us -> 69.8 us
  waiting for transfers between devices: 60.8 us -> 74 us
  starting transfers between devices: 44.4 us -> 54.4 us
    ppermute x0 -> x12, waiting for transfers between devices: none -> 27.7 us  [shift_plane(): return lax.ppermute(value, ('y', 'xh', 'xl'), moves)]
    all_to_all x1 -> x0, blocking collectives: 19.8 us -> none  [gather_pieces(): return lax.all_to_all(copies, PLANE, 0, 0)]
    ppermute x0 -> x12, starting transfers between devices: none -> 16.4 us  [shift_plane(): return lax.ppermute(value, ('y', 'xh', 'xl'), moves)]
    all_to_all x2 -> x1, waiting for transfers between devices: 20.6 us -> 6.49 us  [gather_pieces(): return lax.all_to_all(copies, PLANE, 0, 0)]
    ppermute x4, waiting for transfers between devices: 26.2 us -> 19.9 us  [body(): lax.ppermute(upward[-1], 'z', [(i, (i + 1) % 8) for i in range(8)])]
    all_gather x1, waiting for transfers between devices: 1.7 us -> 7.94 us  [body(): cols = lax.all_gather(extended, ('y', 'xh', 'xl'), axis=0, tiled=True)]
    all_to_all x2 -> x1, starting transfers between devices: 12 us -> 6.56 us  [gather_pieces(): return lax.all_to_all(copies, PLANE, 0, 0)]
    ppermute x4, starting transfers between devices: 6.69 us -> 2.55 us  [body(): lax.ppermute(upward[-1], 'z', [(i, (i + 1) % 8) for i in range(8)])]
  transfers between devices with their start and end apart: 23 -> 34, of which waited for: 10 -> 22; matrix products, arithmetic and copies ran while one was open for 4% -> 4% of each run, Pallas kernels for 0% -> 0%
where the time goes in v6:
time: 245 us
  waiting for transfers between devices  74 us (30%)
  blocking collectives  69.8 us (28%)
  starting transfers between devices  54.4 us (22%)
  Pallas kernels  18 us (7%)
  between operations  13.7 us (6%)
  other arithmetic  8.15 us (3%)
  local copies, waits for them, and re-layouts  7.12 us (3%)
    all_to_all x3, blocking collectives, body(): parts = lax.all_to_all(part, 'z', 0, 0)  69.8 us
    ppermute x12, waiting for transfers between devices, shift_plane(): return lax.ppermute(value, ('y', 'xh', 'xl'), moves)  27.7 us
    ppermute x4, waiting for transfers between devices, body(): lax.ppermute(upward[-1], 'z', [(i, (i + 1) % 8) for i in range(8)])  19.9 us
    ppermute x12, starting transfers between devices, shift_plane(): return lax.ppermute(value, ('y', 'xh', 'xl'), moves)  16.4 us
    ppermute x12, starting transfers between devices, swap_cores(): return lax.ppermute(value, 'core', [(0, 1), (1, 0)])  15 us
    pallas_call x1, Pallas kernels, build_weights(): pl.pallas_call(weights_kernel, out_shape=(jax.ShapeDtypeStruct((TILES, WI...  11.7 us
    ppermute x3, starting transfers between devices, body(): lax.ppermute(downward[-1], 'z', [(i, (i + 7) % 8) for i in range(8)])  8.03 us
    all_gather x1, waiting for transfers between devices, body(): cols = lax.all_gather(extended, ('y', 'xh', 'xl'), axis=0, tiled=True)  7.94 us
  transfers between devices with their start and end apart: 34, of which 22 were waited for; matrix products, arithmetic and copies ran while one was open for 4% of the time, Pallas kernels for 0%

profile of v6, /device:TPU:1, one launch (start us, length us, event | category | flops | bytes accessed | tf_op | source)
XLA Modules:
  0.0 245.1 jit_solution(17413966181015009324)
XLA Ops:
  12.8 4.0 %collective-permute-start.4 = (bf16[128,2048]{1,0:T(8,128)(2,1)S(1)}, bf16[128,2048]{1,0:T(8,128)(2,1)S(1)}, u32[]{:S(2)}, u32[]{:S(2)}) collective-permute-start(bf16[128,2048]{1,0:T(8,128)(2,1)S(1)} %copy-done), channel_id=1, source_target_pairs={{0,28},{4,0},{8,4},{12,8},{16,12},{20,16},{24,20},{28,24},{1,29},{... | collective-permute-start | bytes 1572872 | tf_op jit(solution)/shard_map/ppermute | solution.py:338
  18.9 5.9 %all-to-all-start = ((f32[16,8,256]{2,1,0:T(8,128)}), f32[16,8,256]{2,1,0:T(8,128)S(1)}, u32[]{:S(2)}, u32[]{:S(2)}) async-start(f32[16,8,256]{2,1,0:T(8,128)} %broadcast_in_dim.88), calls=%async_computation | async-start | bytes 262144 | tf_op jit(solution)/shard_map/all_to_all | solution.py:346
  24.9 3.5 %collective-permute-done.refs_1_ = bf16[128,2048]{1,0:T(8,128)(2,1)S(1)} collective-permute-done((bf16[128,2048]{1,0:T(8,128)(2,1)S(1)}, bf16[128,2048]{1,0:T(8,128)(2,1)S(1)}, u32[]{:S(2)}, u32[]{:S(2)}) %collective-permute-start) | collective-permute-done | bytes 524320 | tf_op jit(solution)/shard_map/ppermute | solution.py:335
  28.4 4.9 %all-to-all-done = f32[16,8,256]{2,1,0:T(8,128)S(1)} async-done(((f32[16,8,256]{2,1,0:T(8,128)}), f32[16,8,256]{2,1,0:T(8,128)S(1)}, u32[]{:S(2)}, u32[]{:S(2)}) %all-to-all-start) | async-done | bytes 131104 | tf_op jit(solution)/shard_map/all_to_all | solution.py:346
  35.8 6.7 %collective-permute-done.1.refs_2_ = bf16[128,2048]{1,0:T(8,128)(2,1)S(1)} collective-permute-done((bf16[128,2048]{1,0:T(8,128)(2,1)S(1)}, bf16[128,2048]{1,0:T(8,128)(2,1)S(1)}, u32[]{:S(2)}, u32[]{:S(2)}) %collective-permute-start.1) | collective-permute-done | bytes 524320 | tf_op jit(solution)/shard_map/ppermute | solution.py:335
  50.4 4.9 %collective-permute-done.2.refs_3_ = bf16[128,2048]{1,0:T(8,128)(2,1)} collective-permute-done((bf16[128,2048]{1,0:T(8,128)(2,1)S(1)}, bf16[128,2048]{1,0:T(8,128)(2,1)}, u32[]{:S(2)}, u32[]{:S(2)}) %collective-permute-start.2) | collective-permute-done | bytes 524320 | tf_op jit(solution)/shard_map/ppermute | solution.py:335
  57.4 2.9 %collective-permute-start.13 = (bf16[128,2048]{1,0:T(8,128)(2,1)S(1)}, bf16[128,2048]{1,0:T(8,128)(2,1)}, u32[]{:S(2)}, u32[]{:S(2)}) collective-permute-start(bf16[128,2048]{1,0:T(8,128)(2,1)S(1)} %collective-permute-done.5.refs_6_), channel_id=1, source_target_pairs={{0,1},{1,0},{2,3},{3,2},{4,5},{5,4},{6,7},{7,6},{8,9},{9,8},{10,11... | collective-permute-start | bytes 1572872 | tf_op jit(solution)/shard_map/ppermute | solution.py:298
  62.6 4.9 %collective-permute-done.3.refs_4_ = bf16[128,2048]{1,0:T(8,128)(2,1)} collective-permute-done((bf16[128,2048]{1,0:T(8,128)(2,1)}, bf16[128,2048]{1,0:T(8,128)(2,1)}, u32[]{:S(2)}, u32[]{:S(2)}) %collective-permute-start.3) | collective-permute-done | bytes 524320 | tf_op jit(solution)/shard_map/ppermute | solution.py:335
  67.5 3.7 %collective-permute-start.11 = (bf16[128,2048]{1,0:T(8,128)(2,1)}, bf16[128,2048]{1,0:T(8,128)(2,1)}, u32[]{:S(2)}, u32[]{:S(2)}) collective-permute-start(bf16[128,2048]{1,0:T(8,128)(2,1)} %collective-permute-done.3.refs_4_), channel_id=1, source_target_pairs={{0,1},{1,0},{2,3},{3,2},{4,5},{5,4},{6,7},{7,6},{8,9},{9,8},{10,11... | collective-permute-start | bytes 1572872 | tf_op jit(solution)/shard_map/ppermute | solution.py:298
  71.9 6.6 %all-to-all-start.1 = ((f32[16,8,128]{2,1,0:T(8,128)}), f32[16,8,128]{2,1,0:T(8,128)S(1)}, u32[]{:S(2)}, u32[]{:S(2)}) async-start(f32[16,8,128]{2,1,0:T(8,128)} %broadcast_in_dim_broadcast_in_dim_broadcast_in_dim.2), calls=%async_computation.1 | async-start | bytes 131072 | tf_op jit(solution)/shard_map/all_to_all | solution.py:303
  79.2 6.5 %all-to-all-done.1 = f32[16,8,128]{2,1,0:T(8,128)S(1)} async-done(((f32[16,8,128]{2,1,0:T(8,128)}), f32[16,8,128]{2,1,0:T(8,128)S(1)}, u32[]{:S(2)}, u32[]{:S(2)}) %all-to-all-start.1) | async-done | bytes 65568 | tf_op jit(solution)/shard_map/all_to_all | solution.py:303
  87.7 7.9 %all-gather.2.cloned.1.call-done = bf16[2304,2048]{1,0:T(8,128)(2,1)} async-done(((bf16[144,2048]{1,0:T(8,128)(2,1)}), bf16[2304,2048]{1,0:T(8,128)(2,1)}) %all-gather.2.cloned.1.call-update) | async-done | bytes 9437200 | tf_op jit(solution)/shard_map/all_gather | solution.py:330
  95.6 11.7 %weights.1 = (bf16[64,512,128]{2,1,0:T(8,128)(2,1)}, f32[8,256,128]{2,1,0:T(8,128)}, bf16[8,256,128]{2,1,0:T(8,128)(2,1)S(1)}, f32[8,128]{1,0:T(8,128)S(1)}, f32[8,128]{1,0:T(8,128)S(1)}) custom-call(s32[72]{0:T(128)S(1)} %select_reduce_fusion.pairs, s32[6]{0:T(128)S(1)} %stack.67.meta, s32[5]{0:T(128)S(1)} %and_select_fusion.starts, ...), custom_call_target="tpu_custom_call" | custom-call | flops 4294967296 | bytes 16777216 | tf_op jit(solution)/shard_map/weights/pallas_call | solution.py:173
  110.9 29.0 %all_to_all.25 = bf16[8,272,128]{2,1,0:T(8,128)(2,1)S(1)} all-to-all(bf16[8,272,128]{2,1,0:T(8,128)(2,1)S(1)} %maximum_maximum_fusion), channel_id=1, replica_groups=mesh['y'=4,'xh'=2,'z'=8,'xl'=2,'core'=2] {'z'}, dimensions={0} | all-to-all | bytes 1114112 | tf_op jit(solution)/shard_map/all_to_all | solution.py:396
  149.7 7.2 %collective-permute-done.20.refs_1_ = bf16[4,256,128]{2,1,0:T(8,128)(2,1)S(1)} collective-permute-done((bf16[4,256,128]{2,1,0:T(8,128)(2,1)S(1)}, bf16[4,256,128]{2,1,0:T(8,128)(2,1)S(1)}, u32[]{:S(2)}, u32[]{:S(2)}) %collective-permute-start.20) | collective-permute-done | bytes 262176 | tf_op jit(solution)/shard_map/ppermute | solution.py:310
  157.5 3.8 %collective-permute-done.22.refs_3_ = bf16[4,256,128]{2,1,0:T(8,128)(2,1)S(1)} collective-permute-done((bf16[4,256,128]{2,1,0:T(8,128)(2,1)S(1)}, bf16[4,256,128]{2,1,0:T(8,128)(2,1)S(1)}, u32[]{:S(2)}, u32[]{:S(2)}) %collective-permute-start.22) | collective-permute-done | bytes 262176 | tf_op jit(solution)/shard_map/ppermute | solution.py:310
  161.3 3.1 %spread.2 = (f32[8,256,128]{2,1,0:T(8,128)S(1)}, bf16[8,256,128]{2,1,0:T(8,128)(2,1)S(1)}) custom-call(s32[72]{0:T(128)S(1)} %select_reduce_fusion.pairs, s32[6]{0:T(128)S(1)} %stack.67.meta, s32[5]{0:T(128)S(1)} %and_select_fusion.starts, bf16[64,512,128]{2,1,0:T(8,128)(2,1)} %get-tuple-element.20.weights, ...), custom_call_target="tpu_custom_call" | custom-call | tf_op jit(solution)/shard_map/spread/pallas_call | solution.py:278
  167.3 20.4 %all_to_all.26 = bf16[8,256,128]{2,1,0:T(8,128)(2,1)S(1)} all-to-all(bf16[8,256,128]{2,1,0:T(8,128)(2,1)S(1)} %add_convert_fusion.1), channel_id=1, replica_groups=mesh['y'=4,'xh'=2,'z'=8,'xl'=2,'core'=2] {'z'}, dimensions={0} | all-to-all | bytes 1048576 | tf_op jit(solution)/shard_map/all_to_all | solution.py:396
  189.0 3.7 %collective-permute-start.25 = (bf16[256,128]{1,0:T(8,128)(2,1)S(1)}, bf16[256,128]{1,0:T(8,128)(2,1)S(1)}, u32[]{:S(2)}, u32[]{:S(2)}) collective-permute-start(bf16[256,128]{1,0:T(8,128)(2,1)S(1)} %fusion.3), channel_id=1, source_target_pairs={{0,32},{2,34},{32,0},{34,2},{64,96},{66,98},{96,64},{98,66},{128,1... | collective-permute-start | bytes 196616 | tf_op jit(solution)/shard_map/ppermute | solution.py:310
  196.2 3.5 %collective-permute-start.28 = (bf16[4,256,128]{2,1,0:T(8,128)(2,1)S(1)}, bf16[4,256,128]{2,1,0:T(8,128)(2,1)S(1)}, u32[]{:S(2)}, u32[]{:S(2)}) collective-permute-start(bf16[4,256,128]{2,1,0:T(8,128)(2,1)S(1)} %pad_maximum_fusion.2.refs_0_), channel_id=1, source_target_pairs={{0,128},{2,130},{32,160},{34,162},{64,192},{66,194},{96,224},{98,2... | collective-permute-start | bytes 786440 | tf_op jit(solution)/shard_map/ppermute | solution.py:310
  199.7 3.6 %collective-permute-done.27.refs_1_ = bf16[4,256,128]{2,1,0:T(8,128)(2,1)S(1)} collective-permute-done((bf16[4,256,128]{2,1,0:T(8,128)(2,1)S(1)}, bf16[4,256,128]{2,1,0:T(8,128)(2,1)S(1)}, u32[]{:S(2)}, u32[]{:S(2)}) %collective-permute-start.27) | collective-permute-done | bytes 262176 | tf_op jit(solution)/shard_map/ppermute | solution.py:310
  203.3 6.5 %collective-permute-done.28.refs_2_ = bf16[4,256,128]{2,1,0:T(8,128)(2,1)S(1)} collective-permute-done((bf16[4,256,128]{2,1,0:T(8,128)(2,1)S(1)}, bf16[4,256,128]{2,1,0:T(8,128)(2,1)S(1)}, u32[]{:S(2)}, u32[]{:S(2)}) %collective-permute-start.28) | collective-permute-done | bytes 262176 | tf_op jit(solution)/shard_map/ppermute | solution.py:310
  210.8 3.1 %spread.3 = (f32[8,256,128]{2,1,0:T(8,128)S(1)}, bf16[8,256,128]{2,1,0:T(8,128)(2,1)S(1)}) custom-call(s32[72]{0:T(128)S(1)} %select_reduce_fusion.pairs, s32[6]{0:T(128)S(1)} %stack.67.meta, s32[5]{0:T(128)S(1)} %and_select_fusion.starts, bf16[64,512,128]{2,1,0:T(8,128)(2,1)} %get-tuple-element.20.weights, ...), custom_call_target="tpu_custom_call" | custom-call | tf_op jit(solution)/shard_map/spread/pallas_call | solution.py:278
  217.1 20.4 %all_to_all.27 = bf16[8,256,128]{2,1,0:T(8,128)(2,1)S(1)} all-to-all(bf16[8,256,128]{2,1,0:T(8,128)(2,1)S(1)} %add_convert_fusion), channel_id=1, replica_groups=mesh['y'=4,'xh'=2,'z'=8,'xl'=2,'core'=2] {'z'}, dimensions={0} | all-to-all | bytes 1048576 | tf_op jit(solution)/shard_map/all_to_all | solution.py:396
  (123 shorter events, 53.1 us)
Async XLA Ops:
  6.5 89.0 %all-gather.2.cloned.1.call-start = ((), (), s32[]{:S(2)}) async-start(), calls=%async_computation.5 | async-start | bytes 10027008 | tf_op jit(solution)/shard_map/all_gather | solution.py:330
  10.2 18.1 %collective-permute-start = (bf16[128,2048]{1,0:T(8,128)(2,1)S(1)}, bf16[128,2048]{1,0:T(8,128)(2,1)S(1)}, u32[]{:S(2)}, u32[]{:S(2)}) collective-permute-start(bf16[128,2048]{1,0:T(8,128)(2,1)S(1)} %copy-done), channel_id=1, source_target_pairs={{0,4},{4,8},{8,12},{12,16},{16,20},{20,24},{24,28},{28,0},{1,5},{5... | collective-permute-start | bytes 1572872 | tf_op jit(solution)/shard_map/ppermute | solution.py:335
  12.8 21.4 %collective-permute-start.4 = (bf16[128,2048]{1,0:T(8,128)(2,1)S(1)}, bf16[128,2048]{1,0:T(8,128)(2,1)S(1)}, u32[]{:S(2)}, u32[]{:S(2)}) collective-permute-start(bf16[128,2048]{1,0:T(8,128)(2,1)S(1)} %copy-done), channel_id=1, source_target_pairs={{0,28},{4,0},{8,4},{12,8},{16,12},{20,16},{24,20},{28,24},{1,29},{... | collective-permute-start | bytes 1572872 | tf_op jit(solution)/shard_map/ppermute | solution.py:338
  16.8 40.6 %collective-permute-start.7 = (bf16[128,2048]{1,0:T(8,128)(2,1)S(1)}, bf16[128,2048]{1,0:T(8,128)(2,1)S(1)}, u32[]{:S(2)}, u32[]{:S(2)}) collective-permute-start(bf16[128,2048]{1,0:T(8,128)(2,1)S(1)} %copy-done), channel_id=1, source_target_pairs={{0,1},{1,0},{2,3},{3,2},{4,5},{5,4},{6,7},{7,6},{8,9},{9,8},{10,11... | collective-permute-start | bytes 1572872 | tf_op jit(solution)/shard_map/ppermute | solution.py:298
  18.9 14.4 %all-to-all-start = ((f32[16,8,256]{2,1,0:T(8,128)}), f32[16,8,256]{2,1,0:T(8,128)S(1)}, u32[]{:S(2)}, u32[]{:S(2)}) async-start(f32[16,8,256]{2,1,0:T(8,128)} %broadcast_in_dim.88), calls=%async_computation | async-start | bytes 262144 | tf_op jit(solution)/shard_map/all_to_all | solution.py:346
  28.3 14.1 %collective-permute-start.1 = (bf16[128,2048]{1,0:T(8,128)(2,1)S(1)}, bf16[128,2048]{1,0:T(8,128)(2,1)S(1)}, u32[]{:S(2)}, u32[]{:S(2)}) collective-permute-start(bf16[128,2048]{1,0:T(8,128)(2,1)S(1)} %collective-permute-done.refs_1_), channel_id=1, source_target_pairs={{0,4},{4,8},{8,12},{12,16},{16,20},{20,24},{24,28},{28,0},{1,5},{5... | collective-permute-start | bytes 1572872 | tf_op jit(solution)/shard_map/ppermute | solution.py:335
  34.2 13.9 %collective-permute-start.5 = (bf16[128,2048]{1,0:T(8,128)(2,1)S(1)}, bf16[128,2048]{1,0:T(8,128)(2,1)S(1)}, u32[]{:S(2)}, u32[]{:S(2)}) collective-permute-start(bf16[128,2048]{1,0:T(8,128)(2,1)S(1)} %collective-permute-done.4.refs_7_), channel_id=1, source_target_pairs={{0,28},{4,0},{8,4},{12,8},{16,12},{20,16},{24,20},{28,24},{1,29},{... | collective-permute-start | bytes 1572872 | tf_op jit(solution)/shard_map/ppermute | solution.py:338
  42.4 12.9 %collective-permute-start.2 = (bf16[128,2048]{1,0:T(8,128)(2,1)S(1)}, bf16[128,2048]{1,0:T(8,128)(2,1)}, u32[]{:S(2)}, u32[]{:S(2)}) collective-permute-start(bf16[128,2048]{1,0:T(8,128)(2,1)S(1)} %collective-permute-done.1.refs_2_), channel_id=1, source_target_pairs={{0,4},{4,8},{8,12},{12,16},{16,20},{20,24},{24,28},{28,0},{1,5},{5... | collective-permute-start | bytes 1572872 | tf_op jit(solution)/shard_map/ppermute | solution.py:335
  43.6 16.7 %collective-permute-start.14 = (bf16[128,2048]{1,0:T(8,128)(2,1)S(1)}, bf16[128,2048]{1,0:T(8,128)(2,1)}, u32[]{:S(2)}, u32[]{:S(2)}) collective-permute-start(bf16[128,2048]{1,0:T(8,128)(2,1)S(1)} %collective-permute-done.4.refs_7_), channel_id=1, source_target_pairs={{0,1},{1,0},{2,3},{3,2},{4,5},{5,4},{6,7},{7,6},{8,9},{9,8},{10,11... | collective-permute-start | bytes 1572872 | tf_op jit(solution)/shard_map/ppermute | solution.py:298
  45.5 14.9 %collective-permute-start.8 = (bf16[128,2048]{1,0:T(8,128)(2,1)S(1)}, bf16[128,2048]{1,0:T(8,128)(2,1)}, u32[]{:S(2)}, u32[]{:S(2)}) collective-permute-start(bf16[128,2048]{1,0:T(8,128)(2,1)S(1)} %collective-permute-done.refs_1_), channel_id=1, source_target_pairs={{0,1},{1,0},{2,3},{3,2},{4,5},{5,4},{6,7},{7,6},{8,9},{9,8},{10,11... | collective-permute-start | bytes 1572872 | tf_op jit(solution)/shard_map/ppermute | solution.py:298
  48.0 12.8 %collective-permute-start.6 = (bf16[128,2048]{1,0:T(8,128)(2,1)S(1)}, bf16[128,2048]{1,0:T(8,128)(2,1)}, u32[]{:S(2)}, u32[]{:S(2)}) collective-permute-start(bf16[128,2048]{1,0:T(8,128)(2,1)S(1)} %collective-permute-done.5.refs_6_), channel_id=1, source_target_pairs={{0,28},{4,0},{8,4},{12,8},{16,12},{20,16},{24,20},{28,24},{1,29},{... | collective-permute-start | bytes 1572872 | tf_op jit(solution)/shard_map/ppermute | solution.py:338
  55.3 12.1 %collective-permute-start.3 = (bf16[128,2048]{1,0:T(8,128)(2,1)}, bf16[128,2048]{1,0:T(8,128)(2,1)}, u32[]{:S(2)}, u32[]{:S(2)}) collective-permute-start(bf16[128,2048]{1,0:T(8,128)(2,1)} %collective-permute-done.2.refs_3_), channel_id=1, source_target_pairs={{0,4},{4,8},{8,12},{12,16},{16,20},{20,24},{24,28},{28,0},{1,5},{5... | collective-permute-start | bytes 1572872 | tf_op jit(solution)/shard_map/ppermute | solution.py:335
  57.4 30.2 %collective-permute-start.13 = (bf16[128,2048]{1,0:T(8,128)(2,1)S(1)}, bf16[128,2048]{1,0:T(8,128)(2,1)}, u32[]{:S(2)}, u32[]{:S(2)}) collective-permute-start(bf16[128,2048]{1,0:T(8,128)(2,1)S(1)} %collective-permute-done.5.refs_6_), channel_id=1, source_target_pairs={{0,1},{1,0},{2,3},{3,2},{4,5},{5,4},{6,7},{7,6},{8,9},{9,8},{10,11... | collective-permute-start | bytes 1572872 | tf_op jit(solution)/shard_map/ppermute | solution.py:298
  60.3 27.4 %collective-permute-start.9 = (bf16[128,2048]{1,0:T(8,128)(2,1)S(1)}, bf16[128,2048]{1,0:T(8,128)(2,1)}, u32[]{:S(2)}, u32[]{:S(2)}) collective-permute-start(bf16[128,2048]{1,0:T(8,128)(2,1)S(1)} %collective-permute-done.1.refs_2_), channel_id=1, source_target_pairs={{0,1},{1,0},{2,3},{3,2},{4,5},{5,4},{6,7},{7,6},{8,9},{9,8},{10,11... | collective-permute-start | bytes 1572872 | tf_op jit(solution)/shard_map/ppermute | solution.py:298
  60.4 27.3 %collective-permute-start.10 = (bf16[128,2048]{1,0:T(8,128)(2,1)}, bf16[128,2048]{1,0:T(8,128)(2,1)}, u32[]{:S(2)}, u32[]{:S(2)}) collective-permute-start(bf16[128,2048]{1,0:T(8,128)(2,1)} %collective-permute-done.2.refs_3_), channel_id=1, source_target_pairs={{0,1},{1,0},{2,3},{3,2},{4,5},{5,4},{6,7},{7,6},{8,9},{9,8},{10,11... | collective-permute-start | bytes 1572872 | tf_op jit(solution)/shard_map/ppermute | solution.py:298
  60.8 26.8 %collective-permute-start.12 = (bf16[128,2048]{1,0:T(8,128)(2,1)}, bf16[128,2048]{1,0:T(8,128)(2,1)}, u32[]{:S(2)}, u32[]{:S(2)}) collective-permute-start(bf16[128,2048]{1,0:T(8,128)(2,1)} %collective-permute-done.6.refs_5_), channel_id=1, source_target_pairs={{0,1},{1,0},{2,3},{3,2},{4,5},{5,4},{6,7},{7,6},{8,9},{9,8},{10,11... | collective-permute-start | bytes 1572872 | tf_op jit(solution)/shard_map/ppermute | solution.py:298
  67.5 20.2 %collective-permute-start.11 = (bf16[128,2048]{1,0:T(8,128)(2,1)}, bf16[128,2048]{1,0:T(8,128)(2,1)}, u32[]{:S(2)}, u32[]{:S(2)}) collective-permute-start(bf16[128,2048]{1,0:T(8,128)(2,1)} %collective-permute-done.3.refs_4_), channel_id=1, source_target_pairs={{0,1},{1,0},{2,3},{3,2},{4,5},{5,4},{6,7},{7,6},{8,9},{9,8},{10,11... | collective-permute-start | bytes 1572872 | tf_op jit(solution)/shard_map/ppermute | solution.py:298
  71.9 13.8 %all-to-all-start.1 = ((f32[16,8,128]{2,1,0:T(8,128)}), f32[16,8,128]{2,1,0:T(8,128)S(1)}, u32[]{:S(2)}, u32[]{:S(2)}) async-start(f32[16,8,128]{2,1,0:T(8,128)} %broadcast_in_dim_broadcast_in_dim_broadcast_in_dim.2), calls=%async_computation.1 | async-start | bytes 131072 | tf_op jit(solution)/shard_map/all_to_all | solution.py:303
  146.6 10.3 %collective-permute-start.20 = (bf16[4,256,128]{2,1,0:T(8,128)(2,1)S(1)}, bf16[4,256,128]{2,1,0:T(8,128)(2,1)S(1)}, u32[]{:S(2)}, u32[]{:S(2)}) collective-permute-start(bf16[4,256,128]{2,1,0:T(8,128)(2,1)S(1)} %pad_maximum_fusion.1.refs_0_), channel_id=1, source_target_pairs={{0,64},{2,66},{32,96},{34,98},{64,128},{66,130},{96,160},{98,162},... | collective-permute-start | bytes 786440 | tf_op jit(solution)/shard_map/ppermute | solution.py:310
  147.3 10.2 %collective-permute-start.21 = (bf16[4,256,128]{2,1,0:T(8,128)(2,1)S(1)}, bf16[4,256,128]{2,1,0:T(8,128)(2,1)S(1)}, u32[]{:S(2)}, u32[]{:S(2)}) collective-permute-start(bf16[4,256,128]{2,1,0:T(8,128)(2,1)S(1)} %pad_maximum_fusion.1.refs_0_), channel_id=1, source_target_pairs={{0,128},{2,130},{32,160},{34,162},{64,192},{66,194},{96,224},{98,2... | collective-permute-start | bytes 786440 | tf_op jit(solution)/shard_map/ppermute | solution.py:310
  147.6 13.7 %collective-permute-start.22 = (bf16[4,256,128]{2,1,0:T(8,128)(2,1)S(1)}, bf16[4,256,128]{2,1,0:T(8,128)(2,1)S(1)}, u32[]{:S(2)}, u32[]{:S(2)}) collective-permute-start(bf16[4,256,128]{2,1,0:T(8,128)(2,1)S(1)} %pad_maximum_fusion.1.refs_0_), channel_id=1, source_target_pairs={{0,192},{2,194},{32,224},{34,226},{64,0},{66,2},{96,32},{98,34},{1... | collective-permute-start | bytes 786440 | tf_op jit(solution)/shard_map/ppermute | solution.py:310
  196.1 7.2 %collective-permute-start.27 = (bf16[4,256,128]{2,1,0:T(8,128)(2,1)S(1)}, bf16[4,256,128]{2,1,0:T(8,128)(2,1)S(1)}, u32[]{:S(2)}, u32[]{:S(2)}) collective-permute-start(bf16[4,256,128]{2,1,0:T(8,128)(2,1)S(1)} %pad_maximum_fusion.2.refs_0_), channel_id=1, source_target_pairs={{0,64},{2,66},{32,96},{34,98},{64,128},{66,130},{96,160},{98,162},... | collective-permute-start | bytes 786440 | tf_op jit(solution)/shard_map/ppermute | solution.py:310
  196.2 13.6 %collective-permute-start.28 = (bf16[4,256,128]{2,1,0:T(8,128)(2,1)S(1)}, bf16[4,256,128]{2,1,0:T(8,128)(2,1)S(1)}, u32[]{:S(2)}, u32[]{:S(2)}) collective-permute-start(bf16[4,256,128]{2,1,0:T(8,128)(2,1)S(1)} %pad_maximum_fusion.2.refs_0_), channel_id=1, source_target_pairs={{0,128},{2,130},{32,160},{34,162},{64,192},{66,194},{96,224},{98,2... | collective-permute-start | bytes 786440 | tf_op jit(solution)/shard_map/ppermute | solution.py:310
  199.7 11.0 %collective-permute-start.29 = (bf16[4,256,128]{2,1,0:T(8,128)(2,1)S(1)}, bf16[4,256,128]{2,1,0:T(8,128)(2,1)S(1)}, u32[]{:S(2)}, u32[]{:S(2)}) collective-permute-start(bf16[4,256,128]{2,1,0:T(8,128)(2,1)S(1)} %pad_maximum_fusion.2.refs_0_), channel_id=1, source_target_pairs={{0,192},{2,194},{32,224},{34,226},{64,0},{66,2},{96,32},{98,34},{1... | collective-permute-start | bytes 786440 | tf_op jit(solution)/shard_map/ppermute | solution.py:310
  (13 other events, 65.5 us)
Sparse Core Ops, SparseCore 0:
  10.3 85.2 all-gather.1

commit v7 on v6

--- a/solution.py
+++ b/solution.py
@@ -27,6 +27,31 @@
 VMEM_LIMIT = 48 * 1024 * 1024
 
 
+def prepare_kernel(prints, activity, mask, extended, seeded):
+    value = activity[...].astype(jnp.float32).T * mask[...].astype(jnp.float32)
+    seeded[...] = value
+    labels = value.astype(jnp.bfloat16)
+    extended[:PIECE, :] = prints[...]
+    for group in range(labels.shape[0] // EXTRA):
+        extended[PIECE:, group * PIECE:(group + 1) * PIECE] = labels[
+            group * EXTRA:(group + 1) * EXTRA, :
+        ]
+
+
+def prepare(prints, activity, mask):
+    vmem = pl.BlockSpec(memory_space=pltpu.VMEM)
+    return pl.pallas_call(
+        prepare_kernel,
+        out_shape=(
+            jax.ShapeDtypeStruct((PIECE + EXTRA, prints.shape[1]), jnp.bfloat16),
+            jax.ShapeDtypeStruct((activity.shape[1], PIECE), jnp.float32),
+        ),
+        in_specs=[vmem] * 3,
+        out_specs=(vmem, vmem),
+        name="prepare",
+    )(prints, activity, mask[None])
+
+
 def split_rows(z, total, keep, send):
     half = ROWS // 2
     for piece in range(half):
@@ -38,7 +63,7 @@
 def weights_kernel(pairs, meta, starts, *refs):
     rows = refs[:ROWS]
     (cols, row_sq, col_sq, weights, keep, send, degree_keep, degree_send,
-     col_buf, row_buf, tile_buf, label_raw, labels, total, degree,
+     col_buf, row_buf, tile_buf, label_raw, labels, total, degree, inner_even, inner_odd,
      col_sem, row_sem, tile_sem, label_sem) = refs[ROWS:]
     live = starts[BLOCKS]
     own_offset = meta[1]
@@ -95,56 +120,87 @@
     )
     depth = col_buf.shape[-1]
 
-    def block(j, carry):
-        pltpu.make_async_copy(
-            cols.at[0, :, 0, pl.ds(0, PIECE)], col_buf.at[j], col_sem.at[j]
-        ).wait()
-
-        def pair(q, inner_carry):
-            @pl.when(q + 2 < live)
-            def _():
-                start_rows(q + 2)
-
-            row_copy(q, 0, 0).wait()
-            row_copy(q, 1, 0).wait()
-            one = pairs[2 * q]
-            two = pairs[2 * q + 1]
-            place_one = lax.rem(one, ROWS)
-            place_two = lax.rem(two, ROWS)
-            inner = lax.dot_general(
-                col_buf[j].reshape(WIDTH, depth), row_buf[lax.rem(q, 3)],
-                (((1,), (1,)), ((), ())),
-                preferred_element_type=jnp.float32,
-            )
-            row_part = jnp.concatenate([row_sq[place_one], row_sq[place_two]], axis=1)
-            ratio = inner / (
-                WEIGHT_ROW * row_part
-                + WEIGHT_COL * col_sq[j]
-                + WEIGHT_SHARED * inner
-                + EPSILON
-            )
-            offset = jnp.where(one == own_tile, own_offset, -2 * WIDTH)
-            value = jnp.where(gap == offset, 0.0, jnp.exp(SHARPNESS * (ratio - 0.5)))
-            half = value.astype(jnp.bfloat16)
-            spread = jnp.dot(labels[j], half, preferred_element_type=jnp.float32)
-            sums = jnp.sum(value, axis=0, keepdims=True)
-            tile_buf[one] = half[:, :PIECE]
-            tile_copy(one).start()
-            total[place_one] += spread[:, :PIECE]
-            degree[pl.ds(place_one, 1), :] += sums[:, :PIECE]
-
-            @pl.when(one != two)
-            def _():
-                tile_buf[two] = half[:, PIECE:]
-                tile_copy(two).start()
-                total[place_two] += spread[:, PIECE:]
-                degree[pl.ds(place_two, 1), :] += sums[:, PIECE:]
-
-            return inner_carry
-
-        return lax.fori_loop(starts[j], starts[j + 1], pair, carry)
-
-    lax.fori_loop(0, BLOCKS, block, 0)
+    def arrive(q):
+        j = pairs[2 * q] // ROWS
+
+        @pl.when(q == starts[j])
+        def _():
+            pltpu.make_async_copy(
+                cols.at[0, :, 0, pl.ds(0, PIECE)], col_buf.at[j], col_sem.at[j]
+            ).wait()
+
+        row_copy(q, 0, 0).wait()
+        row_copy(q, 1, 0).wait()
+
+    def multiply(q):
+        return lax.dot_general(
+            col_buf[pairs[2 * q] // ROWS].reshape(WIDTH, depth), row_buf[lax.rem(q, 3)],
+            (((1,), (1,)), ((), ())),
+            preferred_element_type=jnp.float32,
+        )
+
+    @pl.when(live > 0)
+    def _():
+        arrive(0)
+        inner_even[...] = multiply(0)
+
+    def step(q, current, following):
+        @pl.when(q + 2 < live)
+        def _():
+            start_rows(q + 2)
+
+        @pl.when(q + 1 < live)
+        def _():
+            arrive(q + 1)
+
+        following[...] = multiply(jnp.minimum(q + 1, live - 1))
+        one = pairs[2 * q]
+        two = pairs[2 * q + 1]
+        j = one // ROWS
+        place_one = lax.rem(one, ROWS)
+        place_two = lax.rem(two, ROWS)
+        inner = current[...]
+        row_part = jnp.concatenate([row_sq[place_one], row_sq[place_two]], axis=1)
+        ratio = inner / (
+            WEIGHT_ROW * row_part
+            + WEIGHT_COL * col_sq[j]
+            + WEIGHT_SHARED * inner
+            + EPSILON
+        )
+        offset = jnp.where(one == own_tile, own_offset, -2 * WIDTH)
+        value = jnp.where(gap == offset, 0.0, jnp.exp(SHARPNESS * (ratio - 0.5)))
+        half = value.astype(jnp.bfloat16)
+        spread = jnp.dot(labels[j], half, preferred_element_type=jnp.float32)
+        sums = jnp.sum(value, axis=0, keepdims=True)
+        tile_buf[one] = half[:, :PIECE]
+        tile_copy(one).start()
+        total[place_one] += spread[:, :PIECE]
+        degree[pl.ds(place_one, 1), :] += sums[:, :PIECE]
+
+        @pl.when(one != two)
+        def _():
+            tile_buf[two] = half[:, PIECE:]
+            tile_copy(two).start()
+            total[place_two] += spread[:, PIECE:]
+            degree[pl.ds(place_two, 1), :] += sums[:, PIECE:]
+
+    def steps(i, carry):
+        step(2 * i, inner_even, inner_odd)
+
+        @pl.when(2 * i + 1 < live)
+        def _():
+            step(2 * i + 1, inner_odd, inner_even)
+
+        return carry
+
+    lax.fori_loop(0, (live + 1) // 2, steps, 0)
+    for j in range(BLOCKS):
+        @pl.when(starts[j] == starts[j + 1])
+        def _():
+            pltpu.make_async_copy(
+                cols.at[0, :, 0, pl.ds(0, PIECE)], col_buf.at[j], col_sem.at[j]
+            ).wait()
+
     split_rows(z, total, keep, send)
     half_rows = ROWS // 2
     for piece in range(half_rows):
@@ -189,6 +245,8 @@
             pltpu.VMEM((BLOCKS, tasks, WIDTH), jnp.bfloat16),
             pltpu.VMEM((ROWS, tasks, PIECE), jnp.float32),
             pltpu.VMEM((ROWS, PIECE), jnp.float32),
+            pltpu.VMEM((WIDTH, 2 * PIECE), jnp.float32),
+            pltpu.VMEM((WIDTH, 2 * PIECE), jnp.float32),
             pltpu.SemaphoreType.DMA((BLOCKS,)),
             pltpu.SemaphoreType.DMA((3, 2)),
             pltpu.SemaphoreType.DMA((TILES,)),
@@ -204,9 +262,7 @@
     )(pairs, meta, starts, *rows, cols, row_sq, col_sq)
 
 
-def spread_kernel(pairs, meta, starts, weights, *refs):
-    shifted = refs[:4]
-    keep, send, labels, total, tile_buf, tile_sem = refs[4:]
+def spread_kernel(pairs, meta, starts, weights, pieces, keep, send, total, tile_buf, tile_sem):
     live = starts[BLOCKS]
     z = meta[3]
     half = ROWS // 2
@@ -229,13 +285,6 @@
 
     lax.fori_loop(0, live, begin, 0)
     total[...] = jnp.zeros_like(total)
-    for down in range(4):
-        from_y = lax.rem(meta[4] - down + 4, 4)
-        for right in range(4):
-            from_x = lax.rem(meta[5] - right + 4, 4)
-            block = lax.rem(from_x, 2) * 2 + from_y // 2
-            sub = lax.rem(from_y, 2) * 2 + from_x // 2
-            labels[block, sub] = shifted[down][right]
 
     def add(tile_id, value):
         a = lax.rem(tile_id, ROWS)
@@ -254,7 +303,7 @@
 
         j = one // ROWS
         spread = jnp.dot(
-            jnp.concatenate([labels[j, sub] for sub in range(WIDTH // PIECE)], axis=1),
+            jnp.concatenate([pieces[j * 4 + sub] for sub in range(WIDTH // PIECE)], axis=1),
             tile_buf[q], preferred_element_type=jnp.float32,
         )
         add(one, spread[:, :PIECE])
@@ -270,28 +319,27 @@
     send[...] = total[half:].astype(jnp.bfloat16)
 
 
-def spread_rows(pairs, meta, starts, weights, shifted):
+def spread_rows(pairs, meta, starts, weights, pieces):
     smem = pl.BlockSpec(memory_space=pltpu.SMEM)
     vmem = pl.BlockSpec(memory_space=pltpu.VMEM)
     hbm = pl.BlockSpec(memory_space=pl.ANY)
-    tasks = shifted[0].shape[1]
+    tasks = pieces.shape[1]
     return pl.pallas_call(
         spread_kernel,
         out_shape=(
             jax.ShapeDtypeStruct((ROWS // 2, tasks, PIECE), jnp.float32),
             jax.ShapeDtypeStruct((ROWS // 2, tasks, PIECE), jnp.bfloat16),
         ),
-        in_specs=[smem, smem, smem, hbm] + [vmem] * 4,
+        in_specs=[smem, smem, smem, hbm, vmem],
         out_specs=(vmem, vmem),
         scratch_shapes=[
-            pltpu.VMEM((BLOCKS, WIDTH // PIECE, tasks, PIECE), jnp.bfloat16),
             pltpu.VMEM((ROWS, tasks, PIECE), jnp.float32),
             pltpu.VMEM((TILES // 2, WIDTH, 2 * PIECE), jnp.bfloat16),
             pltpu.SemaphoreType.DMA((TILES // 2, 2)),
         ],
         compiler_params=pltpu.CompilerParams(vmem_limit_bytes=VMEM_LIMIT),
         name="spread",
-    )(pairs, meta, starts, weights, *shifted)
+    )(pairs, meta, starts, weights, pieces)
 
 
 def swap_cores(value):
@@ -301,20 +349,6 @@
 def gather_pieces(piece):
     copies = jnp.broadcast_to(piece[None], (ROWS,) + piece.shape)
     return lax.all_to_all(copies, PLANE, 0, 0)
-
-
-def shift_plane(value, down, right):
-    moves = [
-        (y * 4 + x, (y + down) % 4 * 4 + (x + right) % 4) for y in range(4) for x in range(4)
-    ]
-    return lax.ppermute(value, ("y", "xh", "xl"), moves)
-
-
-def gather_shifted(labels):
-    one, three, two = [shift_plane(labels, 0, right) for right in (1, 3, 2)]
-    line = jnp.stack([labels, one, two, three])
-    one, three, two = [shift_plane(line, down, 0) for down in (1, 3, 2)]
-    return [line, one, two, three]
 
 
 def body(fingerprints, activity, label_mask, pattern, counts):
@@ -322,11 +356,7 @@
     depth = fingerprints.shape[1]
     slots = pattern.shape[1]
     tasks = activity.shape[1]
-    seeded = activity.T.astype(jnp.float32) * label_mask.astype(jnp.float32)[None, :]
-    labels = seeded.astype(jnp.bfloat16).reshape(tasks // EXTRA, EXTRA, PIECE)
-    extended = jnp.concatenate(
-        [fingerprints, labels.transpose(1, 0, 2).reshape(EXTRA, depth)], axis=0
-    )
+    extended, seeded = prepare(fingerprints, activity, label_mask)
     cols = lax.all_gather(extended, ("y", "xh", "xl"), axis=0, tiled=True)
     cols = cols.reshape(2, 4, 2, PIECE + EXTRA, depth)
 
@@ -376,7 +406,7 @@
     starts = (jnp.concatenate([block_start, jnp.sum(even)[None]]) // 2).astype(jnp.int32)
     own_tile = (xl * 2 + y // 2) * ROWS
     own_offset = ((y % 2) * 2 + xh) * PIECE
-    meta = jnp.stack([jnp.sum(flat), own_offset, own_tile, z, y, xh * 2 + xl]).astype(jnp.int32)
+    meta = jnp.stack([jnp.sum(flat), own_offset, own_tile, z]).astype(jnp.int32)
 
     weights, keep, send, degree_keep, degree_send = build_weights(
         pairs, meta, starts, rows, cols, row_sq, col_sq
@@ -400,7 +430,7 @@
             summed = summed[:tasks]
         labels = (PROPAGATE * summed / degree_own[None, :] + ANCHOR * seeded).astype(jnp.bfloat16)
         if iteration < ITERS - 1:
-            gathered = gather_shifted(labels)
+            gathered = gather_pieces(labels)
     return labels.T
 
 

time: 245 us -> 242 us (0.988)
  blocking collectives: 69.8 us -> 105 us
  waiting for transfers between devices: 74 us -> 47.7 us
  starting transfers between devices: 54.4 us -> 48.1 us
    all_to_all x0 -> x2, blocking collectives: none -> 41.8 us  [gather_pieces(): return lax.all_to_all(copies, PLANE, 0, 0)]
    ppermute x12 -> x0, waiting for transfers between devices: 27.7 us -> none  [shift_plane(): return lax.ppermute(value, ('y', 'xh', 'xl'), moves)]
    ppermute x12 -> x0, starting transfers between devices: 16.4 us -> none  [shift_plane(): return lax.ppermute(value, ('y', 'xh', 'xl'), moves)]
    ppermute x12, starting transfers between devices: 15 us -> 23.7 us  [swap_cores(): return lax.ppermute(value, 'core', [(0, 1), (1, 0)])]
    ppermute x4, waiting for transfers between devices: 19.9 us -> 26.2 us  [body(): lax.ppermute(upward[-1], 'z', [(i, (i + 1) % 8) for i in range(8)])]
    all_to_all x3, blocking collectives: 69.8 us -> 63.6 us  [body(): parts = lax.all_to_all(part, 'z', 0, 0)]
    all_gather x1, waiting for transfers between devices: 7.94 us -> 2.71 us  [body(): cols = lax.all_gather(extended, ('y', 'xh', 'xl'), axis=0, tiled=True)]
    ppermute x4, starting transfers between devices: 2.55 us -> 6.69 us  [body(): lax.ppermute(upward[-1], 'z', [(i, (i + 1) % 8) for i in range(8)])]
  transfers between devices with their start and end apart: 34 -> 22, of which waited for: 22 -> 9; matrix products, arithmetic and copies ran while one was open for 4% -> 4% of each run, Pallas kernels for 0% -> 0%
where the time goes in v7:
time: 242 us; the launch traced here: 243 us
  blocking collectives  105 us (43%)
  starting transfers between devices  48.1 us (20%)
  waiting for transfers between devices  47.7 us (20%)
  Pallas kernels  15.8 us (7%)
  between operations  13.7 us (6%)
  other arithmetic  6.16 us (3%)
  local copies, waits for them, and re-layouts  5.75 us (2%)
    all_to_all x3, blocking collectives, body(): parts = lax.all_to_all(part, 'z', 0, 0)  63.6 us
    all_to_all x2, blocking collectives, gather_pieces(): return lax.all_to_all(copies, PLANE, 0, 0)  41.8 us
    ppermute x4, waiting for transfers between devices, body(): lax.ppermute(upward[-1], 'z', [(i, (i + 1) % 8) for i in range(8)])  26.2 us
    ppermute x12, starting transfers between devices, swap_cores(): return lax.ppermute(value, 'core', [(0, 1), (1, 0)])  23.7 us
    pallas_call x1, Pallas kernels, build_weights(): pl.pallas_call(weights_kernel, out_shape=(jax.ShapeDtypeStruct((TILES, WI...  8.77 us
    all_to_all x1, waiting for transfers between devices, body(): info = lax.all_to_all(info, ('core', 'z'), 0, 0)[:, 0]  7.85 us
    all_to_all x1, starting transfers between devices, gather_pieces(): return lax.all_to_all(copies, PLANE, 0, 0)  6.75 us
    ppermute x4, starting transfers between devices, body(): lax.ppermute(upward[-1], 'z', [(i, (i + 1) % 8) for i in range(8)])  6.69 us
  transfers between devices with their start and end apart: 22, of which 9 were waited for; matrix products, arithmetic and copies ran while one was open for 4% of the time, Pallas kernels for 0%

profile of v7, /device:TPU:1, one launch (start us, length us, event | category | flops | bytes accessed | tf_op | source)
XLA Modules:
  0.0 242.5 jit_solution(10245973752498745060)
XLA Ops:
  8.7 2.5 %collective-permute-start = (bf16[128,2048]{1,0:T(8,128)(2,1)S(1)}, bf16[128,2048]{1,0:T(8,128)(2,1)S(1)}, u32[]{:S(2)}, u32[]{:S(2)}) collective-permute-start(bf16[128,2048]{1,0:T(8,128)(2,1)S(1)} %copy-done), channel_id=1, source_target_pairs={{0,4},{4,8},{8,12},{12,16},{16,20},{20,24},{24,28},{28,0},{1,5},{5... | collective-permute-start | bytes 1572872 | tf_op jit(solution)/shard_map/ppermute | solution.py:365
  11.2 4.0 %collective-permute-start.4 = (bf16[128,2048]{1,0:T(8,128)(2,1)S(1)}, bf16[128,2048]{1,0:T(8,128)(2,1)S(1)}, u32[]{:S(2)}, u32[]{:S(2)}) collective-permute-start(bf16[128,2048]{1,0:T(8,128)(2,1)S(1)} %copy-done), channel_id=1, source_target_pairs={{0,28},{4,0},{8,4},{12,8},{16,12},{20,16},{24,20},{28,24},{1,29},{... | collective-permute-start | bytes 1572872 | tf_op jit(solution)/shard_map/ppermute | solution.py:368
  17.4 5.9 %all-to-all-start = ((f32[16,8,256]{2,1,0:T(8,128)}), f32[16,8,256]{2,1,0:T(8,128)S(1)}, u32[]{:S(2)}, u32[]{:S(2)}) async-start(f32[16,8,256]{2,1,0:T(8,128)} %broadcast_in_dim.62), calls=%async_computation | async-start | bytes 262144 | tf_op jit(solution)/shard_map/all_to_all | solution.py:376
  23.4 7.8 %all-to-all-done = f32[16,8,256]{2,1,0:T(8,128)S(1)} async-done(((f32[16,8,256]{2,1,0:T(8,128)}), f32[16,8,256]{2,1,0:T(8,128)S(1)}, u32[]{:S(2)}, u32[]{:S(2)}) %all-to-all-start) | async-done | bytes 131104 | tf_op jit(solution)/shard_map/all_to_all | solution.py:376
  31.9 3.0 %collective-permute-start.1 = (bf16[128,2048]{1,0:T(8,128)(2,1)S(1)}, bf16[128,2048]{1,0:T(8,128)(2,1)S(1)}, u32[]{:S(2)}, u32[]{:S(2)}) collective-permute-start(bf16[128,2048]{1,0:T(8,128)(2,1)S(1)} %collective-permute-done.refs_1_), channel_id=1, source_target_pairs={{0,4},{4,8},{8,12},{12,16},{16,20},{20,24},{24,28},{28,0},{1,5},{5... | collective-permute-start | bytes 1572872 | tf_op jit(solution)/shard_map/ppermute | solution.py:365
  35.2 11.1 %collective-permute-done.1.refs_2_ = bf16[128,2048]{1,0:T(8,128)(2,1)S(1)} collective-permute-done((bf16[128,2048]{1,0:T(8,128)(2,1)S(1)}, bf16[128,2048]{1,0:T(8,128)(2,1)S(1)}, u32[]{:S(2)}, u32[]{:S(2)}) %collective-permute-start.1) | collective-permute-done | bytes 524320 | tf_op jit(solution)/shard_map/ppermute | solution.py:365
  51.9 7.9 %collective-permute-done.2.refs_3_ = bf16[128,2048]{1,0:T(8,128)(2,1)} collective-permute-done((bf16[128,2048]{1,0:T(8,128)(2,1)S(1)}, bf16[128,2048]{1,0:T(8,128)(2,1)}, u32[]{:S(2)}, u32[]{:S(2)}) %collective-permute-start.2) | collective-permute-done | bytes 524320 | tf_op jit(solution)/shard_map/ppermute | solution.py:365
  61.6 2.5 %collective-permute-start.9 = (bf16[128,2048]{1,0:T(8,128)(2,1)S(1)}, bf16[128,2048]{1,0:T(8,128)(2,1)}, u32[]{:S(2)}, u32[]{:S(2)}) collective-permute-start(bf16[128,2048]{1,0:T(8,128)(2,1)S(1)} %collective-permute-done.1.refs_2_), channel_id=1, source_target_pairs={{0,1},{1,0},{2,3},{3,2},{4,5},{5,4},{6,7},{7,6},{8,9},{9,8},{10,11... | collective-permute-start | bytes 1572872 | tf_op jit(solution)/shard_map/ppermute | solution.py:346
  65.4 7.2 %collective-permute-done.3.refs_4_ = bf16[128,2048]{1,0:T(8,128)(2,1)} collective-permute-done((bf16[128,2048]{1,0:T(8,128)(2,1)}, bf16[128,2048]{1,0:T(8,128)(2,1)}, u32[]{:S(2)}, u32[]{:S(2)}) %collective-permute-start.3) | collective-permute-done | bytes 524320 | tf_op jit(solution)/shard_map/ppermute | solution.py:365
  72.6 3.1 %collective-permute-start.11 = (bf16[128,2048]{1,0:T(8,128)(2,1)}, bf16[128,2048]{1,0:T(8,128)(2,1)}, u32[]{:S(2)}, u32[]{:S(2)}) collective-permute-start(bf16[128,2048]{1,0:T(8,128)(2,1)} %collective-permute-done.3.refs_4_), channel_id=1, source_target_pairs={{0,1},{1,0},{2,3},{3,2},{4,5},{5,4},{6,7},{7,6},{8,9},{9,8},{10,11... | collective-permute-start | bytes 1572872 | tf_op jit(solution)/shard_map/ppermute | solution.py:346
  76.4 6.8 %all-to-all-start.1 = ((f32[16,8,128]{2,1,0:T(8,128)}), f32[16,8,128]{2,1,0:T(8,128)S(1)}, u32[]{:S(2)}, u32[]{:S(2)}) async-start(f32[16,8,128]{2,1,0:T(8,128)} %broadcast_in_dim_broadcast_in_dim_broadcast_in_dim.2), calls=%async_computation.1 | async-start | bytes 131072 | tf_op jit(solution)/shard_map/all_to_all | solution.py:351
  83.9 6.5 %all-to-all-done.1 = f32[16,8,128]{2,1,0:T(8,128)S(1)} async-done(((f32[16,8,128]{2,1,0:T(8,128)}), f32[16,8,128]{2,1,0:T(8,128)S(1)}, u32[]{:S(2)}, u32[]{:S(2)}) %all-to-all-start.1) | async-done | bytes 65568 | tf_op jit(solution)/shard_map/all_to_all | solution.py:351
  92.3 2.7 %all-gather.2.cloned.1.call-done = bf16[2304,2048]{1,0:T(8,128)(2,1)} async-done(((bf16[144,2048]{1,0:T(8,128)(2,1)}), bf16[2304,2048]{1,0:T(8,128)(2,1)}) %all-gather.2.cloned.1.call-update) | async-done | bytes 9437200 | tf_op jit(solution)/shard_map/all_gather | solution.py:360
  95.1 8.8 %weights.1 = (bf16[64,512,128]{2,1,0:T(8,128)(2,1)}, f32[8,256,128]{2,1,0:T(8,128)}, bf16[8,256,128]{2,1,0:T(8,128)(2,1)S(1)}, f32[8,128]{1,0:T(8,128)S(1)}, f32[8,128]{1,0:T(8,128)S(1)}) custom-call(s32[72]{0:T(128)S(1)} %select_reduce_fusion.pairs, s32[4]{0:T(128)S(1)} %pad_add_fusion.meta, s32[5]{0:T(128)S(1)} %and_select_fusion.starts, ...), custom_call_target="tpu_custom_call" | custom-call | flops 4294967296 | bytes 16777216 | tf_op jit(solution)/shard_map/weights/pallas_call | solution.py:229
  103.8 5.4 %collective-permute-start.15 = (bf16[8,256,128]{2,1,0:T(8,128)(2,1)S(1)}, bf16[8,256,128]{2,1,0:T(8,128)(2,1)S(1)}, u32[]{:S(2)}, u32[]{:S(2)}) collective-permute-start(bf16[8,256,128]{2,1,0:T(8,128)(2,1)S(1)} %get-tuple-element.25), channel_id=1, source_target_pairs={{0,1},{1,0},{2,3},{3,2},{4,5},{5,4},{6,7},{7,6},{8,9},{9,8},{10,11... | collective-permute-start | bytes 1572872 | tf_op jit(solution)/shard_map/ppermute | solution.py:346
  112.4 22.8 %all_to_all.35 = bf16[8,272,128]{2,1,0:T(8,128)(2,1)S(1)} all-to-all(bf16[8,272,128]{2,1,0:T(8,128)(2,1)S(1)} %maximum_maximum_fusion), channel_id=1, replica_groups=mesh['y'=4,'xh'=2,'z'=8,'xl'=2,'core'=2] {'z'}, dimensions={0} | all-to-all | bytes 1114112 | tf_op jit(solution)/shard_map/all_to_all | solution.py:426
  135.5 23.9 %all_to_all.36.pieces = bf16[16,256,128]{2,1,0:T(8,128)(2,1)S(1)} all-to-all(bf16[16,256,128]{2,1,0:T(8,128)(2,1)S(1)} %broadcast_in_dim.114), channel_id=1, replica_groups=mesh['y'=4,'xh'=2,'z'=8,'xl'=2,'core'=2] {'xl','y','xh'}, dimensions={0} | all-to-all | bytes 2097152 | tf_op jit(solution)/shard_map/all_to_all | solution.py:351
  159.4 2.5 %spread.2 = (f32[8,256,128]{2,1,0:T(8,128)S(1)}, bf16[8,256,128]{2,1,0:T(8,128)(2,1)S(1)}) custom-call(s32[72]{0:T(128)S(1)} %select_reduce_fusion.pairs, s32[4]{0:T(128)S(1)} %pad_add_fusion.meta, s32[5]{0:T(128)S(1)} %and_select_fusion.starts, bf16[64,512,128]{2,1,0:T(8,128)(2,1)} %get-tuple-element.23.weights, bf16[16,256,128]{2,1,0:T(8,128)(2,1)S(1)} %all_to_all.36.pieces), custom_call_target="tpu_custom_call" | custom-call | tf_op jit(solution)/shard_map/spread/pallas_call | solution.py:327
  161.9 4.4 %collective-permute-start.17 = (bf16[8,256,128]{2,1,0:T(8,128)(2,1)S(1)}, bf16[8,256,128]{2,1,0:T(8,128)(2,1)S(1)}, u32[]{:S(2)}, u32[]{:S(2)}) collective-permute-start(bf16[8,256,128]{2,1,0:T(8,128)(2,1)S(1)} %get-tuple-element.30), channel_id=1, source_target_pairs={{0,1},{1,0},{2,3},{3,2},{4,5},{5,4},{6,7},{7,6},{8,9},{9,8},{10,11... | collective-permute-start | bytes 1572872 | tf_op jit(solution)/shard_map/ppermute | solution.py:346
  167.9 20.4 %all_to_all.37 = bf16[8,256,128]{2,1,0:T(8,128)(2,1)S(1)} all-to-all(bf16[8,256,128]{2,1,0:T(8,128)(2,1)S(1)} %add_convert_fusion.1), channel_id=1, replica_groups=mesh['y'=4,'xh'=2,'z'=8,'xl'=2,'core'=2] {'z'}, dimensions={0} | all-to-all | bytes 1048576 | tf_op jit(solution)/shard_map/all_to_all | solution.py:426
  188.6 18.0 %all_to_all.38.pieces = bf16[16,256,128]{2,1,0:T(8,128)(2,1)S(1)} all-to-all(bf16[16,256,128]{2,1,0:T(8,128)(2,1)S(1)} %broadcast_in_dim.115), channel_id=1, replica_groups=mesh['y'=4,'xh'=2,'z'=8,'xl'=2,'core'=2] {'xl','y','xh'}, dimensions={0} | all-to-all | bytes 2097152 | tf_op jit(solution)/shard_map/all_to_all | solution.py:351
  206.6 2.5 %spread.3 = (f32[8,256,128]{2,1,0:T(8,128)S(1)}, bf16[8,256,128]{2,1,0:T(8,128)(2,1)S(1)}) custom-call(s32[72]{0:T(128)S(1)} %select_reduce_fusion.pairs, s32[4]{0:T(128)S(1)} %pad_add_fusion.meta, s32[5]{0:T(128)S(1)} %and_select_fusion.starts, bf16[64,512,128]{2,1,0:T(8,128)(2,1)} %get-tuple-element.23.weights, bf16[16,256,128]{2,1,0:T(8,128)(2,1)S(1)} %all_to_all.38.pieces), custom_call_target="tpu_custom_call" | custom-call | tf_op jit(solution)/shard_map/spread/pallas_call | solution.py:327
  209.1 3.7 %collective-permute-start.18 = (bf16[8,256,128]{2,1,0:T(8,128)(2,1)S(1)}, bf16[8,256,128]{2,1,0:T(8,128)(2,1)S(1)}, u32[]{:S(2)}, u32[]{:S(2)}) collective-permute-start(bf16[8,256,128]{2,1,0:T(8,128)(2,1)S(1)} %get-tuple-element.32), channel_id=1, source_target_pairs={{0,1},{1,0},{2,3},{3,2},{4,5},{5,4},{6,7},{7,6},{8,9},{9,8},{10,11... | collective-permute-start | bytes 1572872 | tf_op jit(solution)/shard_map/ppermute | solution.py:346
  214.5 20.4 %all_to_all.39 = bf16[8,256,128]{2,1,0:T(8,128)(2,1)S(1)} all-to-all(bf16[8,256,128]{2,1,0:T(8,128)(2,1)S(1)} %add_convert_fusion), channel_id=1, replica_groups=mesh['y'=4,'xh'=2,'z'=8,'xl'=2,'core'=2] {'z'}, dimensions={0} | all-to-all | bytes 1048576 | tf_op jit(solution)/shard_map/all_to_all | solution.py:426
  (99 shorter events, 25.3 us)
Async XLA Ops:
  6.5 9.8 %copy-start.2 = (s32[2,24]{1,0:T(2,128)S(1)}, s32[2,24]{1,0:T(2,128)}, u32[]{:S(2)}) copy-start(s32[2,24]{1,0:T(2,128)} %param.8) | copy-start | bytes 580
  6.5 88.5 %all-gather.2.cloned.1.call-start = ((), (), s32[]{:S(2)}) async-start(), calls=%async_computation.7 | async-start | bytes 10027008 | tf_op jit(solution)/shard_map/all_gather | solution.py:360
  8.7 23.2 %collective-permute-start = (bf16[128,2048]{1,0:T(8,128)(2,1)S(1)}, bf16[128,2048]{1,0:T(8,128)(2,1)S(1)}, u32[]{:S(2)}, u32[]{:S(2)}) collective-permute-start(bf16[128,2048]{1,0:T(8,128)(2,1)S(1)} %copy-done), channel_id=1, source_target_pairs={{0,4},{4,8},{8,12},{12,16},{16,20},{20,24},{24,28},{28,0},{1,5},{5... | collective-permute-start | bytes 1572872 | tf_op jit(solution)/shard_map/ppermute | solution.py:365
  11.2 23.9 %collective-permute-start.4 = (bf16[128,2048]{1,0:T(8,128)(2,1)S(1)}, bf16[128,2048]{1,0:T(8,128)(2,1)S(1)}, u32[]{:S(2)}, u32[]{:S(2)}) collective-permute-start(bf16[128,2048]{1,0:T(8,128)(2,1)S(1)} %copy-done), channel_id=1, source_target_pairs={{0,28},{4,0},{8,4},{12,8},{16,12},{20,16},{24,20},{28,24},{1,29},{... | collective-permute-start | bytes 1572872 | tf_op jit(solution)/shard_map/ppermute | solution.py:368
  15.2 46.3 %collective-permute-start.7 = (bf16[128,2048]{1,0:T(8,128)(2,1)S(1)}, bf16[128,2048]{1,0:T(8,128)(2,1)S(1)}, u32[]{:S(2)}, u32[]{:S(2)}) collective-permute-start(bf16[128,2048]{1,0:T(8,128)(2,1)S(1)} %copy-done), channel_id=1, source_target_pairs={{0,1},{1,0},{2,3},{3,2},{4,5},{5,4},{6,7},{7,6},{8,9},{9,8},{10,11... | collective-permute-start | bytes 1572872 | tf_op jit(solution)/shard_map/ppermute | solution.py:346
  17.4 13.9 %all-to-all-start = ((f32[16,8,256]{2,1,0:T(8,128)}), f32[16,8,256]{2,1,0:T(8,128)S(1)}, u32[]{:S(2)}, u32[]{:S(2)}) async-start(f32[16,8,256]{2,1,0:T(8,128)} %broadcast_in_dim.62), calls=%async_computation | async-start | bytes 262144 | tf_op jit(solution)/shard_map/all_to_all | solution.py:376
  31.9 14.4 %collective-permute-start.1 = (bf16[128,2048]{1,0:T(8,128)(2,1)S(1)}, bf16[128,2048]{1,0:T(8,128)(2,1)S(1)}, u32[]{:S(2)}, u32[]{:S(2)}) collective-permute-start(bf16[128,2048]{1,0:T(8,128)(2,1)S(1)} %collective-permute-done.refs_1_), channel_id=1, source_target_pairs={{0,4},{4,8},{8,12},{12,16},{16,20},{20,24},{24,28},{28,0},{1,5},{5... | collective-permute-start | bytes 1572872 | tf_op jit(solution)/shard_map/ppermute | solution.py:365
  35.2 15.8 %collective-permute-start.5 = (bf16[128,2048]{1,0:T(8,128)(2,1)S(1)}, bf16[128,2048]{1,0:T(8,128)(2,1)S(1)}, u32[]{:S(2)}, u32[]{:S(2)}) collective-permute-start(bf16[128,2048]{1,0:T(8,128)(2,1)S(1)} %collective-permute-done.4.refs_7_), channel_id=1, source_target_pairs={{0,28},{4,0},{8,4},{12,8},{16,12},{20,16},{24,20},{28,24},{1,29},{... | collective-permute-start | bytes 1572872 | tf_op jit(solution)/shard_map/ppermute | solution.py:368
  46.3 13.5 %collective-permute-start.2 = (bf16[128,2048]{1,0:T(8,128)(2,1)S(1)}, bf16[128,2048]{1,0:T(8,128)(2,1)}, u32[]{:S(2)}, u32[]{:S(2)}) collective-permute-start(bf16[128,2048]{1,0:T(8,128)(2,1)S(1)} %collective-permute-done.1.refs_2_), channel_id=1, source_target_pairs={{0,4},{4,8},{8,12},{12,16},{16,20},{20,24},{24,28},{28,0},{1,5},{5... | collective-permute-start | bytes 1572872 | tf_op jit(solution)/shard_map/ppermute | solution.py:365
  48.7 15.4 %collective-permute-start.8 = (bf16[128,2048]{1,0:T(8,128)(2,1)S(1)}, bf16[128,2048]{1,0:T(8,128)(2,1)}, u32[]{:S(2)}, u32[]{:S(2)}) collective-permute-start(bf16[128,2048]{1,0:T(8,128)(2,1)S(1)} %collective-permute-done.refs_1_), channel_id=1, source_target_pairs={{0,1},{1,0},{2,3},{3,2},{4,5},{5,4},{6,7},{7,6},{8,9},{9,8},{10,11... | collective-permute-start | bytes 1572872 | tf_op jit(solution)/shard_map/ppermute | solution.py:346
  50.8 13.3 %collective-permute-start.14 = (bf16[128,2048]{1,0:T(8,128)(2,1)S(1)}, bf16[128,2048]{1,0:T(8,128)(2,1)}, u32[]{:S(2)}, u32[]{:S(2)}) collective-permute-start(bf16[128,2048]{1,0:T(8,128)(2,1)S(1)} %collective-permute-done.4.refs_7_), channel_id=1, source_target_pairs={{0,1},{1,0},{2,3},{3,2},{4,5},{5,4},{6,7},{7,6},{8,9},{9,8},{10,11... | collective-permute-start | bytes 1572872 | tf_op jit(solution)/shard_map/ppermute | solution.py:346
  50.9 13.6 %collective-permute-start.6 = (bf16[128,2048]{1,0:T(8,128)(2,1)S(1)}, bf16[128,2048]{1,0:T(8,128)(2,1)}, u32[]{:S(2)}, u32[]{:S(2)}) collective-permute-start(bf16[128,2048]{1,0:T(8,128)(2,1)S(1)} %collective-permute-done.5.refs_6_), channel_id=1, source_target_pairs={{0,28},{4,0},{8,4},{12,8},{16,12},{20,16},{24,20},{28,24},{1,29},{... | collective-permute-start | bytes 1572872 | tf_op jit(solution)/shard_map/ppermute | solution.py:368
  59.8 12.8 %collective-permute-start.3 = (bf16[128,2048]{1,0:T(8,128)(2,1)}, bf16[128,2048]{1,0:T(8,128)(2,1)}, u32[]{:S(2)}, u32[]{:S(2)}) collective-permute-start(bf16[128,2048]{1,0:T(8,128)(2,1)} %collective-permute-done.2.refs_3_), channel_id=1, source_target_pairs={{0,4},{4,8},{8,12},{12,16},{16,20},{20,24},{24,28},{28,0},{1,5},{5... | collective-permute-start | bytes 1572872 | tf_op jit(solution)/shard_map/ppermute | solution.py:365
  61.6 30.7 %collective-permute-start.9 = (bf16[128,2048]{1,0:T(8,128)(2,1)S(1)}, bf16[128,2048]{1,0:T(8,128)(2,1)}, u32[]{:S(2)}, u32[]{:S(2)}) collective-permute-start(bf16[128,2048]{1,0:T(8,128)(2,1)S(1)} %collective-permute-done.1.refs_2_), channel_id=1, source_target_pairs={{0,1},{1,0},{2,3},{3,2},{4,5},{5,4},{6,7},{7,6},{8,9},{9,8},{10,11... | collective-permute-start | bytes 1572872 | tf_op jit(solution)/shard_map/ppermute | solution.py:346
  64.0 28.3 %collective-permute-start.13 = (bf16[128,2048]{1,0:T(8,128)(2,1)S(1)}, bf16[128,2048]{1,0:T(8,128)(2,1)}, u32[]{:S(2)}, u32[]{:S(2)}) collective-permute-start(bf16[128,2048]{1,0:T(8,128)(2,1)S(1)} %collective-permute-done.5.refs_6_), channel_id=1, source_target_pairs={{0,1},{1,0},{2,3},{3,2},{4,5},{5,4},{6,7},{7,6},{8,9},{9,8},{10,11... | collective-permute-start | bytes 1572872 | tf_op jit(solution)/shard_map/ppermute | solution.py:346
  64.2 28.2 %collective-permute-start.10 = (bf16[128,2048]{1,0:T(8,128)(2,1)}, bf16[128,2048]{1,0:T(8,128)(2,1)}, u32[]{:S(2)}, u32[]{:S(2)}) collective-permute-start(bf16[128,2048]{1,0:T(8,128)(2,1)} %collective-permute-done.2.refs_3_), channel_id=1, source_target_pairs={{0,1},{1,0},{2,3},{3,2},{4,5},{5,4},{6,7},{7,6},{8,9},{9,8},{10,11... | collective-permute-start | bytes 1572872 | tf_op jit(solution)/shard_map/ppermute | solution.py:346
  64.6 27.8 %collective-permute-start.12 = (bf16[128,2048]{1,0:T(8,128)(2,1)}, bf16[128,2048]{1,0:T(8,128)(2,1)}, u32[]{:S(2)}, u32[]{:S(2)}) collective-permute-start(bf16[128,2048]{1,0:T(8,128)(2,1)} %collective-permute-done.6.refs_5_), channel_id=1, source_target_pairs={{0,1},{1,0},{2,3},{3,2},{4,5},{5,4},{6,7},{7,6},{8,9},{9,8},{10,11... | collective-permute-start | bytes 1572872 | tf_op jit(solution)/shard_map/ppermute | solution.py:346
  72.6 19.8 %collective-permute-start.11 = (bf16[128,2048]{1,0:T(8,128)(2,1)}, bf16[128,2048]{1,0:T(8,128)(2,1)}, u32[]{:S(2)}, u32[]{:S(2)}) collective-permute-start(bf16[128,2048]{1,0:T(8,128)(2,1)} %collective-permute-done.3.refs_4_), channel_id=1, source_target_pairs={{0,1},{1,0},{2,3},{3,2},{4,5},{5,4},{6,7},{7,6},{8,9},{9,8},{10,11... | collective-permute-start | bytes 1572872 | tf_op jit(solution)/shard_map/ppermute | solution.py:346
  76.4 14.0 %all-to-all-start.1 = ((f32[16,8,128]{2,1,0:T(8,128)}), f32[16,8,128]{2,1,0:T(8,128)S(1)}, u32[]{:S(2)}, u32[]{:S(2)}) async-start(f32[16,8,128]{2,1,0:T(8,128)} %broadcast_in_dim_broadcast_in_dim_broadcast_in_dim.2), calls=%async_computation.1 | async-start | bytes 131072 | tf_op jit(solution)/shard_map/all_to_all | solution.py:351
  103.8 7.0 %collective-permute-start.15 = (bf16[8,256,128]{2,1,0:T(8,128)(2,1)S(1)}, bf16[8,256,128]{2,1,0:T(8,128)(2,1)S(1)}, u32[]{:S(2)}, u32[]{:S(2)}) collective-permute-start(bf16[8,256,128]{2,1,0:T(8,128)(2,1)S(1)} %get-tuple-element.25), channel_id=1, source_target_pairs={{0,1},{1,0},{2,3},{3,2},{4,5},{5,4},{6,7},{7,6},{8,9},{9,8},{10,11... | collective-permute-start | bytes 1572872 | tf_op jit(solution)/shard_map/ppermute | solution.py:346
  109.2 1.5 collective-permute-start.16
  112.4 22.9 %copy-start.1 = (f32[256,128]{1,0:T(8,128)S(1)}, f32[256,128]{1,0:T(8,128)}, u32[]{:S(2)}) copy-start(f32[256,128]{1,0:T(8,128)} %get-tuple-element.28) | copy-start | bytes 393220
  161.9 6.0 %collective-permute-start.17 = (bf16[8,256,128]{2,1,0:T(8,128)(2,1)S(1)}, bf16[8,256,128]{2,1,0:T(8,128)(2,1)S(1)}, u32[]{:S(2)}, u32[]{:S(2)}) collective-permute-start(bf16[8,256,128]{2,1,0:T(8,128)(2,1)S(1)} %get-tuple-element.30), channel_id=1, source_target_pairs={{0,1},{1,0},{2,3},{3,2},{4,5},{5,4},{6,7},{7,6},{8,9},{9,8},{10,11... | collective-permute-start | bytes 1572872 | tf_op jit(solution)/shard_map/ppermute | solution.py:346
  209.1 5.3 %collective-permute-start.18 = (bf16[8,256,128]{2,1,0:T(8,128)(2,1)S(1)}, bf16[8,256,128]{2,1,0:T(8,128)(2,1)S(1)}, u32[]{:S(2)}, u32[]{:S(2)}) collective-permute-start(bf16[8,256,128]{2,1,0:T(8,128)(2,1)S(1)} %get-tuple-element.32), channel_id=1, source_target_pairs={{0,1},{1,0},{2,3},{3,2},{4,5},{5,4},{6,7},{7,6},{8,9},{9,8},{10,11... | collective-permute-start | bytes 1572872 | tf_op jit(solution)/shard_map/ppermute | solution.py:346
  (2 other events, 11.8 us)
Sparse Core Ops, SparseCore 0:
  9.8 85.2 all-gather.1

commit v8 on v7

--- a/solution.py
+++ b/solution.py
@@ -62,7 +62,7 @@
 
 def weights_kernel(pairs, meta, starts, *refs):
     rows = refs[:ROWS]
-    (cols, row_sq, col_sq, weights, keep, send, degree_keep, degree_send,
+    (cols, row_sq, col_sq, weights, keep, send,
      col_buf, row_buf, tile_buf, label_raw, labels, total, degree, inner_even, inner_odd,
      col_sem, row_sem, tile_sem, label_sem) = refs[ROWS:]
     live = starts[BLOCKS]
@@ -201,12 +201,23 @@
                 cols.at[0, :, 0, pl.ds(0, PIECE)], col_buf.at[j], col_sem.at[j]
             ).wait()
 
-    split_rows(z, total, keep, send)
     half_rows = ROWS // 2
+    tasks = labels.shape[1]
+    line = lax.broadcasted_iota(jnp.int32, (EXTRA, PIECE), 0)
+
+    def degree_lines(where, first):
+        whole = degree[pl.ds(where, 1), :]
+        high = whole.astype(jnp.bfloat16).astype(jnp.float32)
+        return jnp.where(
+            line == first, high, jnp.where(line == first + 1, whole - high, 0.0)
+        )
+
     for piece in range(half_rows):
         place = lax.rem(z - piece + half_rows, half_rows)
-        degree_keep[piece:piece + 1, :] = degree[pl.ds(place, 1), :]
-        degree_send[piece:piece + 1, :] = degree[pl.ds(half_rows + place, 1), :]
+        keep[piece, :tasks, :] = total[place]
+        keep[piece, tasks:, :] = degree_lines(place, 0)
+        send[piece, :tasks, :] = total[half_rows + place].astype(jnp.bfloat16)
+        send[piece, tasks:, :] = degree_lines(half_rows + place, 2).astype(jnp.bfloat16)
 
     def finish(q, carry):
         tile_copy(pairs[2 * q]).wait()
@@ -230,13 +241,11 @@
         weights_kernel,
         out_shape=(
             jax.ShapeDtypeStruct((TILES, WIDTH, PIECE), jnp.bfloat16),
-            jax.ShapeDtypeStruct((ROWS // 2, tasks, PIECE), jnp.float32),
-            jax.ShapeDtypeStruct((ROWS // 2, tasks, PIECE), jnp.bfloat16),
-            jax.ShapeDtypeStruct((ROWS // 2, PIECE), jnp.float32),
-            jax.ShapeDtypeStruct((ROWS // 2, PIECE), jnp.float32),
+            jax.ShapeDtypeStruct((ROWS // 2, tasks + EXTRA, PIECE), jnp.float32),
+            jax.ShapeDtypeStruct((ROWS // 2, tasks + EXTRA, PIECE), jnp.bfloat16),
         ),
         in_specs=[smem, smem, smem] + [hbm] * ROWS + [hbm, vmem, vmem],
-        out_specs=(hbm, vmem, vmem, vmem, vmem),
+        out_specs=(hbm, vmem, vmem),
         scratch_shapes=[
             pltpu.VMEM((BLOCKS, WIDTH // PIECE, PIECE, depth), jnp.bfloat16),
             pltpu.VMEM((3, 2 * PIECE, depth), jnp.bfloat16),
@@ -408,25 +417,18 @@
     own_offset = ((y % 2) * 2 + xh) * PIECE
     meta = jnp.stack([jnp.sum(flat), own_offset, own_tile, z]).astype(jnp.int32)
 
-    weights, keep, send, degree_keep, degree_send = build_weights(
+    weights, keep, send = build_weights(
         pairs, meta, starts, rows, cols, row_sq, col_sq
     )
-    degree_sum = degree_keep + swap_cores(degree_send)
-    high = lax.reduce_precision(degree_sum, 8, 7)
-    low = degree_sum - high
-    degree_rows = jnp.stack([high, low], axis=1).astype(jnp.bfloat16)
-    degree_rows = jnp.concatenate([degree_rows, jnp.zeros((8, 14, PIECE), jnp.bfloat16)], axis=1)
 
     for iteration in range(ITERS):
         if iteration > 0:
             keep, send = spread_rows(pairs, meta, starts, weights, gathered)
         part = (keep + swap_cores(send).astype(jnp.float32)).astype(jnp.bfloat16)
-        if iteration == 0:
-            part = jnp.concatenate([part, degree_rows], axis=1)
         parts = lax.all_to_all(part, "z", 0, 0)
         summed = jnp.sum(parts.astype(jnp.float32), axis=0)
         if iteration == 0:
-            degree_own = summed[tasks] + summed[tasks + 1]
+            degree_own = jnp.sum(summed[tasks:tasks + 4], axis=0)
             summed = summed[:tasks]
         labels = (PROPAGATE * summed / degree_own[None, :] + ANCHOR * seeded).astype(jnp.bfloat16)
         if iteration < ITERS - 1:

time: 242 us -> 242 us (level)
  starting transfers between devices: 48.1 us -> 37.2 us
  Pallas kernels: 15.8 us -> 25.1 us
  waiting for transfers between devices: 47.7 us -> 51.6 us
    ppermute x12 -> x11, starting transfers between devices: 23.7 us -> 16.7 us  [swap_cores(): return lax.ppermute(value, 'core', [(0, 1), (1, 0)])]
    pallas_call x1, Pallas kernels: 8.77 us -> 15.2 us  [build_weights(): pl.pallas_call(weights_kernel, out_shape=(jax.ShapeDtypeStruct((TILES, WI...]
    all_to_all x2, blocking collectives: 41.8 us -> 36 us  [gather_pieces(): return lax.all_to_all(copies, PLANE, 0, 0)]
    ppermute x4, starting transfers between devices: 6.69 us -> 1.53 us  [body(): lax.ppermute(upward[-1], 'z', [(i, (i + 1) % 8) for i in range(8)])]
    all_to_all x1, waiting for transfers between devices: 7.85 us -> 11.4 us  [body(): info = lax.all_to_all(info, ('core', 'z'), 0, 0)[:, 0]]
    all_to_all x3, blocking collectives: 63.6 us -> 66.7 us  [body(): parts = lax.all_to_all(part, 'z', 0, 0)]
    ppermute x3, starting transfers between devices: 5.04 us -> 8.09 us  [body(): lax.ppermute(downward[-1], 'z', [(i, (i + 7) % 8) for i in range(8)])]
    pallas_call x2, Pallas kernels: 4.93 us -> 7.86 us  [spread_rows(): pl.pallas_call(spread_kernel, out_shape=(jax.ShapeDtypeStruct((ROWS // 2,...]
  transfers between devices with their start and end apart: 22 -> 21, of which waited for: 9 -> 9; matrix products, arithmetic and copies ran while one was open for 4% -> 4% of each run, Pallas kernels for 0% -> 0%
where the time goes in v8:
time: 242 us
  blocking collectives  103 us (43%)
  waiting for transfers between devices  51.6 us (21%)
  starting transfers between devices  37.2 us (15%)
  Pallas kernels  25.1 us (10%)
  between operations  13.6 us (6%)
  other arithmetic  5.97 us (2%)
  local copies, waits for them, and re-layouts  5.62 us (2%)
    all_to_all x3, blocking collectives, body(): parts = lax.all_to_all(part, 'z', 0, 0)  66.7 us
    all_to_all x2, blocking collectives, gather_pieces(): return lax.all_to_all(copies, PLANE, 0, 0)  36 us
    ppermute x4, waiting for transfers between devices, body(): lax.ppermute(upward[-1], 'z', [(i, (i + 1) % 8) for i in range(8)])  27 us
    ppermute x11, starting transfers between devices, swap_cores(): return lax.ppermute(value, 'core', [(0, 1), (1, 0)])  16.7 us
    pallas_call x1, Pallas kernels, build_weights(): pl.pallas_call(weights_kernel, out_shape=(jax.ShapeDtypeStruct((TILES, WI...  15.2 us
    all_to_all x1, waiting for transfers between devices, body(): info = lax.all_to_all(info, ('core', 'z'), 0, 0)[:, 0]  11.4 us
    ppermute x3, starting transfers between devices, body(): lax.ppermute(downward[-1], 'z', [(i, (i + 7) % 8) for i in range(8)])  8.09 us
    pallas_call x2, Pallas kernels, spread_rows(): pl.pallas_call(spread_kernel, out_shape=(jax.ShapeDtypeStruct((ROWS // 2,...  7.86 us
  transfers between devices with their start and end apart: 21, of which 9 were waited for; matrix products, arithmetic and copies ran while one was open for 4% of the time, Pallas kernels for 0%

profile of v8, /device:TPU:1, one launch (start us, length us, event | category | flops | bytes accessed | tf_op | source)
XLA Modules:
  0.0 241.9 jit_solution(13945836894990691146)
XLA Ops:
  6.5 2.1 prepare.1
  8.7 3.3 %collective-permute-start.7 = (bf16[128,2048]{1,0:T(8,128)(2,1)S(1)}, bf16[128,2048]{1,0:T(8,128)(2,1)S(1)}, u32[]{:S(2)}, u32[]{:S(2)}) collective-permute-start(bf16[128,2048]{1,0:T(8,128)(2,1)S(1)} %copy-done), channel_id=1, source_target_pairs={{0,1},{1,0},{2,3},{3,2},{4,5},{5,4},{6,7},{7,6},{8,9},{9,8},{10,11... | collective-permute-start | bytes 1572872 | tf_op jit(solution)/shard_map/ppermute | solution.py:355
  12.0 3.9 %collective-permute-start.4 = (bf16[128,2048]{1,0:T(8,128)(2,1)S(1)}, bf16[128,2048]{1,0:T(8,128)(2,1)S(1)}, u32[]{:S(2)}, u32[]{:S(2)}) collective-permute-start(bf16[128,2048]{1,0:T(8,128)(2,1)S(1)} %copy-done), channel_id=1, source_target_pairs={{0,28},{4,0},{8,4},{12,8},{16,12},{20,16},{24,20},{28,24},{1,29},{... | collective-permute-start | bytes 1572872 | tf_op jit(solution)/shard_map/ppermute | solution.py:377
  17.0 5.0 %all-to-all-start = ((f32[16,8,256]{2,1,0:T(8,128)}), f32[16,8,256]{2,1,0:T(8,128)S(1)}, u32[]{:S(2)}, u32[]{:S(2)}) async-start(f32[16,8,256]{2,1,0:T(8,128)} %broadcast_in_dim.60), calls=%async_computation | async-start | bytes 262144 | tf_op jit(solution)/shard_map/all_to_all | solution.py:385
  22.2 11.4 %all-to-all-done = f32[16,8,256]{2,1,0:T(8,128)S(1)} async-done(((f32[16,8,256]{2,1,0:T(8,128)}), f32[16,8,256]{2,1,0:T(8,128)S(1)}, u32[]{:S(2)}, u32[]{:S(2)}) %all-to-all-start) | async-done | bytes 131104 | tf_op jit(solution)/shard_map/all_to_all | solution.py:385
  37.2 11.3 %collective-permute-done.1.refs_2_ = bf16[128,2048]{1,0:T(8,128)(2,1)S(1)} collective-permute-done((bf16[128,2048]{1,0:T(8,128)(2,1)S(1)}, bf16[128,2048]{1,0:T(8,128)(2,1)S(1)}, u32[]{:S(2)}, u32[]{:S(2)}) %collective-permute-start.1) | collective-permute-done | bytes 524320 | tf_op jit(solution)/shard_map/ppermute | solution.py:374
  51.4 2.7 %collective-permute-start.6 = (bf16[128,2048]{1,0:T(8,128)(2,1)S(1)}, bf16[128,2048]{1,0:T(8,128)(2,1)}, u32[]{:S(2)}, u32[]{:S(2)}) collective-permute-start(bf16[128,2048]{1,0:T(8,128)(2,1)S(1)} %collective-permute-done.5.refs_6_), channel_id=1, source_target_pairs={{0,28},{4,0},{8,4},{12,8},{16,12},{20,16},{24,20},{28,24},{1,29},{... | collective-permute-start | bytes 1572872 | tf_op jit(solution)/shard_map/ppermute | solution.py:377
  54.1 7.8 %collective-permute-done.2.refs_3_ = bf16[128,2048]{1,0:T(8,128)(2,1)} collective-permute-done((bf16[128,2048]{1,0:T(8,128)(2,1)S(1)}, bf16[128,2048]{1,0:T(8,128)(2,1)}, u32[]{:S(2)}, u32[]{:S(2)}) %collective-permute-start.2) | collective-permute-done | bytes 524320 | tf_op jit(solution)/shard_map/ppermute | solution.py:374
  63.8 2.3 collective-permute-start.13
  66.8 7.9 %collective-permute-done.3.refs_4_ = bf16[128,2048]{1,0:T(8,128)(2,1)} collective-permute-done((bf16[128,2048]{1,0:T(8,128)(2,1)}, bf16[128,2048]{1,0:T(8,128)(2,1)}, u32[]{:S(2)}, u32[]{:S(2)}) %collective-permute-start.3) | collective-permute-done | bytes 524320 | tf_op jit(solution)/shard_map/ppermute | solution.py:374
  74.6 3.2 %collective-permute-start.11 = (bf16[128,2048]{1,0:T(8,128)(2,1)}, bf16[128,2048]{1,0:T(8,128)(2,1)}, u32[]{:S(2)}, u32[]{:S(2)}) collective-permute-start(bf16[128,2048]{1,0:T(8,128)(2,1)} %collective-permute-done.3.refs_4_), channel_id=1, source_target_pairs={{0,1},{1,0},{2,3},{3,2},{4,5},{5,4},{6,7},{7,6},{8,9},{9,8},{10,11... | collective-permute-start | bytes 1572872 | tf_op jit(solution)/shard_map/ppermute | solution.py:355
  78.5 5.8 %all-to-all-start.1 = ((f32[16,8,128]{2,1,0:T(8,128)}), f32[16,8,128]{2,1,0:T(8,128)S(1)}, u32[]{:S(2)}, u32[]{:S(2)}) async-start(f32[16,8,128]{2,1,0:T(8,128)} %broadcast_in_dim_broadcast_in_dim_broadcast_in_dim.2), calls=%async_computation.1 | async-start | bytes 131072 | tf_op jit(solution)/shard_map/all_to_all | solution.py:360
  85.1 6.5 %all-to-all-done.1 = f32[16,8,128]{2,1,0:T(8,128)S(1)} async-done(((f32[16,8,128]{2,1,0:T(8,128)}), f32[16,8,128]{2,1,0:T(8,128)S(1)}, u32[]{:S(2)}, u32[]{:S(2)}) %all-to-all-start.1) | async-done | bytes 65568 | tf_op jit(solution)/shard_map/all_to_all | solution.py:360
  95.1 15.2 %weights.1 = (bf16[64,512,128]{2,1,0:T(8,128)(2,1)}, f32[8,272,128]{2,1,0:T(8,128)}, bf16[8,272,128]{2,1,0:T(8,128)(2,1)}) custom-call(s32[72]{0:T(128)S(1)} %select_reduce_fusion.pairs, s32[4]{0:T(128)S(1)} %pad_add_fusion.meta, s32[5]{0:T(128)S(1)} %and_select_fusion.starts, bf16[128,2048]{1,0:T(8,128)(2,1)S(1)} %copy-done, ...), custom_call_target="tpu_custom_call" | custom-call | flops 4294967296 | bytes 16777216 | tf_op jit(solution)/shard_map/weights/pallas_call | solution.py:240
  110.4 2.1 collective-permute-done.15
  113.9 26.0 %all_to_all.35 = bf16[8,272,128]{2,1,0:T(8,128)(2,1)S(1)} all-to-all(bf16[8,272,128]{2,1,0:T(8,128)(2,1)S(1)} %add_convert_fusion), channel_id=1, replica_groups=mesh['y'=4,'xh'=2,'z'=8,'xl'=2,'core'=2] {'z'}, dimensions={0} | all-to-all | bytes 1114112 | tf_op jit(solution)/shard_map/all_to_all | solution.py:428
  140.2 18.2 %all_to_all.36.pieces = bf16[16,256,128]{2,1,0:T(8,128)(2,1)S(1)} all-to-all(bf16[16,256,128]{2,1,0:T(8,128)(2,1)S(1)} %broadcast_in_dim.110), channel_id=1, replica_groups=mesh['y'=4,'xh'=2,'z'=8,'xl'=2,'core'=2] {'xl','y','xh'}, dimensions={0} | all-to-all | bytes 2097152 | tf_op jit(solution)/shard_map/all_to_all | solution.py:360
  158.4 3.9 %spread.2 = (f32[8,256,128]{2,1,0:T(8,128)S(1)}, bf16[8,256,128]{2,1,0:T(8,128)(2,1)S(1)}) custom-call(s32[72]{0:T(128)S(1)} %select_reduce_fusion.pairs, s32[4]{0:T(128)S(1)} %pad_add_fusion.meta, s32[5]{0:T(128)S(1)} %and_select_fusion.starts, bf16[64,512,128]{2,1,0:T(8,128)(2,1)} %get-tuple-element.21.weights, bf16[16,256,128]{2,1,0:T(8,128)(2,1)S(1)} %all_to_all.36.pieces), custom_call_target="tpu_custom_call" | custom-call | tf_op jit(solution)/shard_map/spread/pallas_call | solution.py:336
  162.4 3.2 %collective-permute-start.16 = (bf16[8,256,128]{2,1,0:T(8,128)(2,1)S(1)}, bf16[8,256,128]{2,1,0:T(8,128)(2,1)S(1)}, u32[]{:S(2)}, u32[]{:S(2)}) collective-permute-start(bf16[8,256,128]{2,1,0:T(8,128)(2,1)S(1)} %get-tuple-element.26), channel_id=1, source_target_pairs={{0,1},{1,0},{2,3},{3,2},{4,5},{5,4},{6,7},{7,6},{8,9},{9,8},{10,11... | collective-permute-start | bytes 1572872 | tf_op jit(solution)/shard_map/ppermute | solution.py:355
  167.2 20.4 %all_to_all.37 = bf16[8,256,128]{2,1,0:T(8,128)(2,1)S(1)} all-to-all(bf16[8,256,128]{2,1,0:T(8,128)(2,1)S(1)} %add_convert_fusion.2), channel_id=1, replica_groups=mesh['y'=4,'xh'=2,'z'=8,'xl'=2,'core'=2] {'z'}, dimensions={0} | all-to-all | bytes 1048576 | tf_op jit(solution)/shard_map/all_to_all | solution.py:428
  187.9 17.8 %all_to_all.38.pieces = bf16[16,256,128]{2,1,0:T(8,128)(2,1)S(1)} all-to-all(bf16[16,256,128]{2,1,0:T(8,128)(2,1)S(1)} %broadcast_in_dim.111), channel_id=1, replica_groups=mesh['y'=4,'xh'=2,'z'=8,'xl'=2,'core'=2] {'xl','y','xh'}, dimensions={0} | all-to-all | bytes 2097152 | tf_op jit(solution)/shard_map/all_to_all | solution.py:360
  205.7 3.9 %spread.3 = (f32[8,256,128]{2,1,0:T(8,128)S(1)}, bf16[8,256,128]{2,1,0:T(8,128)(2,1)S(1)}) custom-call(s32[72]{0:T(128)S(1)} %select_reduce_fusion.pairs, s32[4]{0:T(128)S(1)} %pad_add_fusion.meta, s32[5]{0:T(128)S(1)} %and_select_fusion.starts, bf16[64,512,128]{2,1,0:T(8,128)(2,1)} %get-tuple-element.21.weights, bf16[16,256,128]{2,1,0:T(8,128)(2,1)S(1)} %all_to_all.38.pieces), custom_call_target="tpu_custom_call" | custom-call | tf_op jit(solution)/shard_map/spread/pallas_call | solution.py:336
  209.7 2.5 %collective-permute-start.17 = (bf16[8,256,128]{2,1,0:T(8,128)(2,1)S(1)}, bf16[8,256,128]{2,1,0:T(8,128)(2,1)S(1)}, u32[]{:S(2)}, u32[]{:S(2)}) collective-permute-start(bf16[8,256,128]{2,1,0:T(8,128)(2,1)S(1)} %get-tuple-element.28), channel_id=1, source_target_pairs={{0,1},{1,0},{2,3},{3,2},{4,5},{5,4},{6,7},{7,6},{8,9},{9,8},{10,11... | collective-permute-start | bytes 1572872 | tf_op jit(solution)/shard_map/ppermute | solution.py:355
  213.8 20.4 %all_to_all.39 = bf16[8,256,128]{2,1,0:T(8,128)(2,1)S(1)} all-to-all(bf16[8,256,128]{2,1,0:T(8,128)(2,1)S(1)} %add_convert_fusion.1), channel_id=1, replica_groups=mesh['y'=4,'xh'=2,'z'=8,'xl'=2,'core'=2] {'z'}, dimensions={0} | all-to-all | bytes 1048576 | tf_op jit(solution)/shard_map/all_to_all | solution.py:428
  (91 shorter events, 21.6 us)
Async XLA Ops:
  6.5 9.3 %copy-start.3 = (s32[2]{0:T(128)S(1)}, s32[2]{0:T(128)}, u32[]{:S(2)}) copy-start(s32[2]{0:T(128)} %param.9) | copy-start | bytes 28
  6.5 9.4 %copy-start.2 = (s32[2,24]{1,0:T(2,128)S(1)}, s32[2,24]{1,0:T(2,128)}, u32[]{:S(2)}) copy-start(s32[2,24]{1,0:T(2,128)} %param.8) | copy-start | bytes 580
  6.5 88.6 %all-gather.2.cloned.1.call-start = ((), (), s32[]{:S(2)}) async-start(), calls=%async_computation.7 | async-start | bytes 10027008 | tf_op jit(solution)/shard_map/all_gather | solution.py:369
  8.7 55.1 %collective-permute-start.7 = (bf16[128,2048]{1,0:T(8,128)(2,1)S(1)}, bf16[128,2048]{1,0:T(8,128)(2,1)S(1)}, u32[]{:S(2)}, u32[]{:S(2)}) collective-permute-start(bf16[128,2048]{1,0:T(8,128)(2,1)S(1)} %copy-done), channel_id=1, source_target_pairs={{0,1},{1,0},{2,3},{3,2},{4,5},{5,4},{6,7},{7,6},{8,9},{9,8},{10,11... | collective-permute-start | bytes 1572872 | tf_op jit(solution)/shard_map/ppermute | solution.py:355
  12.0 23.7 %collective-permute-start.4 = (bf16[128,2048]{1,0:T(8,128)(2,1)S(1)}, bf16[128,2048]{1,0:T(8,128)(2,1)S(1)}, u32[]{:S(2)}, u32[]{:S(2)}) collective-permute-start(bf16[128,2048]{1,0:T(8,128)(2,1)S(1)} %copy-done), channel_id=1, source_target_pairs={{0,28},{4,0},{8,4},{12,8},{16,12},{20,16},{24,20},{28,24},{1,29},{... | collective-permute-start | bytes 1572872 | tf_op jit(solution)/shard_map/ppermute | solution.py:377
  15.9 18.3 %collective-permute-start = (bf16[128,2048]{1,0:T(8,128)(2,1)S(1)}, bf16[128,2048]{1,0:T(8,128)(2,1)S(1)}, u32[]{:S(2)}, u32[]{:S(2)}) collective-permute-start(bf16[128,2048]{1,0:T(8,128)(2,1)S(1)} %copy-done), channel_id=1, source_target_pairs={{0,4},{4,8},{8,12},{12,16},{16,20},{20,24},{24,28},{28,0},{1,5},{5... | collective-permute-start | bytes 1572872 | tf_op jit(solution)/shard_map/ppermute | solution.py:374
  17.0 16.5 %all-to-all-start = ((f32[16,8,256]{2,1,0:T(8,128)}), f32[16,8,256]{2,1,0:T(8,128)S(1)}, u32[]{:S(2)}, u32[]{:S(2)}) async-start(f32[16,8,256]{2,1,0:T(8,128)} %broadcast_in_dim.60), calls=%async_computation | async-start | bytes 262144 | tf_op jit(solution)/shard_map/all_to_all | solution.py:385
  34.2 14.3 %collective-permute-start.1 = (bf16[128,2048]{1,0:T(8,128)(2,1)S(1)}, bf16[128,2048]{1,0:T(8,128)(2,1)S(1)}, u32[]{:S(2)}, u32[]{:S(2)}) collective-permute-start(bf16[128,2048]{1,0:T(8,128)(2,1)S(1)} %collective-permute-done.refs_1_), channel_id=1, source_target_pairs={{0,4},{4,8},{8,12},{12,16},{16,20},{20,24},{24,28},{28,0},{1,5},{5... | collective-permute-start | bytes 1572872 | tf_op jit(solution)/shard_map/ppermute | solution.py:374
  35.7 15.7 %collective-permute-start.5 = (bf16[128,2048]{1,0:T(8,128)(2,1)S(1)}, bf16[128,2048]{1,0:T(8,128)(2,1)S(1)}, u32[]{:S(2)}, u32[]{:S(2)}) collective-permute-start(bf16[128,2048]{1,0:T(8,128)(2,1)S(1)} %collective-permute-done.4.refs_7_), channel_id=1, source_target_pairs={{0,28},{4,0},{8,4},{12,8},{16,12},{20,16},{24,20},{28,24},{1,29},{... | collective-permute-start | bytes 1572872 | tf_op jit(solution)/shard_map/ppermute | solution.py:377
  48.5 13.4 %collective-permute-start.2 = (bf16[128,2048]{1,0:T(8,128)(2,1)S(1)}, bf16[128,2048]{1,0:T(8,128)(2,1)}, u32[]{:S(2)}, u32[]{:S(2)}) collective-permute-start(bf16[128,2048]{1,0:T(8,128)(2,1)S(1)} %collective-permute-done.1.refs_2_), channel_id=1, source_target_pairs={{0,4},{4,8},{8,12},{12,16},{16,20},{20,24},{24,28},{28,0},{1,5},{5... | collective-permute-start | bytes 1572872 | tf_op jit(solution)/shard_map/ppermute | solution.py:374
  49.9 16.2 %collective-permute-start.14 = (bf16[128,2048]{1,0:T(8,128)(2,1)S(1)}, bf16[128,2048]{1,0:T(8,128)(2,1)}, u32[]{:S(2)}, u32[]{:S(2)}) collective-permute-start(bf16[128,2048]{1,0:T(8,128)(2,1)S(1)} %collective-permute-done.4.refs_7_), channel_id=1, source_target_pairs={{0,1},{1,0},{2,3},{3,2},{4,5},{5,4},{6,7},{7,6},{8,9},{9,8},{10,11... | collective-permute-start | bytes 1572872 | tf_op jit(solution)/shard_map/ppermute | solution.py:355
  51.3 14.9 %collective-permute-start.8 = (bf16[128,2048]{1,0:T(8,128)(2,1)S(1)}, bf16[128,2048]{1,0:T(8,128)(2,1)}, u32[]{:S(2)}, u32[]{:S(2)}) collective-permute-start(bf16[128,2048]{1,0:T(8,128)(2,1)S(1)} %collective-permute-done.refs_1_), channel_id=1, source_target_pairs={{0,1},{1,0},{2,3},{3,2},{4,5},{5,4},{6,7},{7,6},{8,9},{9,8},{10,11... | collective-permute-start | bytes 1572872 | tf_op jit(solution)/shard_map/ppermute | solution.py:355
  51.4 15.2 %collective-permute-start.6 = (bf16[128,2048]{1,0:T(8,128)(2,1)S(1)}, bf16[128,2048]{1,0:T(8,128)(2,1)}, u32[]{:S(2)}, u32[]{:S(2)}) collective-permute-start(bf16[128,2048]{1,0:T(8,128)(2,1)S(1)} %collective-permute-done.5.refs_6_), channel_id=1, source_target_pairs={{0,28},{4,0},{8,4},{12,8},{16,12},{20,16},{24,20},{28,24},{1,29},{... | collective-permute-start | bytes 1572872 | tf_op jit(solution)/shard_map/ppermute | solution.py:377
  61.9 12.7 %collective-permute-start.3 = (bf16[128,2048]{1,0:T(8,128)(2,1)}, bf16[128,2048]{1,0:T(8,128)(2,1)}, u32[]{:S(2)}, u32[]{:S(2)}) collective-permute-start(bf16[128,2048]{1,0:T(8,128)(2,1)} %collective-permute-done.2.refs_3_), channel_id=1, source_target_pairs={{0,4},{4,8},{8,12},{12,16},{16,20},{20,24},{24,28},{28,0},{1,5},{5... | collective-permute-start | bytes 1572872 | tf_op jit(solution)/shard_map/ppermute | solution.py:374
  63.8 29.7 %collective-permute-start.13 = (bf16[128,2048]{1,0:T(8,128)(2,1)S(1)}, bf16[128,2048]{1,0:T(8,128)(2,1)}, u32[]{:S(2)}, u32[]{:S(2)}) collective-permute-start(bf16[128,2048]{1,0:T(8,128)(2,1)S(1)} %collective-permute-done.5.refs_6_), channel_id=1, source_target_pairs={{0,1},{1,0},{2,3},{3,2},{4,5},{5,4},{6,7},{7,6},{8,9},{9,8},{10,11... | collective-permute-start | bytes 1572872 | tf_op jit(solution)/shard_map/ppermute | solution.py:355
  66.1 27.4 %collective-permute-start.9 = (bf16[128,2048]{1,0:T(8,128)(2,1)S(1)}, bf16[128,2048]{1,0:T(8,128)(2,1)}, u32[]{:S(2)}, u32[]{:S(2)}) collective-permute-start(bf16[128,2048]{1,0:T(8,128)(2,1)S(1)} %collective-permute-done.1.refs_2_), channel_id=1, source_target_pairs={{0,1},{1,0},{2,3},{3,2},{4,5},{5,4},{6,7},{7,6},{8,9},{9,8},{10,11... | collective-permute-start | bytes 1572872 | tf_op jit(solution)/shard_map/ppermute | solution.py:355
  66.2 27.3 %collective-permute-start.10 = (bf16[128,2048]{1,0:T(8,128)(2,1)}, bf16[128,2048]{1,0:T(8,128)(2,1)}, u32[]{:S(2)}, u32[]{:S(2)}) collective-permute-start(bf16[128,2048]{1,0:T(8,128)(2,1)} %collective-permute-done.2.refs_3_), channel_id=1, source_target_pairs={{0,1},{1,0},{2,3},{3,2},{4,5},{5,4},{6,7},{7,6},{8,9},{9,8},{10,11... | collective-permute-start | bytes 1572872 | tf_op jit(solution)/shard_map/ppermute | solution.py:355
  66.6 26.9 %collective-permute-start.12 = (bf16[128,2048]{1,0:T(8,128)(2,1)}, bf16[128,2048]{1,0:T(8,128)(2,1)}, u32[]{:S(2)}, u32[]{:S(2)}) collective-permute-start(bf16[128,2048]{1,0:T(8,128)(2,1)} %collective-permute-done.6.refs_5_), channel_id=1, source_target_pairs={{0,1},{1,0},{2,3},{3,2},{4,5},{5,4},{6,7},{7,6},{8,9},{9,8},{10,11... | collective-permute-start | bytes 1572872 | tf_op jit(solution)/shard_map/ppermute | solution.py:355
  74.6 18.9 %collective-permute-start.11 = (bf16[128,2048]{1,0:T(8,128)(2,1)}, bf16[128,2048]{1,0:T(8,128)(2,1)}, u32[]{:S(2)}, u32[]{:S(2)}) collective-permute-start(bf16[128,2048]{1,0:T(8,128)(2,1)} %collective-permute-done.3.refs_4_), channel_id=1, source_target_pairs={{0,1},{1,0},{2,3},{3,2},{4,5},{5,4},{6,7},{7,6},{8,9},{9,8},{10,11... | collective-permute-start | bytes 1572872 | tf_op jit(solution)/shard_map/ppermute | solution.py:355
  78.5 13.1 %all-to-all-start.1 = ((f32[16,8,128]{2,1,0:T(8,128)}), f32[16,8,128]{2,1,0:T(8,128)S(1)}, u32[]{:S(2)}, u32[]{:S(2)}) async-start(f32[16,8,128]{2,1,0:T(8,128)} %broadcast_in_dim_broadcast_in_dim_broadcast_in_dim.2), calls=%async_computation.1 | async-start | bytes 131072 | tf_op jit(solution)/shard_map/all_to_all | solution.py:360
  110.3 2.3 collective-permute-start.15
  113.9 26.1 %copy-start.1 = (f32[256,128]{1,0:T(8,128)S(1)}, f32[256,128]{1,0:T(8,128)}, u32[]{:S(2)}) copy-start(f32[256,128]{1,0:T(8,128)} %get-tuple-element.24) | copy-start | bytes 393220
  162.4 4.7 %collective-permute-start.16 = (bf16[8,256,128]{2,1,0:T(8,128)(2,1)S(1)}, bf16[8,256,128]{2,1,0:T(8,128)(2,1)S(1)}, u32[]{:S(2)}, u32[]{:S(2)}) collective-permute-start(bf16[8,256,128]{2,1,0:T(8,128)(2,1)S(1)} %get-tuple-element.26), channel_id=1, source_target_pairs={{0,1},{1,0},{2,3},{3,2},{4,5},{5,4},{6,7},{7,6},{8,9},{9,8},{10,11... | collective-permute-start | bytes 1572872 | tf_op jit(solution)/shard_map/ppermute | solution.py:355
  209.7 4.0 %collective-permute-start.17 = (bf16[8,256,128]{2,1,0:T(8,128)(2,1)S(1)}, bf16[8,256,128]{2,1,0:T(8,128)(2,1)S(1)}, u32[]{:S(2)}, u32[]{:S(2)}) collective-permute-start(bf16[8,256,128]{2,1,0:T(8,128)(2,1)S(1)} %get-tuple-element.28), channel_id=1, source_target_pairs={{0,1},{1,0},{2,3},{3,2},{4,5},{5,4},{6,7},{7,6},{8,9},{9,8},{10,11... | collective-permute-start | bytes 1572872 | tf_op jit(solution)/shard_map/ppermute | solution.py:355
  (1 other events, 2.1 us)
Sparse Core Ops, SparseCore 0:
  9.8 85.2 all-gather.1

commit v9 on v7

--- a/solution.py
+++ b/solution.py
@@ -144,16 +144,14 @@
         arrive(0)
         inner_even[...] = multiply(0)
 
-    def step(q, current, following):
+    def step(q, current, following, more):
         @pl.when(q + 2 < live)
         def _():
             start_rows(q + 2)
 
-        @pl.when(q + 1 < live)
-        def _():
+        if more:
             arrive(q + 1)
-
-        following[...] = multiply(jnp.minimum(q + 1, live - 1))
+            following[...] = multiply(q + 1)
         one = pairs[2 * q]
         two = pairs[2 * q + 1]
         j = one // ROWS
@@ -185,11 +183,16 @@
             degree[pl.ds(place_two, 1), :] += sums[:, PIECE:]
 
     def steps(i, carry):
-        step(2 * i, inner_even, inner_odd)
-
-        @pl.when(2 * i + 1 < live)
-        def _():
-            step(2 * i + 1, inner_odd, inner_even)
+        for q, current, following in (
+            (2 * i, inner_even, inner_odd), (2 * i + 1, inner_odd, inner_even)
+        ):
+            @pl.when(q + 1 < live)
+            def _():
+                step(q, current, following, True)
+
+            @pl.when(q + 1 == live)
+            def _():
+                step(q, current, following, False)
 
         return carry
 

time: 242 us -> 241 us (level)
  starting transfers between devices: 48.1 us -> 39.7 us
  Pallas kernels: 15.8 us -> 20.1 us
    ppermute x12, starting transfers between devices: 23.7 us -> 15.3 us  [swap_cores(): return lax.ppermute(value, 'core', [(0, 1), (1, 0)])]
    all_to_all x3, blocking collectives: 63.6 us -> 68.1 us  [body(): parts = lax.all_to_all(part, 'z', 0, 0)]
    all_to_all x2, blocking collectives: 41.8 us -> 39 us  [gather_pieces(): return lax.all_to_all(copies, PLANE, 0, 0)]
    pallas_call x1, Pallas kernels: 8.77 us -> 11.6 us  [build_weights(): pl.pallas_call(weights_kernel, out_shape=(jax.ShapeDtypeStruct((TILES, WI...]
where the time goes in v9:
time: 241 us; the launch traced here: 240 us
  blocking collectives  107 us (44%)
  waiting for transfers between devices  47.7 us (20%)
  starting transfers between devices  39.7 us (16%)
  Pallas kernels  20.1 us (8%)
  between operations  13.7 us (6%)
  other arithmetic  6.16 us (3%)
  local copies, waits for them, and re-layouts  5.75 us (2%)
    all_to_all x3, blocking collectives, body(): parts = lax.all_to_all(part, 'z', 0, 0)  68.1 us
    all_to_all x2, blocking collectives, gather_pieces(): return lax.all_to_all(copies, PLANE, 0, 0)  39 us
    ppermute x4, waiting for transfers between devices, body(): lax.ppermute(upward[-1], 'z', [(i, (i + 1) % 8) for i in range(8)])  26.2 us
    ppermute x12, starting transfers between devices, swap_cores(): return lax.ppermute(value, 'core', [(0, 1), (1, 0)])  15.3 us
    pallas_call x1, Pallas kernels, build_weights(): pl.pallas_call(weights_kernel, out_shape=(jax.ShapeDtypeStruct((TILES, WI...  11.6 us
    all_to_all x1, waiting for transfers between devices, body(): info = lax.all_to_all(info, ('core', 'z'), 0, 0)[:, 0]  7.85 us
    all_to_all x1, starting transfers between devices, gather_pieces(): return lax.all_to_all(copies, PLANE, 0, 0)  6.75 us
    ppermute x4, starting transfers between devices, body(): lax.ppermute(upward[-1], 'z', [(i, (i + 1) % 8) for i in range(8)])  6.69 us
  transfers between devices with their start and end apart: 22, of which 9 were waited for; matrix products, arithmetic and copies ran while one was open for 4% of the time, Pallas kernels for 0%

profile of v9, /device:TPU:1, one launch (start us, length us, event | category | flops | bytes accessed | tf_op | source)
XLA Modules:
  0.0 240.0 jit_solution(13854478092206105169)
XLA Ops:
  8.7 2.5 %collective-permute-start = (bf16[128,2048]{1,0:T(8,128)(2,1)S(1)}, bf16[128,2048]{1,0:T(8,128)(2,1)S(1)}, u32[]{:S(2)}, u32[]{:S(2)}) collective-permute-start(bf16[128,2048]{1,0:T(8,128)(2,1)S(1)} %copy-done), channel_id=1, source_target_pairs={{0,4},{4,8},{8,12},{12,16},{16,20},{20,24},{24,28},{28,0},{1,5},{5... | collective-permute-start | bytes 1572872 | tf_op jit(solution)/shard_map/ppermute | solution.py:368
  11.2 4.0 %collective-permute-start.4 = (bf16[128,2048]{1,0:T(8,128)(2,1)S(1)}, bf16[128,2048]{1,0:T(8,128)(2,1)S(1)}, u32[]{:S(2)}, u32[]{:S(2)}) collective-permute-start(bf16[128,2048]{1,0:T(8,128)(2,1)S(1)} %copy-done), channel_id=1, source_target_pairs={{0,28},{4,0},{8,4},{12,8},{16,12},{20,16},{24,20},{28,24},{1,29},{... | collective-permute-start | bytes 1572872 | tf_op jit(solution)/shard_map/ppermute | solution.py:371
  17.4 5.9 %all-to-all-start = ((f32[16,8,256]{2,1,0:T(8,128)}), f32[16,8,256]{2,1,0:T(8,128)S(1)}, u32[]{:S(2)}, u32[]{:S(2)}) async-start(f32[16,8,256]{2,1,0:T(8,128)} %broadcast_in_dim.62), calls=%async_computation | async-start | bytes 262144 | tf_op jit(solution)/shard_map/all_to_all | solution.py:379
  23.4 7.8 %all-to-all-done = f32[16,8,256]{2,1,0:T(8,128)S(1)} async-done(((f32[16,8,256]{2,1,0:T(8,128)}), f32[16,8,256]{2,1,0:T(8,128)S(1)}, u32[]{:S(2)}, u32[]{:S(2)}) %all-to-all-start) | async-done | bytes 131104 | tf_op jit(solution)/shard_map/all_to_all | solution.py:379
  31.9 3.0 %collective-permute-start.1 = (bf16[128,2048]{1,0:T(8,128)(2,1)S(1)}, bf16[128,2048]{1,0:T(8,128)(2,1)S(1)}, u32[]{:S(2)}, u32[]{:S(2)}) collective-permute-start(bf16[128,2048]{1,0:T(8,128)(2,1)S(1)} %collective-permute-done.refs_1_), channel_id=1, source_target_pairs={{0,4},{4,8},{8,12},{12,16},{16,20},{20,24},{24,28},{28,0},{1,5},{5... | collective-permute-start | bytes 1572872 | tf_op jit(solution)/shard_map/ppermute | solution.py:368
  35.2 11.1 %collective-permute-done.1.refs_2_ = bf16[128,2048]{1,0:T(8,128)(2,1)S(1)} collective-permute-done((bf16[128,2048]{1,0:T(8,128)(2,1)S(1)}, bf16[128,2048]{1,0:T(8,128)(2,1)S(1)}, u32[]{:S(2)}, u32[]{:S(2)}) %collective-permute-start.1) | collective-permute-done | bytes 524320 | tf_op jit(solution)/shard_map/ppermute | solution.py:368
  48.7 2.1 collective-permute-start.8
  51.9 7.9 %collective-permute-done.2.refs_3_ = bf16[128,2048]{1,0:T(8,128)(2,1)} collective-permute-done((bf16[128,2048]{1,0:T(8,128)(2,1)S(1)}, bf16[128,2048]{1,0:T(8,128)(2,1)}, u32[]{:S(2)}, u32[]{:S(2)}) %collective-permute-start.2) | collective-permute-done | bytes 524320 | tf_op jit(solution)/shard_map/ppermute | solution.py:368
  61.6 2.5 %collective-permute-start.9 = (bf16[128,2048]{1,0:T(8,128)(2,1)S(1)}, bf16[128,2048]{1,0:T(8,128)(2,1)}, u32[]{:S(2)}, u32[]{:S(2)}) collective-permute-start(bf16[128,2048]{1,0:T(8,128)(2,1)S(1)} %collective-permute-done.1.refs_2_), channel_id=1, source_target_pairs={{0,1},{1,0},{2,3},{3,2},{4,5},{5,4},{6,7},{7,6},{8,9},{9,8},{10,11... | collective-permute-start | bytes 1572872 | tf_op jit(solution)/shard_map/ppermute | solution.py:349
  65.4 7.2 %collective-permute-done.3.refs_4_ = bf16[128,2048]{1,0:T(8,128)(2,1)} collective-permute-done((bf16[128,2048]{1,0:T(8,128)(2,1)}, bf16[128,2048]{1,0:T(8,128)(2,1)}, u32[]{:S(2)}, u32[]{:S(2)}) %collective-permute-start.3) | collective-permute-done | bytes 524320 | tf_op jit(solution)/shard_map/ppermute | solution.py:368
  72.6 3.1 %collective-permute-start.11 = (bf16[128,2048]{1,0:T(8,128)(2,1)}, bf16[128,2048]{1,0:T(8,128)(2,1)}, u32[]{:S(2)}, u32[]{:S(2)}) collective-permute-start(bf16[128,2048]{1,0:T(8,128)(2,1)} %collective-permute-done.3.refs_4_), channel_id=1, source_target_pairs={{0,1},{1,0},{2,3},{3,2},{4,5},{5,4},{6,7},{7,6},{8,9},{9,8},{10,11... | collective-permute-start | bytes 1572872 | tf_op jit(solution)/shard_map/ppermute | solution.py:349
  76.4 6.8 %all-to-all-start.1 = ((f32[16,8,128]{2,1,0:T(8,128)}), f32[16,8,128]{2,1,0:T(8,128)S(1)}, u32[]{:S(2)}, u32[]{:S(2)}) async-start(f32[16,8,128]{2,1,0:T(8,128)} %broadcast_in_dim_broadcast_in_dim_broadcast_in_dim.2), calls=%async_computation.1 | async-start | bytes 131072 | tf_op jit(solution)/shard_map/all_to_all | solution.py:354
  83.9 6.5 %all-to-all-done.1 = f32[16,8,128]{2,1,0:T(8,128)S(1)} async-done(((f32[16,8,128]{2,1,0:T(8,128)}), f32[16,8,128]{2,1,0:T(8,128)S(1)}, u32[]{:S(2)}, u32[]{:S(2)}) %all-to-all-start.1) | async-done | bytes 65568 | tf_op jit(solution)/shard_map/all_to_all | solution.py:354
  92.3 2.7 %all-gather.2.cloned.1.call-done = bf16[2304,2048]{1,0:T(8,128)(2,1)} async-done(((bf16[144,2048]{1,0:T(8,128)(2,1)}), bf16[2304,2048]{1,0:T(8,128)(2,1)}) %all-gather.2.cloned.1.call-update) | async-done | bytes 9437200 | tf_op jit(solution)/shard_map/all_gather | solution.py:363
  95.1 11.6 %weights.1 = (bf16[64,512,128]{2,1,0:T(8,128)(2,1)}, f32[8,256,128]{2,1,0:T(8,128)}, bf16[8,256,128]{2,1,0:T(8,128)(2,1)S(1)}, f32[8,128]{1,0:T(8,128)S(1)}, f32[8,128]{1,0:T(8,128)S(1)}) custom-call(s32[72]{0:T(128)S(1)} %select_reduce_fusion.pairs, s32[4]{0:T(128)S(1)} %pad_add_fusion.meta, s32[5]{0:T(128)S(1)} %and_select_fusion.starts, ...), custom_call_target="tpu_custom_call" | custom-call | flops 4294967296 | bytes 16777216 | tf_op jit(solution)/shard_map/weights/pallas_call | solution.py:232
  110.2 27.3 %all_to_all.35 = bf16[8,272,128]{2,1,0:T(8,128)(2,1)S(1)} all-to-all(bf16[8,272,128]{2,1,0:T(8,128)(2,1)S(1)} %maximum_maximum_fusion), channel_id=1, replica_groups=mesh['y'=4,'xh'=2,'z'=8,'xl'=2,'core'=2] {'z'}, dimensions={0} | all-to-all | bytes 1114112 | tf_op jit(solution)/shard_map/all_to_all | solution.py:429
  137.9 20.5 %all_to_all.36.pieces = bf16[16,256,128]{2,1,0:T(8,128)(2,1)S(1)} all-to-all(bf16[16,256,128]{2,1,0:T(8,128)(2,1)S(1)} %broadcast_in_dim.114), channel_id=1, replica_groups=mesh['y'=4,'xh'=2,'z'=8,'xl'=2,'core'=2] {'xl','y','xh'}, dimensions={0} | all-to-all | bytes 2097152 | tf_op jit(solution)/shard_map/all_to_all | solution.py:354
  158.4 3.2 %spread.2 = (f32[8,256,128]{2,1,0:T(8,128)S(1)}, bf16[8,256,128]{2,1,0:T(8,128)(2,1)S(1)}) custom-call(s32[72]{0:T(128)S(1)} %select_reduce_fusion.pairs, s32[4]{0:T(128)S(1)} %pad_add_fusion.meta, s32[5]{0:T(128)S(1)} %and_select_fusion.starts, bf16[64,512,128]{2,1,0:T(8,128)(2,1)} %get-tuple-element.23.weights, bf16[16,256,128]{2,1,0:T(8,128)(2,1)S(1)} %all_to_all.36.pieces), custom_call_target="tpu_custom_call" | custom-call | tf_op jit(solution)/shard_map/spread/pallas_call | solution.py:330
  161.6 2.5 %collective-permute-start.17 = (bf16[8,256,128]{2,1,0:T(8,128)(2,1)S(1)}, bf16[8,256,128]{2,1,0:T(8,128)(2,1)S(1)}, u32[]{:S(2)}, u32[]{:S(2)}) collective-permute-start(bf16[8,256,128]{2,1,0:T(8,128)(2,1)S(1)} %get-tuple-element.30), channel_id=1, source_target_pairs={{0,1},{1,0},{2,3},{3,2},{4,5},{5,4},{6,7},{7,6},{8,9},{9,8},{10,11... | collective-permute-start | bytes 1572872 | tf_op jit(solution)/shard_map/ppermute | solution.py:349
  165.7 20.4 %all_to_all.37 = bf16[8,256,128]{2,1,0:T(8,128)(2,1)S(1)} all-to-all(bf16[8,256,128]{2,1,0:T(8,128)(2,1)S(1)} %add_convert_fusion.1), channel_id=1, replica_groups=mesh['y'=4,'xh'=2,'z'=8,'xl'=2,'core'=2] {'z'}, dimensions={0} | all-to-all | bytes 1048576 | tf_op jit(solution)/shard_map/all_to_all | solution.py:429
  186.4 18.4 %all_to_all.38.pieces = bf16[16,256,128]{2,1,0:T(8,128)(2,1)S(1)} all-to-all(bf16[16,256,128]{2,1,0:T(8,128)(2,1)S(1)} %broadcast_in_dim.115), channel_id=1, replica_groups=mesh['y'=4,'xh'=2,'z'=8,'xl'=2,'core'=2] {'xl','y','xh'}, dimensions={0} | all-to-all | bytes 2097152 | tf_op jit(solution)/shard_map/all_to_all | solution.py:354
  204.9 3.2 %spread.3 = (f32[8,256,128]{2,1,0:T(8,128)S(1)}, bf16[8,256,128]{2,1,0:T(8,128)(2,1)S(1)}) custom-call(s32[72]{0:T(128)S(1)} %select_reduce_fusion.pairs, s32[4]{0:T(128)S(1)} %pad_add_fusion.meta, s32[5]{0:T(128)S(1)} %and_select_fusion.starts, bf16[64,512,128]{2,1,0:T(8,128)(2,1)} %get-tuple-element.23.weights, bf16[16,256,128]{2,1,0:T(8,128)(2,1)S(1)} %all_to_all.38.pieces), custom_call_target="tpu_custom_call" | custom-call | tf_op jit(solution)/shard_map/spread/pallas_call | solution.py:330
  208.1 2.2 collective-permute-start.18
  212.0 20.4 %all_to_all.39 = bf16[8,256,128]{2,1,0:T(8,128)(2,1)S(1)} all-to-all(bf16[8,256,128]{2,1,0:T(8,128)(2,1)S(1)} %add_convert_fusion), channel_id=1, replica_groups=mesh['y'=4,'xh'=2,'z'=8,'xl'=2,'core'=2] {'z'}, dimensions={0} | all-to-all | bytes 1048576 | tf_op jit(solution)/shard_map/all_to_all | solution.py:429
  (99 shorter events, 23.6 us)
Async XLA Ops:
  6.5 9.8 %copy-start.2 = (s32[2,24]{1,0:T(2,128)S(1)}, s32[2,24]{1,0:T(2,128)}, u32[]{:S(2)}) copy-start(s32[2,24]{1,0:T(2,128)} %param.8) | copy-start | bytes 580
  6.5 88.5 %all-gather.2.cloned.1.call-start = ((), (), s32[]{:S(2)}) async-start(), calls=%async_computation.7 | async-start | bytes 10027008 | tf_op jit(solution)/shard_map/all_gather | solution.py:363
  8.7 23.2 %collective-permute-start = (bf16[128,2048]{1,0:T(8,128)(2,1)S(1)}, bf16[128,2048]{1,0:T(8,128)(2,1)S(1)}, u32[]{:S(2)}, u32[]{:S(2)}) collective-permute-start(bf16[128,2048]{1,0:T(8,128)(2,1)S(1)} %copy-done), channel_id=1, source_target_pairs={{0,4},{4,8},{8,12},{12,16},{16,20},{20,24},{24,28},{28,0},{1,5},{5... | collective-permute-start | bytes 1572872 | tf_op jit(solution)/shard_map/ppermute | solution.py:368
  11.2 23.9 %collective-permute-start.4 = (bf16[128,2048]{1,0:T(8,128)(2,1)S(1)}, bf16[128,2048]{1,0:T(8,128)(2,1)S(1)}, u32[]{:S(2)}, u32[]{:S(2)}) collective-permute-start(bf16[128,2048]{1,0:T(8,128)(2,1)S(1)} %copy-done), channel_id=1, source_target_pairs={{0,28},{4,0},{8,4},{12,8},{16,12},{20,16},{24,20},{28,24},{1,29},{... | collective-permute-start | bytes 1572872 | tf_op jit(solution)/shard_map/ppermute | solution.py:371
  15.2 46.3 %collective-permute-start.7 = (bf16[128,2048]{1,0:T(8,128)(2,1)S(1)}, bf16[128,2048]{1,0:T(8,128)(2,1)S(1)}, u32[]{:S(2)}, u32[]{:S(2)}) collective-permute-start(bf16[128,2048]{1,0:T(8,128)(2,1)S(1)} %copy-done), channel_id=1, source_target_pairs={{0,1},{1,0},{2,3},{3,2},{4,5},{5,4},{6,7},{7,6},{8,9},{9,8},{10,11... | collective-permute-start | bytes 1572872 | tf_op jit(solution)/shard_map/ppermute | solution.py:349
  17.4 13.9 %all-to-all-start = ((f32[16,8,256]{2,1,0:T(8,128)}), f32[16,8,256]{2,1,0:T(8,128)S(1)}, u32[]{:S(2)}, u32[]{:S(2)}) async-start(f32[16,8,256]{2,1,0:T(8,128)} %broadcast_in_dim.62), calls=%async_computation | async-start | bytes 262144 | tf_op jit(solution)/shard_map/all_to_all | solution.py:379
  31.9 14.4 %collective-permute-start.1 = (bf16[128,2048]{1,0:T(8,128)(2,1)S(1)}, bf16[128,2048]{1,0:T(8,128)(2,1)S(1)}, u32[]{:S(2)}, u32[]{:S(2)}) collective-permute-start(bf16[128,2048]{1,0:T(8,128)(2,1)S(1)} %collective-permute-done.refs_1_), channel_id=1, source_target_pairs={{0,4},{4,8},{8,12},{12,16},{16,20},{20,24},{24,28},{28,0},{1,5},{5... | collective-permute-start | bytes 1572872 | tf_op jit(solution)/shard_map/ppermute | solution.py:368
  35.2 15.8 %collective-permute-start.5 = (bf16[128,2048]{1,0:T(8,128)(2,1)S(1)}, bf16[128,2048]{1,0:T(8,128)(2,1)S(1)}, u32[]{:S(2)}, u32[]{:S(2)}) collective-permute-start(bf16[128,2048]{1,0:T(8,128)(2,1)S(1)} %collective-permute-done.4.refs_7_), channel_id=1, source_target_pairs={{0,28},{4,0},{8,4},{12,8},{16,12},{20,16},{24,20},{28,24},{1,29},{... | collective-permute-start | bytes 1572872 | tf_op jit(solution)/shard_map/ppermute | solution.py:371
  46.3 13.5 %collective-permute-start.2 = (bf16[128,2048]{1,0:T(8,128)(2,1)S(1)}, bf16[128,2048]{1,0:T(8,128)(2,1)}, u32[]{:S(2)}, u32[]{:S(2)}) collective-permute-start(bf16[128,2048]{1,0:T(8,128)(2,1)S(1)} %collective-permute-done.1.refs_2_), channel_id=1, source_target_pairs={{0,4},{4,8},{8,12},{12,16},{16,20},{20,24},{24,28},{28,0},{1,5},{5... | collective-permute-start | bytes 1572872 | tf_op jit(solution)/shard_map/ppermute | solution.py:368
  48.7 15.4 %collective-permute-start.8 = (bf16[128,2048]{1,0:T(8,128)(2,1)S(1)}, bf16[128,2048]{1,0:T(8,128)(2,1)}, u32[]{:S(2)}, u32[]{:S(2)}) collective-permute-start(bf16[128,2048]{1,0:T(8,128)(2,1)S(1)} %collective-permute-done.refs_1_), channel_id=1, source_target_pairs={{0,1},{1,0},{2,3},{3,2},{4,5},{5,4},{6,7},{7,6},{8,9},{9,8},{10,11... | collective-permute-start | bytes 1572872 | tf_op jit(solution)/shard_map/ppermute | solution.py:349
  50.8 13.3 %collective-permute-start.14 = (bf16[128,2048]{1,0:T(8,128)(2,1)S(1)}, bf16[128,2048]{1,0:T(8,128)(2,1)}, u32[]{:S(2)}, u32[]{:S(2)}) collective-permute-start(bf16[128,2048]{1,0:T(8,128)(2,1)S(1)} %collective-permute-done.4.refs_7_), channel_id=1, source_target_pairs={{0,1},{1,0},{2,3},{3,2},{4,5},{5,4},{6,7},{7,6},{8,9},{9,8},{10,11... | collective-permute-start | bytes 1572872 | tf_op jit(solution)/shard_map/ppermute | solution.py:349
  50.9 13.6 %collective-permute-start.6 = (bf16[128,2048]{1,0:T(8,128)(2,1)S(1)}, bf16[128,2048]{1,0:T(8,128)(2,1)}, u32[]{:S(2)}, u32[]{:S(2)}) collective-permute-start(bf16[128,2048]{1,0:T(8,128)(2,1)S(1)} %collective-permute-done.5.refs_6_), channel_id=1, source_target_pairs={{0,28},{4,0},{8,4},{12,8},{16,12},{20,16},{24,20},{28,24},{1,29},{... | collective-permute-start | bytes 1572872 | tf_op jit(solution)/shard_map/ppermute | solution.py:371
  59.8 12.8 %collective-permute-start.3 = (bf16[128,2048]{1,0:T(8,128)(2,1)}, bf16[128,2048]{1,0:T(8,128)(2,1)}, u32[]{:S(2)}, u32[]{:S(2)}) collective-permute-start(bf16[128,2048]{1,0:T(8,128)(2,1)} %collective-permute-done.2.refs_3_), channel_id=1, source_target_pairs={{0,4},{4,8},{8,12},{12,16},{16,20},{20,24},{24,28},{28,0},{1,5},{5... | collective-permute-start | bytes 1572872 | tf_op jit(solution)/shard_map/ppermute | solution.py:368
  61.6 30.7 %collective-permute-start.9 = (bf16[128,2048]{1,0:T(8,128)(2,1)S(1)}, bf16[128,2048]{1,0:T(8,128)(2,1)}, u32[]{:S(2)}, u32[]{:S(2)}) collective-permute-start(bf16[128,2048]{1,0:T(8,128)(2,1)S(1)} %collective-permute-done.1.refs_2_), channel_id=1, source_target_pairs={{0,1},{1,0},{2,3},{3,2},{4,5},{5,4},{6,7},{7,6},{8,9},{9,8},{10,11... | collective-permute-start | bytes 1572872 | tf_op jit(solution)/shard_map/ppermute | solution.py:349
  64.0 28.3 %collective-permute-start.13 = (bf16[128,2048]{1,0:T(8,128)(2,1)S(1)}, bf16[128,2048]{1,0:T(8,128)(2,1)}, u32[]{:S(2)}, u32[]{:S(2)}) collective-permute-start(bf16[128,2048]{1,0:T(8,128)(2,1)S(1)} %collective-permute-done.5.refs_6_), channel_id=1, source_target_pairs={{0,1},{1,0},{2,3},{3,2},{4,5},{5,4},{6,7},{7,6},{8,9},{9,8},{10,11... | collective-permute-start | bytes 1572872 | tf_op jit(solution)/shard_map/ppermute | solution.py:349
  64.2 28.2 %collective-permute-start.10 = (bf16[128,2048]{1,0:T(8,128)(2,1)}, bf16[128,2048]{1,0:T(8,128)(2,1)}, u32[]{:S(2)}, u32[]{:S(2)}) collective-permute-start(bf16[128,2048]{1,0:T(8,128)(2,1)} %collective-permute-done.2.refs_3_), channel_id=1, source_target_pairs={{0,1},{1,0},{2,3},{3,2},{4,5},{5,4},{6,7},{7,6},{8,9},{9,8},{10,11... | collective-permute-start | bytes 1572872 | tf_op jit(solution)/shard_map/ppermute | solution.py:349
  64.6 27.8 %collective-permute-start.12 = (bf16[128,2048]{1,0:T(8,128)(2,1)}, bf16[128,2048]{1,0:T(8,128)(2,1)}, u32[]{:S(2)}, u32[]{:S(2)}) collective-permute-start(bf16[128,2048]{1,0:T(8,128)(2,1)} %collective-permute-done.6.refs_5_), channel_id=1, source_target_pairs={{0,1},{1,0},{2,3},{3,2},{4,5},{5,4},{6,7},{7,6},{8,9},{9,8},{10,11... | collective-permute-start | bytes 1572872 | tf_op jit(solution)/shard_map/ppermute | solution.py:349
  72.6 19.8 %collective-permute-start.11 = (bf16[128,2048]{1,0:T(8,128)(2,1)}, bf16[128,2048]{1,0:T(8,128)(2,1)}, u32[]{:S(2)}, u32[]{:S(2)}) collective-permute-start(bf16[128,2048]{1,0:T(8,128)(2,1)} %collective-permute-done.3.refs_4_), channel_id=1, source_target_pairs={{0,1},{1,0},{2,3},{3,2},{4,5},{5,4},{6,7},{7,6},{8,9},{9,8},{10,11... | collective-permute-start | bytes 1572872 | tf_op jit(solution)/shard_map/ppermute | solution.py:349
  76.4 14.0 %all-to-all-start.1 = ((f32[16,8,128]{2,1,0:T(8,128)}), f32[16,8,128]{2,1,0:T(8,128)S(1)}, u32[]{:S(2)}, u32[]{:S(2)}) async-start(f32[16,8,128]{2,1,0:T(8,128)} %broadcast_in_dim_broadcast_in_dim_broadcast_in_dim.2), calls=%async_computation.1 | async-start | bytes 131072 | tf_op jit(solution)/shard_map/all_to_all | solution.py:354
  106.6 2.0 collective-permute-start.15
  106.7 1.9 collective-permute-start.16
  110.2 27.4 %copy-start.1 = (f32[256,128]{1,0:T(8,128)S(1)}, f32[256,128]{1,0:T(8,128)}, u32[]{:S(2)}) copy-start(f32[256,128]{1,0:T(8,128)} %get-tuple-element.28) | copy-start | bytes 393220
  161.6 4.0 %collective-permute-start.17 = (bf16[8,256,128]{2,1,0:T(8,128)(2,1)S(1)}, bf16[8,256,128]{2,1,0:T(8,128)(2,1)S(1)}, u32[]{:S(2)}, u32[]{:S(2)}) collective-permute-start(bf16[8,256,128]{2,1,0:T(8,128)(2,1)S(1)} %get-tuple-element.30), channel_id=1, source_target_pairs={{0,1},{1,0},{2,3},{3,2},{4,5},{5,4},{6,7},{7,6},{8,9},{9,8},{10,11... | collective-permute-start | bytes 1572872 | tf_op jit(solution)/shard_map/ppermute | solution.py:349
  208.1 3.7 %collective-permute-start.18 = (bf16[8,256,128]{2,1,0:T(8,128)(2,1)S(1)}, bf16[8,256,128]{2,1,0:T(8,128)(2,1)S(1)}, u32[]{:S(2)}, u32[]{:S(2)}) collective-permute-start(bf16[8,256,128]{2,1,0:T(8,128)(2,1)S(1)} %get-tuple-element.32), channel_id=1, source_target_pairs={{0,1},{1,0},{2,3},{3,2},{4,5},{5,4},{6,7},{7,6},{8,9},{9,8},{10,11... | collective-permute-start | bytes 1572872 | tf_op jit(solution)/shard_map/ppermute | solution.py:349
  (2 other events, 11.8 us)
Sparse Core Ops, SparseCore 0:
  9.8 85.2 all-gather.1
